TPU v7x, 512 devices: a whole 4x4x16 slice. The times are simulated.
512 devices in a mesh: zero: 16 (over y, x), dp: 32 (over z, core).
Axes of the slice: x: 4, y: 4, z: 16, core: 2. Of those that a mesh axis runs over, the one named last changes fastest.
Arguments:
- hidden: bfloat16 [32, 4096, 1536], P('dp', 'zero'), may hold values from -6 to 6
- grad_out: bfloat16 [32, 4096, 4096], P('dp', 'zero'), may hold values from -0.015625 to 0.015625
- seed_table: int32 [32, 16, 1, 32], P('dp', 'zero'), may hold values from 0 to 8388607
Outputs:
- weight_grad: bfloat16 [1, 1536, 4096], P(None, 'zero')
All inputs are finite; a program needn't handle non-finite values.
Results may differ from a plain program's by a relative error of at most 0.03.
Values may be sent and summed in bfloat16 or wider, within the bound.
No kernel may reach another device: no remote copies, remote signals or barrier semaphores. Data moves between devices by JAX's collectives and lax.ppermute only.
A program may use at most 128 MiB of HBM per device.

v0:
```python
import jax
import jax.numpy as jnp
from jax import lax
from jax.sharding import PartitionSpec as P


def from_partner(block, axis, distance):
    count = lax.axis_size(axis)
    route = []
    for low in range(count):
        high = low | 1 << distance
        if high != low and high < count:
            route += [(low, high), (high, low)]
    return lax.ppermute(block, axis, route)


def scramble(hashed):
    hashed = hashed ^ lax.shift_right_logical(hashed, jnp.int32(16))
    hashed = hashed * jnp.int32(73244475)
    hashed = hashed ^ lax.shift_right_logical(hashed, jnp.int32(16))
    hashed = hashed * jnp.int32(73244475)
    hashed = hashed ^ lax.shift_right_logical(hashed, jnp.int32(16))
    return hashed


def dither_round(summed_pair, seed_row, row_start, step_no):
    row_total, feature_count = summed_pair.shape
    word_count = seed_row.shape[0]
    groups = feature_count // word_count
    row_ids = row_start + jnp.arange(row_total, dtype=jnp.int32)[:, None, None]
    group_ids = jnp.arange(groups, dtype=jnp.int32)[None, :, None]
    hashed = (
        seed_row[None, None, :]
        + jnp.int32(131071) * row_ids
        + jnp.int32(65599) * group_ids
        + jnp.int32(7919 * step_no)
    )
    hashed = scramble(hashed) & jnp.int32(65535)
    uniform_part = hashed.astype(jnp.float32) / 65536.0
    shaped = summed_pair.reshape(row_total, groups, word_count)
    dithered = shaped + shaped * ((uniform_part - 0.5) * (1.0 / 8.0))
    return dithered.reshape(row_total, feature_count).astype(jnp.bfloat16)


def replica_sum(owned_block):
    return lax.psum(owned_block.astype(jnp.float32).astype(jnp.bfloat16), "dp")


def local_gradient(bucket_hidden, grad_local):
    row_total = bucket_hidden.shape[1]
    block_rows = 512
    pieces = []
    for first_row in range(0, row_total, block_rows):
        product = lax.dot_general(
            bucket_hidden[:, first_row : first_row + block_rows],
            grad_local,
            (((0,), (0,)), ((), ())),
            preferred_element_type=jnp.float32,
        )
        pieces.append(product.astype(jnp.bfloat16))
    return jnp.concatenate(pieces, axis=0)


def per_device(hidden, grad_out, seed_table):
    hidden_local = hidden[0]
    grad_local = grad_out[0]
    seed_local = seed_table[0, 0]
    zero_count = lax.axis_size("zero")
    halving_steps = zero_count.bit_length() - 1
    zero_index = lax.axis_index("zero")
    current = local_gradient(hidden_local, grad_local)
    row_start = jnp.int32(0)
    for step_no in range(halving_steps):
        bit_pos = halving_steps - 1 - step_no
        half_rows = current.shape[0] // 2
        upper_side = zero_index >> bit_pos & 1
        kept_half = lax.dynamic_slice_in_dim(current, upper_side * half_rows, half_rows, 0)
        sent_half = lax.dynamic_slice_in_dim(current, (1 - upper_side) * half_rows, half_rows, 0)
        received = from_partner(sent_half, "zero", bit_pos)
        row_start = row_start + upper_side * half_rows
        summed_pair = kept_half.astype(jnp.float32) + received.astype(jnp.float32)
        current = dither_round(summed_pair, seed_local[0], row_start, step_no)
    owned_list = [current]
    result = jnp.concatenate([replica_sum(owned_piece[None]) for owned_piece in owned_list], axis=0)
    return result


def solution(mesh):
    return jax.shard_map(
        per_device,
        mesh=mesh,
        in_specs=(P("dp", "zero", None), P("dp", "zero", None), P("dp", "zero", None, None)),
        out_specs=P(None, "zero", None),
        check_vma=False,
    )
```

profile of v0, /device:TPU:1, one launch (start us, length us, event | category | flops | bytes accessed | tf_op | source)
XLA Modules:
  0.0 560.6 jit_solution(13090230390780258061)
XLA Ops:
  6.5 0.0 copy-start
  6.5 0.0 copy-start.6
  6.5 0.0 all-reduce.2.cloned.1.call-start
  6.5 1.6 copy-done
  8.1 4.2 convolution_convert_fusion
  12.3 0.0 copy-done.6
  12.3 3.2 convolution_convert_fusion.1
  15.5 3.2 convolution_convert_fusion.2
  18.8 7.3 %pad_maximum_fusion = bf16[1536,4096]{1,0:T(8,128)(2,1)S(1)} fusion(bf16[512,4096]{1,0:T(8,128)(2,1)} %convolution_convert_fusion, bf16[512,4096]{1,0:T(8,128)(2,1)} %convolution_convert_fusion.1, bf16[512,4096]{1,0:T(8,128)(2,1)} %convolution_convert_fusion.2), kind=kLoop, calls=%fused_computation.11 | loop fusion | flops 37748736 | bytes 25165824 | tf_op jit(solution)/shard_map/concatenate | solution.py:61
  26.1 0.0 copy-start.2
  26.1 0.0 copy-start.7
  26.1 3.3 constant_dynamic-slice_fusion.3
  29.4 3.1 copy-done.2
  32.5 5.6 %collective-permute-start = (bf16[768,4096]{1,0:T(8,128)(2,1)}, bf16[768,4096]{1,0:T(8,128)(2,1)}, u32[]{:S(2)}, u32[]{:S(2)}) collective-permute-start(bf16[768,4096]{1,0:T(8,128)(2,1)} %constant_dynamic-slice_fusion.3), channel_id=1, source_target_pairs={{0,256},{256,0},{32,288},{288,32},{64,320},{320,64},{96,352},{352,... | collective-permute-start | bytes 18874376 | tf_op jit(solution)/shard_map/ppermute | solution.py:14
  38.1 0.0 copy-done.7
  38.1 0.1 broadcast_add_fusion
  38.2 6.2 %add.299 = s32[768,128,32]{0,2,1:T(8,128)} broadcast(s32[768,32]{0,1:T(8,128)S(1)} %broadcast_add_fusion), dimensions={0,2} | broadcast | bytes 12681216 | tf_op jit(solution)/shard_map/add | solution.py:33
  44.4 12.7 %copy.4 = s32[768,4096]{1,0:T(8,128)} copy(s32[768,4096]{0,1:T(8,128)} %bitcast.15) | data formatting | bytes 25165824 | tf_op jit(solution)/shard_map/add | solution.py:33
  57.1 0.1 add.301
  57.2 0.1 add.302
  57.2 113.1 %collective-permute-done = bf16[768,4096]{1,0:T(8,128)(2,1)} collective-permute-done((bf16[768,4096]{1,0:T(8,128)(2,1)}, bf16[768,4096]{1,0:T(8,128)(2,1)}, u32[]{:S(2)}, u32[]{:S(2)}) %collective-permute-start) | collective-permute-done | bytes 6291488 | tf_op jit(solution)/shard_map/ppermute | solution.py:14
  170.3 12.2 %fusion.7 = bf16[768,4096]{1,0:T(8,128)(2,1)S(1)} fusion(s32[768,4096]{1,0:T(8,128)} %copy.4, bf16[768,4096]{1,0:T(8,128)(2,1)} %collective-permute-done, s32[4096]{0:T(1024)S(1)} %add.302, bf16[1536,4096]{1,0:T(8,128)(2,1)} %copy-done.2, s32[]{:T(128)S(6)} %select_n.24), kind=kLoop, calls=%fused_computation.12 | loop fusion | flops 62914560 | bytes 31473668 | tf_op jit(solution)/shard_map/convert_element_type | solution.py:42
  182.5 0.0 copy-start.3
  182.5 2.6 copy-done.3
  185.2 1.9 constant_dynamic-slice_fusion.2
  187.0 6.4 %collective-permute-start.1 = (bf16[384,4096]{1,0:T(8,128)(2,1)}, bf16[384,4096]{1,0:T(8,128)(2,1)}, u32[]{:S(2)}, u32[]{:S(2)}) collective-permute-start(bf16[384,4096]{1,0:T(8,128)(2,1)} %constant_dynamic-slice_fusion.2), channel_id=1, source_target_pairs={{0,128},{128,0},{32,160},{160,32},{64,192},{192,64},{96,224},{224,... | collective-permute-start | bytes 9437192 | tf_op jit(solution)/shard_map/ppermute | solution.py:14
  193.5 0.1 broadcast_add_fusion.1
  193.6 3.4 add.315
  196.9 6.6 %copy.5 = s32[384,4096]{1,0:T(8,128)} copy(s32[384,4096]{0,1:T(8,128)} %bitcast.16) | data formatting | bytes 12582912 | tf_op jit(solution)/shard_map/add | solution.py:33
  203.5 56.5 %collective-permute-done.1 = bf16[384,4096]{1,0:T(8,128)(2,1)} collective-permute-done((bf16[384,4096]{1,0:T(8,128)(2,1)}, bf16[384,4096]{1,0:T(8,128)(2,1)}, u32[]{:S(2)}, u32[]{:S(2)}) %collective-permute-start.1) | collective-permute-done | bytes 3145760 | tf_op jit(solution)/shard_map/ppermute | solution.py:14
  260.0 7.0 %fusion.15 = bf16[384,4096]{1,0:T(8,128)(2,1)S(1)} fusion(s32[384,4096]{1,0:T(8,128)} %copy.5, bf16[384,4096]{1,0:T(8,128)(2,1)} %collective-permute-done.1, s32[4096]{0:T(1024)S(1)} %add.302, bf16[768,4096]{1,0:T(8,128)(2,1)} %copy-done.3, s32[]{:T(128)S(6)} %select_n.26), kind=kLoop, calls=%fused_computation.24 | loop fusion | flops 33030144 | bytes 15745028 | tf_op jit(solution)/shard_map/convert_element_type | solution.py:42
  267.1 0.0 copy-start.4
  267.1 1.7 copy-done.4
  268.8 0.1 constant_dynamic-slice_fusion.1
  268.9 4.9 collective-permute-start.2
  273.9 0.1 broadcast_add_fusion.2
  273.9 2.5 add.331
  276.4 5.3 copy.6
  281.7 24.1 %collective-permute-done.2 = bf16[192,4096]{1,0:T(8,128)(2,1)} collective-permute-done((bf16[192,4096]{1,0:T(8,128)(2,1)S(1)}, bf16[192,4096]{1,0:T(8,128)(2,1)}, u32[]{:S(2)}, u32[]{:S(2)}) %collective-permute-start.2) | collective-permute-done | bytes 1572896 | tf_op jit(solution)/shard_map/ppermute | solution.py:14
  305.8 4.9 fusion.23
  310.7 0.0 copy-start.5
  310.8 1.1 copy-done.5
  311.9 0.1 constant_dynamic-slice_fusion
  312.0 3.4 collective-permute-start.3
  315.4 0.1 broadcast_add_fusion.3
  315.5 1.6 add.347
  317.1 0.0 copy-start.1
  317.1 3.0 copy.7
  320.1 9.6 %collective-permute-done.3 = bf16[96,4096]{1,0:T(8,128)(2,1)} collective-permute-done((bf16[96,4096]{1,0:T(8,128)(2,1)S(1)}, bf16[96,4096]{1,0:T(8,128)(2,1)}, u32[]{:S(2)}, u32[]{:S(2)}) %collective-permute-start.3) | collective-permute-done | bytes 786464 | tf_op jit(solution)/shard_map/ppermute | solution.py:14
  329.6 3.8 fusion.35
  333.4 0.0 all-reduce.2.cloned.1.call-update
  333.4 218.2 %all-reduce.2.cloned.1.call-done = bf16[1,96,4096]{2,1,0:T(8,128)(2,1)} async-done(((bf16[1,96,4096]{2,1,0:T(8,128)(2,1)}), bf16[1,96,4096]{2,1,0:T(8,128)(2,1)}) %all-reduce.2.cloned.1.call-update) | async-done | bytes 786448 | tf_op jit(solution)/shard_map/psum | solution.py:46
  551.7 2.1 copy.9
  553.7 0.0 copy-done.1
  (5 shorter events, 0.0 us)
Async XLA Ops:
  6.5 1.6 copy-start
  6.5 5.8 %copy-start.6 = (bf16[1,256,1536]{2,1,0:T(8,128)(2,1)S(1)}, bf16[1,256,1536]{2,1,0:T(8,128)(2,1)}, u32[]{:S(2)}) copy-start(bf16[1,256,1536]{2,1,0:T(8,128)(2,1)} %param.3) | copy-start | bytes 2359300
  6.5 545.1 %all-reduce.2.cloned.1.call-start = ((), (), s32[]{:S(2)}) async-start(), calls=%async_computation | async-start | bytes 1572864 | tf_op jit(solution)/shard_map/psum | solution.py:46
  26.1 6.4 %copy-start.2 = (bf16[1536,4096]{1,0:T(8,128)(2,1)}, bf16[1536,4096]{1,0:T(8,128)(2,1)S(1)}, u32[]{:S(2)}) copy-start(bf16[1536,4096]{1,0:T(8,128)(2,1)S(1)} %pad_maximum_fusion) | copy-start | bytes 37748740
  26.1 12.1 %copy-start.7 = (s32[1,1,1,32]{3,2,1,0:T(1,128)S(1)}, s32[1,1,1,32]{3,2,1,0:T(1,128)}, u32[]{:S(2)}) copy-start(s32[1,1,1,32]{3,2,1,0:T(1,128)} %param.5) | copy-start | bytes 388
  32.5 137.9 %collective-permute-start = (bf16[768,4096]{1,0:T(8,128)(2,1)}, bf16[768,4096]{1,0:T(8,128)(2,1)}, u32[]{:S(2)}, u32[]{:S(2)}) collective-permute-start(bf16[768,4096]{1,0:T(8,128)(2,1)} %constant_dynamic-slice_fusion.3), channel_id=1, source_target_pairs={{0,256},{256,0},{32,288},{288,32},{64,320},{320,64},{96,352},{352,... | collective-permute-start | bytes 18874376 | tf_op jit(solution)/shard_map/ppermute | solution.py:14
  182.5 2.7 copy-start.3
  187.0 73.0 %collective-permute-start.1 = (bf16[384,4096]{1,0:T(8,128)(2,1)}, bf16[384,4096]{1,0:T(8,128)(2,1)}, u32[]{:S(2)}, u32[]{:S(2)}) collective-permute-start(bf16[384,4096]{1,0:T(8,128)(2,1)} %constant_dynamic-slice_fusion.2), channel_id=1, source_target_pairs={{0,128},{128,0},{32,160},{160,32},{64,192},{192,64},{96,224},{224,... | collective-permute-start | bytes 9437192 | tf_op jit(solution)/shard_map/ppermute | solution.py:14
  267.1 1.7 copy-start.4
  268.9 36.9 %collective-permute-start.2 = (bf16[192,4096]{1,0:T(8,128)(2,1)S(1)}, bf16[192,4096]{1,0:T(8,128)(2,1)}, u32[]{:S(2)}, u32[]{:S(2)}) collective-permute-start(bf16[192,4096]{1,0:T(8,128)(2,1)S(1)} %constant_dynamic-slice_fusion.1), channel_id=1, source_target_pairs={{0,64},{64,0},{32,96},{96,32},{128,192},{192,128},{160,224},{224,1... | collective-permute-start | bytes 4718600 | tf_op jit(solution)/shard_map/ppermute | solution.py:14
  310.7 1.2 copy-start.5
  312.0 17.7 %collective-permute-start.3 = (bf16[96,4096]{1,0:T(8,128)(2,1)S(1)}, bf16[96,4096]{1,0:T(8,128)(2,1)}, u32[]{:S(2)}, u32[]{:S(2)}) collective-permute-start(bf16[96,4096]{1,0:T(8,128)(2,1)S(1)} %constant_dynamic-slice_fusion), channel_id=1, source_target_pairs={{0,32},{32,0},{64,96},{96,64},{128,160},{160,128},{192,224},{224,1... | collective-permute-start | bytes 2359304 | tf_op jit(solution)/shard_map/ppermute | solution.py:14
  317.1 236.7 %copy-start.1 = (bf16[1,256,4096]{2,1,0:T(8,128)(2,1)S(1)}, bf16[1,256,4096]{2,1,0:T(8,128)(2,1)}, u32[]{:S(2)}) copy-start(bf16[1,256,4096]{2,1,0:T(8,128)(2,1)} %param.4) | copy-start | bytes 6291460
Sparse Core Ops, SparseCore 0:
  333.6 218.0 all-reduce.1
where the time goes:
time: 561 us
  waiting for transfers between devices  422 us (75%)
  local copies, waits for them, and re-layouts  58.9 us (10%)
  other arithmetic  35.5 us (6%)
  starting transfers between devices  20.4 us (4%)
  between operations  13.6 us (2%)
  matrix products  10.7 us (2%)
    psum x1, waiting for transfers between devices, replica_sum(): return lax.psum(owned_block.astype(jnp.float32).astype(jnp.bfloat16), 'dp')  218 us
    ppermute x4, waiting for transfers between devices, from_partner(): return lax.ppermute(block, axis, route)  203 us
    add x10, local copies, waits for them, and re-layouts, dither_round(): seed_row[None, None, :] + jnp.int32(131071) * row_ids  41.4 us
    convert_element_type x3, other arithmetic, dither_round(): return dithered.reshape(row_total, feature_count).astype(jnp.bfloat16)  24.1 us
    ppermute x4, starting transfers between devices, from_partner(): return lax.ppermute(block, axis, route)  20.4 us
    unnamed x17, local copies, waits for them, and re-layouts  12.2 us
  transfers between devices with their start and end apart: 5, of which 5 were waited for; matrix products, arithmetic and copies ran while one was open for 7% of the time, Pallas kernels for 0%

commit v1 on v0

v1 whole, which is shorter than its diff:
```python
import jax
import jax.numpy as jnp
from jax import lax
from jax.experimental import pallas as pl
from jax.experimental.pallas import tpu as pltpu
from jax.sharding import Mesh, PartitionSpec as P

SWAP = [(0, 1), (1, 0)]
MIX = 73244475
CHUNKS = 2


def factor(base, offset):
    k = base + offset
    k = k ^ lax.shift_right_logical(k, 16)
    k = k * MIX
    k = k ^ lax.shift_right_logical(k, 16)
    k = k * MIX
    k = (k ^ lax.shift_right_logical(k, 16)) & 65535
    return k.astype(jnp.float32) + 491520.0


def leaf_kernel(place, ha_ref, hb_ref, ga_ref, gb_ref, words_ref, out_ref, base_ref, *, tile):
    owner = pl.program_id(0)
    z, core, group0 = place[0], place[1], place[2]
    rows, width = out_ref.shape[1:]
    lane = lax.broadcasted_iota(jnp.int32, (8, 128), 1)
    sub = lax.broadcasted_iota(jnp.int32, (8, 128), 0)
    shared = 65599 * (lane >> 5) + 131071 * sub + (131071 * rows * owner + 65599 * group0)
    for rep in range(2):
        for step in range(4):
            low = 7 >> step
            keeper = (owner & (15 - low)) | (z & low)
            seeds = words_ref[pl.ds(keeper * 2 + (core ^ rep), 1), :]
            base_ref[rep, step] = seeds + shared + 7919 * step

    def columns(at, carry):
        first = pl.multiple_of(at * tile, tile)
        parts = [
            jnp.dot(h[...], g[:, pl.ds(first, tile)], preferred_element_type=jnp.float32)
            for h, g in ((ha_ref, ga_ref), (hb_ref, gb_ref))
        ]
        for row in range(0, rows, 16):
            for col in range(0, tile, 128):
                halves = []
                for top in (row, row + 8):
                    offset = (at * (tile // 128) + col // 128) * (4 * 65599) + 131071 * top
                    total = None
                    for rep in range(2):
                        f = [factor(base_ref[rep, step], offset) for step in range(4)]
                        scale = ((f[0] * f[1]) * (f[2] * f[3])) * (2.0**-76)
                        term = parts[rep][top : top + 8, col : col + 128] * scale
                        total = term if total is None else total + term
                    halves.append(total)
                block = jnp.concatenate(halves, axis=0).astype(jnp.bfloat16)
                out_ref[0, row : row + 16, pl.ds(pl.multiple_of(first + col, 128), 128)] = block
        return carry

    lax.fori_loop(0, width // tile, columns, 0)


def leaf(place, ha, hb, ga, gb, words, owners):
    rows_all, tokens = ha.shape
    width = ga.shape[1]
    rows = rows_all // owners
    tile = min(512, width)
    body = lambda *refs: leaf_kernel(*refs, tile=tile)
    return pl.pallas_call(
        body,
        grid_spec=pltpu.PrefetchScalarGridSpec(
            num_scalar_prefetch=1,
            grid=(owners,),
            in_specs=[
                pl.BlockSpec((rows, tokens), lambda i, p: (i, 0)),
                pl.BlockSpec((rows, tokens), lambda i, p: (i, 0)),
                pl.BlockSpec((tokens, width), lambda i, p: (0, 0)),
                pl.BlockSpec((tokens, width), lambda i, p: (0, 0)),
                pl.BlockSpec(words.shape, lambda i, p: (0, 0)),
            ],
            out_specs=pl.BlockSpec((1, rows, width), lambda i, p: (i, 0, 0)),
            scratch_shapes=[pltpu.VMEM((2, 4, 8, 128), jnp.int32)],
        ),
        out_shape=jax.ShapeDtypeStruct((owners, rows, width), jnp.bfloat16),
        compiler_params=pltpu.CompilerParams(vmem_limit_bytes=24 * 2**20),
        cost_estimate=pl.CostEstimate(
            flops=80 * rows_all * tokens * width, bytes_accessed=2 * rows_all * width * 2, transcendentals=0
        ),
    )(place, ha, hb, ga, gb, words)


def exchange(blocks, axes):
    return lax.all_to_all(blocks, axes, 0, 0, tiled=True)


def added(blocks):
    return jnp.sum(blocks.astype(jnp.float32), axis=0).astype(jnp.bfloat16)


def per_device(hidden, grad_out, seed_table):
    owners = lax.axis_size("y") * lax.axis_size("x")
    depth = lax.axis_size("z")
    core = lax.axis_index("core")
    z = lax.axis_index("y") * lax.axis_size("x") + lax.axis_index("x")
    h_own = hidden[0].T
    g_all = grad_out[0]
    half = g_all.shape[1] // 2
    h_other = lax.ppermute(h_own, "core", SWAP)
    g_own = lax.dynamic_slice_in_dim(g_all, core * half, half, 1)
    g_other = lax.ppermute(lax.dynamic_slice_in_dim(g_all, (1 - core) * half, half, 1), "core", SWAP)
    seeds = jnp.tile(seed_table[0, 0], (1, 4))
    words = exchange(jnp.broadcast_to(seeds, (2 * owners, 128)), ("y", "x", "core"))

    width = half // CHUNKS
    rows = h_own.shape[0] // owners
    across = min(depth, width // 128)
    down = depth // across
    mine = []
    for chunk in range(CHUNKS):
        place = jnp.stack([z, core, (core * half + chunk * width) // 32]).astype(jnp.int32)
        cut = slice(chunk * width, (chunk + 1) * width)
        partial = leaf(place, h_own, h_other, g_own[:, cut], g_other[:, cut], words, owners)
        owned = added(exchange(partial, ("y", "x")))
        cells = owned.reshape(down, rows // down, across, width // across).transpose(0, 2, 1, 3)
        cells = cells.reshape(depth, rows // down, width // across)
        cell = added(exchange(cells, "z"))
        everyone = exchange(jnp.broadcast_to(cell, cells.shape), "z")
        block = everyone.reshape(down, across, rows // down, width // across).transpose(0, 2, 1, 3)
        mine.append(block.reshape(rows, width))
    here = jnp.concatenate(mine, axis=1)
    there = lax.ppermute(here, "core", SWAP)
    first = core == 0
    result = jnp.concatenate([jnp.where(first, here, there), jnp.where(first, there, here)], axis=1)
    return result[None]


def solution(mesh):
    devices = mesh.devices
    zero, dp = devices.shape
    split = Mesh(devices.reshape(4, zero // 4, dp // 2, 2), ("y", "x", "z", "core"))
    return jax.shard_map(
        per_device,
        mesh=split,
        in_specs=(
            P(("z", "core"), ("y", "x"), None),
            P(("z", "core"), ("y", "x"), None),
            P(("z", "core"), ("y", "x"), None, None),
        ),
        out_specs=P(None, ("y", "x"), None),
        check_vma=False,
    )
```

time: 561 us -> 252 us (0.45)
  waiting for transfers between devices: 422 us -> 115 us
  Pallas kernels: 0 us -> 55.4 us
  local copies, waits for them, and re-layouts: 58.9 us -> 8.16 us
  starting transfers between devices: 20.4 us -> 65.1 us
  other arithmetic: 35.5 us -> 4.41 us
  between operations: 13.6 us -> 0.24 us
  matrix products: 10.7 us -> 0 us
    psum x1 -> x0, waiting for transfers between devices: 218 us -> none  [replica_sum(): return lax.psum(owned_block.astype(jnp.float32).astype(jnp.bfloat16), 'dp')]
    ppermute x4 -> x3, waiting for transfers between devices: 203 us -> 1.33 us  [the longest x1 1.32 us: per_device(): there = lax.ppermute(here, 'core', SWAP)]
    all_to_all x0 -> x7, waiting for transfers between devices: none -> 114 us  [exchange(): return lax.all_to_all(blocks, axes, 0, 0, tiled=True)]
    pallas_call x0 -> x2, Pallas kernels: none -> 55.4 us  [leaf(): pl.pallas_call(body, grid_spec=pltpu.PrefetchScalarGridSpec(num_scalar_pr...]
    all_to_all x0 -> x7, starting transfers between devices: none -> 46.9 us  [exchange(): return lax.all_to_all(blocks, axes, 0, 0, tiled=True)]
    add x10 -> x0, local copies, waits for them, and re-layouts: 41.4 us -> none  [dither_round(): seed_row[None, None, :] + jnp.int32(131071) * row_ids]
    convert_element_type x3 -> x0, other arithmetic: 24.1 us -> none  [dither_round(): return dithered.reshape(row_total, feature_count).astype(jnp.bfloat16)]
    unnamed x17 -> x8, local copies, waits for them, and re-layouts: 12.2 us -> 0.36 us
  transfers between devices with their start and end apart: 5 -> 10, of which waited for: 5 -> 8; matrix products, arithmetic and copies ran while one was open for 7% -> 3% of each run, Pallas kernels for 0% -> 11%
where the time goes in v1:
time: 252 us; the launch traced here: 248 us
  waiting for transfers between devices  115 us (46%)
  starting transfers between devices  65.1 us (26%)
  Pallas kernels  55.4 us (22%)
  local copies, waits for them, and re-layouts  8.16 us (3%)
  other arithmetic  4.41 us (2%)
    all_to_all x7, waiting for transfers between devices, exchange(): return lax.all_to_all(blocks, axes, 0, 0, tiled=True)  114 us
    pallas_call x2, Pallas kernels, leaf(): pl.pallas_call(body, grid_spec=pltpu.PrefetchScalarGridSpec(num_scalar_pr...  55.4 us
    all_to_all x7, starting transfers between devices, exchange(): return lax.all_to_all(blocks, axes, 0, 0, tiled=True)  46.9 us
    ppermute x1, starting transfers between devices, per_device(): lax.ppermute(lax.dynamic_slice_in_dim(g_all, (1 - core) * half, half, 1),...  8.78 us
    ppermute x1, starting transfers between devices, per_device(): there = lax.ppermute(here, 'core', SWAP)  7.52 us
  transfers between devices with their start and end apart: 10, of which 8 were waited for; matrix products, arithmetic and copies ran while one was open for 3% of the time, Pallas kernels for 11%

profile of v1, /device:TPU:1, one launch (start us, length us, event | category | flops | bytes accessed | tf_op | source)
XLA Modules:
  0.0 248.4 jit_solution(6158706673758182922)
XLA Ops:
  0.0 0.0 copy-start
  0.0 0.0 copy-start.1
  0.0 2.8 %dynamic-slice_bitcast_fusion = (bf16[256,2048]{1,0:T(8,128)(2,1)}, bf16[256,2048]{1,0:T(8,128)(2,1)S(1)}) fusion(bf16[1,256,4096]{2,1,0:T(8,128)(2,1)} %param.4, s32[]{:T(128)S(6)} %select_n.29, s32[]{:T(128)S(6)} %select_n.28), kind=kLoop, calls=%fused_computation | loop fusion | bytes 4194312 | tf_op jit(solution)/shard_map/dynamic_slice | solution.py:109
  2.8 8.8 %collective-permute-start.1 = (bf16[256,2048]{1,0:T(8,128)(2,1)}, bf16[256,2048]{1,0:T(8,128)(2,1)}, u32[]{:S(2)}, u32[]{:S(2)}) collective-permute-start(bf16[256,2048]{1,0:T(8,128)(2,1)} %get-tuple-element.5), channel_id=1, source_target_pairs={{0,1},{1,0},{2,3},{3,2},{4,5},{5,4},{6,7},{7,6},{8,9},{9,8},{10,11... | collective-permute-start | bytes 3145736 | tf_op jit(solution)/shard_map/ppermute | solution.py:109
  11.6 0.0 copy-done
  11.6 0.3 copy.11
  11.8 1.9 collective-permute-start
  13.8 0.0 copy-done.1
  13.8 0.1 tile.12
  13.9 0.6 broadcast_in_dim.14
  14.5 4.0 %all-to-all-start = ((s32[32,1,128]{2,1,0:T(1,128)}), s32[32,1,128]{2,1,0:T(1,128)S(1)}, u32[]{:S(2)}, u32[]{:S(2)}) async-start(s32[32,1,128]{2,1,0:T(1,128)} %broadcast_in_dim.14), calls=%async_computation | async-start | bytes 32768 | tf_op jit(solution)/shard_map/all_to_all | solution.py:92
  18.5 0.1 pad_add_fusion.2.refs_0_
  18.6 0.1 pad_add_fusion.refs_0_
  18.7 0.1 fusion.1
  18.7 0.0 collective-permute-done.1
  18.8 1.3 fusion
  20.0 5.4 %all-to-all-done = s32[32,1,128]{2,1,0:T(1,128)S(1)} async-done(((s32[32,1,128]{2,1,0:T(1,128)}), s32[32,1,128]{2,1,0:T(1,128)S(1)}, u32[]{:S(2)}, u32[]{:S(2)}) %all-to-all-start) | async-done | bytes 16416 | tf_op jit(solution)/shard_map/all_to_all | solution.py:92
  25.5 0.0 collective-permute-done.refs_2_
  25.5 27.7 %shard_map.38 = bf16[16,96,1024]{2,1,0:T(8,128)(2,1)} custom-call(s32[3]{0:T(128)S(1)} %pad_add_fusion.2.refs_0_, bf16[1536,256]{1,0:T(8,128)(2,1)S(1)} %bitcast.46, bf16[1536,256]{1,0:T(8,128)(2,1)} %collective-permute-done.refs_2_, bf16[256,1024]{1,0:T(8,128)(2,1)S(1)} %get-tuple-element.9.refs_3_, bf16[256,1024]{1,0:T(8,128)(2,1)S(1)} %get-tuple-element.7.refs_4_, ...), custom_call_target="tpu_custom_call" | custom-call | flops 32212254720 | bytes 6291456 | tf_op jit(solution)/shard_map/pallas_call | solution.py:68
  53.1 4.5 %all-to-all-start.4 = ((bf16[16,96,1024]{2,1,0:T(8,128)(2,1)}), bf16[16,96,1024]{2,1,0:T(8,128)(2,1)}, u32[]{:S(2)}, u32[]{:S(2)}) async-start(bf16[16,96,1024]{2,1,0:T(8,128)(2,1)} %shard_map.38), calls=%async_computation.4 | async-start | bytes 6291456 | tf_op jit(solution)/shard_map/all_to_all | solution.py:92
  57.6 27.7 %shard_map.37 = bf16[16,96,1024]{2,1,0:T(8,128)(2,1)} custom-call(s32[3]{0:T(128)S(1)} %pad_add_fusion.refs_0_, bf16[1536,256]{1,0:T(8,128)(2,1)S(1)} %bitcast.47, bf16[1536,256]{1,0:T(8,128)(2,1)} %collective-permute-done.refs_2_, bf16[256,1024]{1,0:T(8,128)(2,1)S(1)} %get-tuple-element.10.refs_3_, bf16[256,1024]{1,0:T(8,128)(2,1)S(1)} %get-tuple-element.8.refs_4_, ...), custom_call_target="tpu_custom_call" | custom-call | flops 32212254720 | bytes 6291456 | tf_op jit(solution)/shard_map/pallas_call | solution.py:68
  85.4 19.8 %all-to-all-done.4 = bf16[16,96,1024]{2,1,0:T(8,128)(2,1)} async-done(((bf16[16,96,1024]{2,1,0:T(8,128)(2,1)}), bf16[16,96,1024]{2,1,0:T(8,128)(2,1)}, u32[]{:S(2)}, u32[]{:S(2)}) %all-to-all-start.4) | async-done | bytes 3145760 | tf_op jit(solution)/shard_map/all_to_all | solution.py:92
  105.2 4.1 %all-to-all-start.1 = ((bf16[16,96,1024]{2,1,0:T(8,128)(2,1)}), bf16[16,96,1024]{2,1,0:T(8,128)(2,1)S(1)}, u32[]{:S(2)}, u32[]{:S(2)}) async-start(bf16[16,96,1024]{2,1,0:T(8,128)(2,1)} %shard_map.37), calls=%async_computation.1 | async-start | bytes 6291456 | tf_op jit(solution)/shard_map/all_to_all | solution.py:92
  109.3 2.5 %reduce_sum.50 = bf16[96,1024]{1,0:T(8,128)(2,1)S(1)} reduce(bf16[16,96,1024]{2,1,0:T(8,128)(2,1)} %all-to-all-done.4, bf16[]{:T(256)} %constant.53.clone.1), dimensions={0}, to_apply=%region_2.3 | reduce | flops 1474560 | bytes 3342338 | tf_op jit(solution)/shard_map/reduce_sum | solution.py:96
  111.9 0.7 copy.14
  112.7 40.7 %all-to-all-done.1 = bf16[16,96,1024]{2,1,0:T(8,128)(2,1)S(1)} async-done(((bf16[16,96,1024]{2,1,0:T(8,128)(2,1)}), bf16[16,96,1024]{2,1,0:T(8,128)(2,1)S(1)}, u32[]{:S(2)}, u32[]{:S(2)}) %all-to-all-start.1) | async-done | bytes 3145760 | tf_op jit(solution)/shard_map/all_to_all | solution.py:92
  153.3 13.0 %all-to-all-start.5 = ((bf16[16,48,128]{2,1,0:T(8,128)(2,1)}), bf16[16,48,128]{2,1,0:T(8,128)(2,1)S(1)}, u32[]{:S(2)}, u32[]{:S(2)}) async-start(bf16[16,48,128]{2,1,0:T(8,128)(2,1)} %bitcast.16), calls=%async_computation.5 | async-start | bytes 393216 | tf_op jit(solution)/shard_map/all_to_all | solution.py:92
  166.3 0.6 reduce_sum.48
  167.1 0.7 copy.12
  167.8 10.9 %all-to-all-done.5 = bf16[16,48,128]{2,1,0:T(8,128)(2,1)S(1)} async-done(((bf16[16,48,128]{2,1,0:T(8,128)(2,1)}), bf16[16,48,128]{2,1,0:T(8,128)(2,1)S(1)}, u32[]{:S(2)}, u32[]{:S(2)}) %all-to-all-start.5) | async-done | bytes 196640 | tf_op jit(solution)/shard_map/all_to_all | solution.py:92
  178.7 7.0 %all-to-all-start.2 = ((bf16[16,48,128]{2,1,0:T(8,128)(2,1)}), bf16[16,48,128]{2,1,0:T(8,128)(2,1)S(1)}, u32[]{:S(2)}, u32[]{:S(2)}) async-start(bf16[16,48,128]{2,1,0:T(8,128)(2,1)} %bitcast.11), calls=%async_computation.2 | async-start | bytes 393216 | tf_op jit(solution)/shard_map/all_to_all | solution.py:92
  185.8 12.3 %all-to-all-done.2 = bf16[16,48,128]{2,1,0:T(8,128)(2,1)S(1)} async-done(((bf16[16,48,128]{2,1,0:T(8,128)(2,1)}), bf16[16,48,128]{2,1,0:T(8,128)(2,1)S(1)}, u32[]{:S(2)}, u32[]{:S(2)}) %all-to-all-start.2) | async-done | bytes 196640 | tf_op jit(solution)/shard_map/all_to_all | solution.py:92
  198.1 0.7 broadcast_in_dim.16
  198.8 7.2 %all-to-all-start.6 = ((bf16[16,48,128]{2,1,0:T(8,128)(2,1)}), bf16[16,48,128]{2,1,0:T(8,128)(2,1)S(1)}, u32[]{:S(2)}, u32[]{:S(2)}) async-start(bf16[16,48,128]{2,1,0:T(8,128)(2,1)} %broadcast_in_dim.16), calls=%async_computation.6 | async-start | bytes 393216 | tf_op jit(solution)/shard_map/all_to_all | solution.py:92
  206.0 12.3 %all-to-all-done.6 = bf16[16,48,128]{2,1,0:T(8,128)(2,1)S(1)} async-done(((bf16[16,48,128]{2,1,0:T(8,128)(2,1)}), bf16[16,48,128]{2,1,0:T(8,128)(2,1)S(1)}, u32[]{:S(2)}, u32[]{:S(2)}) %all-to-all-start.6) | async-done | bytes 196640 | tf_op jit(solution)/shard_map/all_to_all | solution.py:92
  218.3 0.7 broadcast_in_dim.15
  219.0 7.1 %all-to-all-start.3 = ((bf16[16,48,128]{2,1,0:T(8,128)(2,1)}), bf16[16,48,128]{2,1,0:T(8,128)(2,1)S(1)}, u32[]{:S(2)}, u32[]{:S(2)}) async-start(bf16[16,48,128]{2,1,0:T(8,128)(2,1)} %broadcast_in_dim.15), calls=%async_computation.3 | async-start | bytes 393216 | tf_op jit(solution)/shard_map/all_to_all | solution.py:92
  226.1 0.1 copy.15
  226.2 12.3 %all-to-all-done.3 = bf16[16,48,128]{2,1,0:T(8,128)(2,1)S(1)} async-done(((bf16[16,48,128]{2,1,0:T(8,128)(2,1)}), bf16[16,48,128]{2,1,0:T(8,128)(2,1)S(1)}, u32[]{:S(2)}, u32[]{:S(2)}) %all-to-all-start.3) | async-done | bytes 196640 | tf_op jit(solution)/shard_map/all_to_all | solution.py:92
  238.5 0.1 copy.13
  238.6 7.5 %collective-permute-start.2 = (bf16[96,2048]{1,0:T(8,128)(2,1)S(1)}, bf16[96,2048]{1,0:T(8,128)(2,1)S(1)}, u32[]{:S(2)}, u32[]{:S(2)}) collective-permute-start(bf16[96,2048]{1,0:T(8,128)(2,1)S(1)} %bitcast_dynamic-update-slice_fusion), channel_id=1, source_target_pairs={{0,1},{1,0},{2,3},{3,2},{4,5},{5,4},{6,7},{7,6},{8,9},{9,8},{10,11... | collective-permute-start | bytes 1179656 | tf_op jit(solution)/shard_map/ppermute | solution.py:130
  246.1 1.3 collective-permute-done.2
  247.4 0.1 broadcast_select_fusion.1
  247.5 0.9 maximum_bitcast_fusion
  (9 shorter events, 0.2 us)
Async XLA Ops:
  0.0 11.6 %copy-start = (bf16[1,256,1536]{2,1,0:T(8,128)(2,1)S(1)}, bf16[1,256,1536]{2,1,0:T(8,128)(2,1)}, u32[]{:S(2)}) copy-start(bf16[1,256,1536]{2,1,0:T(8,128)(2,1)} %param.3) | copy-start | bytes 2359300
  0.0 13.8 %copy-start.1 = (s32[1,1,1,32]{3,2,1,0:T(1,128)S(1)}, s32[1,1,1,32]{3,2,1,0:T(1,128)}, u32[]{:S(2)}) copy-start(s32[1,1,1,32]{3,2,1,0:T(1,128)} %param.5) | copy-start | bytes 388
  2.8 16.0 %collective-permute-start.1 = (bf16[256,2048]{1,0:T(8,128)(2,1)}, bf16[256,2048]{1,0:T(8,128)(2,1)}, u32[]{:S(2)}, u32[]{:S(2)}) collective-permute-start(bf16[256,2048]{1,0:T(8,128)(2,1)} %get-tuple-element.5), channel_id=1, source_target_pairs={{0,1},{1,0},{2,3},{3,2},{4,5},{5,4},{6,7},{7,6},{8,9},{9,8},{10,11... | collective-permute-start | bytes 3145736 | tf_op jit(solution)/shard_map/ppermute | solution.py:109
  11.8 13.6 %collective-permute-start = (bf16[1536,256]{1,0:T(8,128)(2,1)S(1)}, bf16[1536,256]{1,0:T(8,128)(2,1)}, u32[]{:S(2)}, u32[]{:S(2)}) collective-permute-start(bf16[1536,256]{1,0:T(8,128)(2,1)S(1)} %bitcast.45), channel_id=1, source_target_pairs={{0,1},{1,0},{2,3},{3,2},{4,5},{5,4},{6,7},{7,6},{8,9},{9,8},{10,11... | collective-permute-start | bytes 2359304 | tf_op jit(solution)/shard_map/ppermute | solution.py:107
  14.5 11.0 %all-to-all-start = ((s32[32,1,128]{2,1,0:T(1,128)}), s32[32,1,128]{2,1,0:T(1,128)S(1)}, u32[]{:S(2)}, u32[]{:S(2)}) async-start(s32[32,1,128]{2,1,0:T(1,128)} %broadcast_in_dim.14), calls=%async_computation | async-start | bytes 32768 | tf_op jit(solution)/shard_map/all_to_all | solution.py:92
  53.1 52.1 %all-to-all-start.4 = ((bf16[16,96,1024]{2,1,0:T(8,128)(2,1)}), bf16[16,96,1024]{2,1,0:T(8,128)(2,1)}, u32[]{:S(2)}, u32[]{:S(2)}) async-start(bf16[16,96,1024]{2,1,0:T(8,128)(2,1)} %shard_map.38), calls=%async_computation.4 | async-start | bytes 6291456 | tf_op jit(solution)/shard_map/all_to_all | solution.py:92
  105.2 48.1 %all-to-all-start.1 = ((bf16[16,96,1024]{2,1,0:T(8,128)(2,1)}), bf16[16,96,1024]{2,1,0:T(8,128)(2,1)S(1)}, u32[]{:S(2)}, u32[]{:S(2)}) async-start(bf16[16,96,1024]{2,1,0:T(8,128)(2,1)} %shard_map.37), calls=%async_computation.1 | async-start | bytes 6291456 | tf_op jit(solution)/shard_map/all_to_all | solution.py:92
  153.3 25.4 %all-to-all-start.5 = ((bf16[16,48,128]{2,1,0:T(8,128)(2,1)}), bf16[16,48,128]{2,1,0:T(8,128)(2,1)S(1)}, u32[]{:S(2)}, u32[]{:S(2)}) async-start(bf16[16,48,128]{2,1,0:T(8,128)(2,1)} %bitcast.16), calls=%async_computation.5 | async-start | bytes 393216 | tf_op jit(solution)/shard_map/all_to_all | solution.py:92
  178.7 19.4 %all-to-all-start.2 = ((bf16[16,48,128]{2,1,0:T(8,128)(2,1)}), bf16[16,48,128]{2,1,0:T(8,128)(2,1)S(1)}, u32[]{:S(2)}, u32[]{:S(2)}) async-start(bf16[16,48,128]{2,1,0:T(8,128)(2,1)} %bitcast.11), calls=%async_computation.2 | async-start | bytes 393216 | tf_op jit(solution)/shard_map/all_to_all | solution.py:92
  198.8 19.5 %all-to-all-start.6 = ((bf16[16,48,128]{2,1,0:T(8,128)(2,1)}), bf16[16,48,128]{2,1,0:T(8,128)(2,1)S(1)}, u32[]{:S(2)}, u32[]{:S(2)}) async-start(bf16[16,48,128]{2,1,0:T(8,128)(2,1)} %broadcast_in_dim.16), calls=%async_computation.6 | async-start | bytes 393216 | tf_op jit(solution)/shard_map/all_to_all | solution.py:92
  219.0 19.5 %all-to-all-start.3 = ((bf16[16,48,128]{2,1,0:T(8,128)(2,1)}), bf16[16,48,128]{2,1,0:T(8,128)(2,1)S(1)}, u32[]{:S(2)}, u32[]{:S(2)}) async-start(bf16[16,48,128]{2,1,0:T(8,128)(2,1)} %broadcast_in_dim.15), calls=%async_computation.3 | async-start | bytes 393216 | tf_op jit(solution)/shard_map/all_to_all | solution.py:92
  238.6 8.9 %collective-permute-start.2 = (bf16[96,2048]{1,0:T(8,128)(2,1)S(1)}, bf16[96,2048]{1,0:T(8,128)(2,1)S(1)}, u32[]{:S(2)}, u32[]{:S(2)}) collective-permute-start(bf16[96,2048]{1,0:T(8,128)(2,1)S(1)} %bitcast_dynamic-update-slice_fusion), channel_id=1, source_target_pairs={{0,1},{1,0},{2,3},{3,2},{4,5},{5,4},{6,7},{7,6},{8,9},{9,8},{10,11... | collective-permute-start | bytes 1179656 | tf_op jit(solution)/shard_map/ppermute | solution.py:130

commit v2 on v1

v2 whole, which is shorter than its diff:
```python
import functools

import jax
import jax.numpy as jnp
from jax import lax
from jax.experimental import pallas as pl
from jax.experimental.pallas import tpu as pltpu
from jax.sharding import Mesh, PartitionSpec as P

SWAP = [(0, 1), (1, 0)]
MIX = 73244475
SIDE = 4


def factor(base, offset):
    k = base + offset
    k = k ^ lax.shift_right_logical(k, 16)
    k = k * MIX
    k = k ^ lax.shift_right_logical(k, 16)
    k = k * MIX
    k = (k ^ lax.shift_right_logical(k, 16)) & 65535
    return k.astype(jnp.float32) + 491520.0


def column_kernel(place, h_ref, g_ref, words_ref, *refs, tile):
    more_ref, out_ref, base_ref = refs if len(refs) == 3 else (None, *refs)
    owner = pl.program_id(0)
    x, group0 = place[0], place[1]
    owner_y, owner_x = owner >> 2, owner & 3
    rows, width = out_ref.shape[2:]
    lane = lax.broadcasted_iota(jnp.int32, (8, 128), 1)
    sub = lax.broadcasted_iota(jnp.int32, (8, 128), 0)
    shared = 65599 * (lane >> 5) + 131071 * sub + (131071 * rows * owner + 65599 * group0)
    keepers = (
        ((owner_y & 2) * 4 + x, 0),
        (((owner_y & 2) | 1) * 4 + x, 0),
        (owner_y * 4 + x, 1),
        (owner_y * 4 + ((owner_x & 2) | (x & 1)), 2),
        (owner, 3),
    )
    for at, (keeper, step) in enumerate(keepers):
        base_ref[at] = words_ref[pl.ds(keeper, 1), :] + shared + 7919 * step

    def columns(at, carry):
        first = pl.multiple_of(at * tile, tile)

        def product(y):
            return jnp.dot(h_ref[y], g_ref[y, :, pl.ds(first, tile)], preferred_element_type=jnp.float32)

        pairs = [product(0) + product(2), product(1) + product(3)]
        for row in range(0, rows, 16):
            for col in range(0, tile, 128):
                halves = []
                for top in (row, row + 8):
                    offset = (at * (tile // 128) + col // 128) * (4 * 65599) + 131071 * top
                    f = [factor(base_ref[n], offset) for n in range(5)]
                    cut = (slice(top, top + 8), slice(col, col + 128))
                    summed = pairs[0][cut] * f[0] + pairs[1][cut] * f[1]
                    halves.append(summed * ((f[2] * (2.0**-38)) * ((f[3] * (2.0**-38)) * f[4])))
                block = jnp.concatenate(halves, axis=0)
                spot = (0, 0, slice(row, row + 16), pl.ds(pl.multiple_of(first + col, 128), 128))
                if more_ref is not None:
                    block = block + more_ref[spot].astype(jnp.float32)
                out_ref[spot] = block.astype(jnp.bfloat16)
        return carry

    lax.fori_loop(0, width // tile, columns, 0)


def column_part(place, h, g, words, more=None):
    sources, rows_all, tokens = h.shape
    width = g.shape[2] // 2
    owners = SIDE * SIDE
    rows = rows_all // owners
    body = functools.partial(column_kernel, tile=min(512, width))
    cell = pl.BlockSpec((1, 1, rows, width), lambda i, p: (i % SIDE, i // SIDE, 0, 0))
    specs = [
        pl.BlockSpec((sources, rows, tokens), lambda i, p: (0, i, 0)),
        pl.BlockSpec((sources, tokens, width), lambda i, p: (0, 0, p[2])),
        pl.BlockSpec(words.shape, lambda i, p: (0, 0)),
    ]
    args = [h, g, words]
    if more is not None:
        specs.append(cell)
        args.append(more)
    return pl.pallas_call(
        body,
        grid_spec=pltpu.PrefetchScalarGridSpec(
            num_scalar_prefetch=1,
            grid=(owners,),
            in_specs=specs,
            out_specs=cell,
            scratch_shapes=[pltpu.VMEM((5, 8, 128), jnp.int32)],
        ),
        out_shape=jax.ShapeDtypeStruct((SIDE, SIDE, rows, width), jnp.bfloat16),
        compiler_params=pltpu.CompilerParams(vmem_limit_bytes=24 * 2**20),
        cost_estimate=pl.CostEstimate(
            flops=2 * sources * rows_all * tokens * width, bytes_accessed=2 * rows_all * width * 2, transcendentals=0
        ),
    )(place, *args)


def exchange(blocks, axes):
    return lax.all_to_all(blocks, axes, 0, 0, tiled=True)


def added(blocks, axis=0):
    return jnp.sum(blocks.astype(jnp.float32), axis=axis).astype(jnp.bfloat16)


def per_device(hidden, grad_out, seed_table):
    depth = lax.axis_size("z")
    x, y, core = lax.axis_index("x"), lax.axis_index("y"), lax.axis_index("core")
    h = lax.all_gather(hidden[0].T, "y")
    tokens, columns = grad_out.shape[1:]
    quarter = columns // SIDE
    half = quarter // 2
    words = exchange(jnp.broadcast_to(jnp.tile(seed_table[0, 0], (1, 4)), (SIDE * SIDE, 128)), ("y", "x"))
    g = grad_out[0].reshape(tokens, SIDE, quarter).transpose(1, 0, 2)
    g, words = lax.optimization_barrier((g, words))
    g = exchange(g, "y")

    def place(which):
        return jnp.stack([x, (y * quarter + which * half) // 32, which]).astype(jnp.int32)

    sent = column_part(place(1 - core), h, g, words)
    received = lax.ppermute(sent, "core", SWAP)
    both = column_part(place(core), h, g, words, received)
    owned = added(exchange(both, "x"))

    rows = owned.shape[1]
    across = min(depth, half // 128, SIDE)
    down = depth // across
    cells = owned.reshape(SIDE, down, rows // down, across, half // across).transpose(0, 1, 3, 2, 4)
    cells = cells.reshape(SIDE * depth, rows // down, half // across)
    cells = exchange(cells, ("y", "z")).reshape(SIDE, depth, rows // down, half // across)
    cell = added(cells, 1)
    everyone = exchange(jnp.broadcast_to(cell, (depth, *cell.shape)), "z")
    here = everyone.reshape(down, across, SIDE, rows // down, half // across).transpose(0, 3, 2, 1, 4)
    here = here.reshape(rows, SIDE, half)
    there = lax.ppermute(here, "core", SWAP)
    first = core == 0
    result = jnp.stack([jnp.where(first, here, there), jnp.where(first, there, here)], axis=2)
    return result.reshape(1, rows, columns)


def solution(mesh):
    devices = mesh.devices
    zero, dp = devices.shape
    split = Mesh(devices.reshape(SIDE, zero // SIDE, dp // 2, 2), ("y", "x", "z", "core"))
    return jax.shard_map(
        per_device,
        mesh=split,
        in_specs=(
            P(("z", "core"), ("y", "x"), None),
            P(("z", "core"), ("y", "x"), None),
            P(("z", "core"), ("y", "x"), None, None),
        ),
        out_specs=P(None, ("y", "x"), None),
        check_vma=False,
    )
```

time: 252 us -> 223 us (0.88)
  blocking collectives: 0 us -> 83.7 us
  waiting for transfers between devices: 115 us -> 57.9 us
  starting transfers between devices: 65.1 us -> 25.5 us
  Pallas kernels: 55.4 us -> 27.2 us
  between operations: 0.24 us -> 13.6 us
  local copies, waits for them, and re-layouts: 8.16 us -> 13.2 us
  other arithmetic: 4.41 us -> 0.74 us
    all_to_all x7 -> x2, waiting for transfers between devices: 114 us -> 0.54 us  [exchange(): return lax.all_to_all(blocks, axes, 0, 0, tiled=True)]
    all_to_all x0 -> x3, blocking collectives: none -> 83.7 us  [exchange(): return lax.all_to_all(blocks, axes, 0, 0, tiled=True)]
    all_gather x0 -> x1, waiting for transfers between devices: none -> 52 us  [per_device(): h = lax.all_gather(hidden[0].T, 'y')]
    all_to_all x7 -> x2, starting transfers between devices: 46.9 us -> 12 us  [exchange(): return lax.all_to_all(blocks, axes, 0, 0, tiled=True)]
    pallas_call x2, Pallas kernels: 55.4 us -> 27.2 us  [column_part(): pl.pallas_call(body, grid_spec=pltpu.PrefetchScalarGridSpec(num_scalar_pr...]
    ppermute x2 -> x1, starting transfers between devices: 10.7 us -> 2.35 us  [per_device(): received = lax.ppermute(sent, 'core', SWAP)]
    another operation x2 -> x4, local copies, waits for them, and re-layouts: 0.09 us -> 4.06 us  [the longest x1 2.51 us: per_device(): g = grad_out[0].reshape(tokens, SIDE, quarter).transpose(1, 0, 2)]
    ppermute x1, starting transfers between devices: 7.52 us -> 11.1 us  [per_device(): there = lax.ppermute(here, 'core', SWAP)]
  transfers between devices with their start and end apart: 10 -> 5, of which waited for: 8 -> 4; matrix products, arithmetic and copies ran while one was open for 3% -> 5% of each run, Pallas kernels for 11% -> 0%
where the time goes in v2:
time: 223 us; the launch traced here: 222 us
  blocking collectives  83.7 us (38%)
  waiting for transfers between devices  57.9 us (26%)
  Pallas kernels  27.2 us (12%)
  starting transfers between devices  25.5 us (11%)
  between operations  13.6 us (6%)
  local copies, waits for them, and re-layouts  13.2 us (6%)
    all_to_all x3, blocking collectives, exchange(): return lax.all_to_all(blocks, axes, 0, 0, tiled=True)  83.7 us
    all_gather x1, waiting for transfers between devices, per_device(): h = lax.all_gather(hidden[0].T, 'y')  52 us
    pallas_call x2, Pallas kernels, column_part(): pl.pallas_call(body, grid_spec=pltpu.PrefetchScalarGridSpec(num_scalar_pr...  27.2 us
    all_to_all x2, starting transfers between devices, exchange(): return lax.all_to_all(blocks, axes, 0, 0, tiled=True)  12 us
    ppermute x1, starting transfers between devices, per_device(): there = lax.ppermute(here, 'core', SWAP)  11.1 us
  transfers between devices with their start and end apart: 5, of which 4 were waited for; matrix products, arithmetic and copies ran while one was open for 5% of the time, Pallas kernels for 0%

profile of v2, /device:TPU:1, one launch (start us, length us, event | category | flops | bytes accessed | tf_op | source)
XLA Modules:
  0.0 221.6 jit_solution(1934469908873211017)
XLA Ops:
  6.5 0.0 all-gather.3.cloned.1.call-start
  6.5 0.7 all-gather.3.cloned.1.call-update
  7.3 0.7 tile.11
  7.9 0.1 tile.12
  8.0 0.6 broadcast_in_dim.8
  8.6 7.6 %all-to-all-start = ((s32[16,1,128]{2,1,0:T(1,128)}), s32[16,1,128]{2,1,0:T(1,128)S(1)}, u32[]{:S(2)}, u32[]{:S(2)}) async-start(s32[16,1,128]{2,1,0:T(1,128)} %broadcast_in_dim.8), calls=%async_computation | async-start | bytes 16384 | tf_op jit(solution)/shard_map/all_to_all | solution.py:104
  16.2 3.3 %copy.17 = bf16[1,256,4096]{1,2,0:T(8,128)(2,1)S(1)} copy(bf16[1,256,4096]{2,1,0:T(8,128)(2,1)} %param.4) | data formatting | bytes 4194304 | tf_op args[1]
  19.5 2.5 %copy.18 = bf16[256,4,1024]{2,0,1:T(8,128)(2,1)} copy(bf16[256,4,1024]{0,2,1:T(8,128)(2,1)S(1)} %bitcast.32) | data formatting | bytes 4194304 | tf_op jit(solution)/shard_map/reshape;squeeze | solution.py:119
  22.0 0.5 all-to-all-done
  22.5 4.4 %all-to-all-start.1 = ((bf16[4,256,1024]{2,1,0:T(8,128)(2,1)}), bf16[4,256,1024]{2,1,0:T(8,128)(2,1)}, u32[]{:S(2)}, u32[]{:S(2)}) async-start(bf16[4,256,1024]{2,1,0:T(8,128)(2,1)} %bitcast.7), calls=%async_computation.1 | async-start | bytes 4194304 | tf_op jit(solution)/shard_map/all_to_all | solution.py:104
  27.0 0.1 pad_add_fusion.1.place
  27.1 52.0 %all-gather.3.cloned.1.call-done = bf16[6144,256]{0,1:T(8,128)(2,1)} async-done(((bf16[1536,256]{0,1:T(8,128)(2,1)}), bf16[6144,256]{0,1:T(8,128)(2,1)}) %all-gather.3.cloned.1.call-update) | async-done | bytes 3145744 | tf_op jit(solution)/shard_map/all_gather | solution.py:114
  79.1 3.2 %copy.16 = bf16[6144,256]{1,0:T(8,128)(2,1)S(1)} copy(bf16[6144,256]{0,1:T(8,128)(2,1)} %all-gather.3.cloned.1.call-done) | data formatting | bytes 6291456 | tf_op jit(solution)/shard_map/all_gather | solution.py:114
  82.3 0.0 all-to-all-done.1.g_ref
  82.3 12.9 %shard_map.37 = bf16[4,4,96,512]{3,2,1,0:T(8,128)(2,1)} custom-call(s32[3]{0:T(128)S(1)} %pad_add_fusion.1.place, bf16[4,1536,256]{2,1,0:T(8,128)(2,1)S(1)} %bitcast.28, bf16[4,256,1024]{2,1,0:T(8,128)(2,1)} %all-to-all-done.1.g_ref, s32[16,128]{1,0:T(8,128)S(1)} %bitcast.30), custom_call_target="tpu_custom_call" | custom-call | flops 1610612736 | bytes 3145728 | tf_op jit(solution)/shard_map/pallas_call | solution.py:86
  95.2 2.4 %collective-permute-start = (bf16[4,4,96,512]{3,2,1,0:T(8,128)(2,1)}, bf16[4,4,96,512]{3,2,1,0:T(8,128)(2,1)}, u32[]{:S(2)}, u32[]{:S(2)}) collective-permute-start(bf16[4,4,96,512]{3,2,1,0:T(8,128)(2,1)} %shard_map.37), channel_id=1, source_target_pairs={{0,1},{1,0},{2,3},{3,2},{4,5},{5,4},{6,7},{7,6},{8,9},{9,8},{10,11... | collective-permute-start | bytes 4718600 | tf_op jit(solution)/shard_map/ppermute | solution.py:127
  97.6 0.1 pad_add_fusion.place
  97.7 3.3 %collective-permute-done.refs_0_ = bf16[4,4,96,512]{3,2,1,0:T(8,128)(2,1)} collective-permute-done((bf16[4,4,96,512]{3,2,1,0:T(8,128)(2,1)}, bf16[4,4,96,512]{3,2,1,0:T(8,128)(2,1)}, u32[]{:S(2)}, u32[]{:S(2)}) %collective-permute-start) | collective-permute-done | bytes 1572896 | tf_op jit(solution)/shard_map/ppermute | solution.py:127
  100.9 14.2 %shard_map.38 = bf16[4,4,96,512]{3,2,1,0:T(8,128)(2,1)S(1)} custom-call(s32[3]{0:T(128)S(1)} %pad_add_fusion.place, bf16[4,1536,256]{2,1,0:T(8,128)(2,1)S(1)} %bitcast.29, bf16[4,256,1024]{2,1,0:T(8,128)(2,1)} %all-to-all-done.1.g_ref, s32[16,128]{1,0:T(8,128)S(1)} %bitcast.31, bf16[4,4,96,512]{3,2,1,0:T(8,128)(2,1)} %collective-permute-done.refs_0_), custom_call_target="tpu_custom_call" | custom-call | flops 1610612736 | bytes 3145728 | tf_op jit(solution)/shard_map/pallas_call | solution.py:86
  115.2 23.3 %all_to_all.29 = bf16[4,4,96,512]{3,2,1,0:T(8,128)(2,1)S(1)} all-to-all(bf16[4,4,96,512]{3,2,1,0:T(8,128)(2,1)S(1)} %shard_map.38), channel_id=1, replica_groups=mesh['y'=4,'x'=4,'z'=16,'core'=2] {'x'}, dimensions={0} | all-to-all | bytes 3145728 | tf_op jit(solution)/shard_map/all_to_all | solution.py:104
  138.4 0.4 reduce_sum.24
  138.8 0.1 reshape.28
  138.9 0.1 copy.19
  139.0 39.5 %all_to_all.30 = bf16[64,24,128]{2,1,0:T(8,128)(2,1)S(1)} all-to-all(bf16[64,24,128]{2,1,0:T(8,128)(2,1)S(1)} %bitcast.34), channel_id=1, replica_groups=mesh['y'=4,'x'=4,'z'=16,'core'=2] {'y','z'}, dimensions={0} | all-to-all | bytes 786432 | tf_op jit(solution)/shard_map/all_to_all | solution.py:104
  178.5 0.1 bitcast_reduce_fusion
  178.6 0.1 broadcast_in_dim.9
  178.7 20.9 %all_to_all.31 = bf16[16,4,24,128]{3,2,1,0:T(8,128)(2,1)S(1)} all-to-all(bf16[16,4,24,128]{3,2,1,0:T(8,128)(2,1)S(1)} %broadcast_in_dim.9), channel_id=1, replica_groups=mesh['y'=4,'x'=4,'z'=16,'core'=2] {'z'}, dimensions={0} | all-to-all | bytes 786432 | tf_op jit(solution)/shard_map/all_to_all | solution.py:104
  199.5 0.2 copy.20
  199.7 0.2 reshape.32
  199.9 11.1 %collective-permute-start.1 = (bf16[96,4,512]{2,0,1:T(8,128)(2,1)S(1)}, bf16[96,4,512]{2,0,1:T(8,128)(2,1)S(1)}, u32[]{:S(2)}, u32[]{:S(2)}) collective-permute-start(bf16[96,4,512]{2,0,1:T(8,128)(2,1)S(1)} %reshape.32), channel_id=1, source_target_pairs={{0,1},{1,0},{2,3},{3,2},{4,5},{5,4},{6,7},{7,6},{8,9},{9,8},{10,11... | collective-permute-start | bytes 1179656 | tf_op jit(solution)/shard_map/ppermute | solution.py:141
  211.0 1.3 collective-permute-done.1
  212.4 0.1 select_bitcast_fusion.1
  212.4 0.1 pad_maximum_fusion
  212.5 0.8 copy.22
  213.3 1.5 reshape.33
Async XLA Ops:
  6.5 72.6 %all-gather.3.cloned.1.call-start = ((), (), s32[]{:S(2)}) async-start(), calls=%async_computation.5 | async-start | bytes 3932160 | tf_op jit(solution)/shard_map/all_gather | solution.py:114
  8.6 13.9 %all-to-all-start = ((s32[16,1,128]{2,1,0:T(1,128)}), s32[16,1,128]{2,1,0:T(1,128)S(1)}, u32[]{:S(2)}, u32[]{:S(2)}) async-start(s32[16,1,128]{2,1,0:T(1,128)} %broadcast_in_dim.8), calls=%async_computation | async-start | bytes 16384 | tf_op jit(solution)/shard_map/all_to_all | solution.py:104
  22.5 59.7 %all-to-all-start.1 = ((bf16[4,256,1024]{2,1,0:T(8,128)(2,1)}), bf16[4,256,1024]{2,1,0:T(8,128)(2,1)}, u32[]{:S(2)}, u32[]{:S(2)}) async-start(bf16[4,256,1024]{2,1,0:T(8,128)(2,1)} %bitcast.7), calls=%async_computation.1 | async-start | bytes 4194304 | tf_op jit(solution)/shard_map/all_to_all | solution.py:104
  95.2 5.7 %collective-permute-start = (bf16[4,4,96,512]{3,2,1,0:T(8,128)(2,1)}, bf16[4,4,96,512]{3,2,1,0:T(8,128)(2,1)}, u32[]{:S(2)}, u32[]{:S(2)}) collective-permute-start(bf16[4,4,96,512]{3,2,1,0:T(8,128)(2,1)} %shard_map.37), channel_id=1, source_target_pairs={{0,1},{1,0},{2,3},{3,2},{4,5},{5,4},{6,7},{7,6},{8,9},{9,8},{10,11... | collective-permute-start | bytes 4718600 | tf_op jit(solution)/shard_map/ppermute | solution.py:127
  199.9 12.5 %collective-permute-start.1 = (bf16[96,4,512]{2,0,1:T(8,128)(2,1)S(1)}, bf16[96,4,512]{2,0,1:T(8,128)(2,1)S(1)}, u32[]{:S(2)}, u32[]{:S(2)}) collective-permute-start(bf16[96,4,512]{2,0,1:T(8,128)(2,1)S(1)} %reshape.32), channel_id=1, source_target_pairs={{0,1},{1,0},{2,3},{3,2},{4,5},{5,4},{6,7},{7,6},{8,9},{9,8},{10,11... | collective-permute-start | bytes 1179656 | tf_op jit(solution)/shard_map/ppermute | solution.py:141
Sparse Core Ops, SparseCore 0:
  9.5 69.5 all-gather.2

commit v3 on v2

v3 whole, which is shorter than its diff:
```python
import jax
import jax.numpy as jnp
from jax import lax
from jax.experimental import pallas as pl
from jax.experimental.pallas import tpu as pltpu
from jax.sharding import Mesh, PartitionSpec as P

SWAP = [(0, 1), (1, 0)]
MIX = 73244475
SIDE = 4
OWNERS = SIDE * SIDE


def factor(base, offset):
    k = base + offset
    k = k ^ lax.shift_right_logical(k, 16)
    k = k * MIX
    k = k ^ lax.shift_right_logical(k, 16)
    k = k * MIX
    k = (k ^ lax.shift_right_logical(k, 16)) & 65535
    return k.astype(jnp.float32) + 491520.0


def factor_kernel(place, words_ref, out_ref, base_ref, *, tile):
    owner = pl.program_id(0)
    x, y, group0 = place[0], place[1], place[2]
    owner_y, owner_x = owner >> 2, owner & 3
    rows, width = out_ref.shape[1:]
    lane = lax.broadcasted_iota(jnp.int32, (8, 128), 1)
    sub = lax.broadcasted_iota(jnp.int32, (8, 128), 0)
    shared = 65599 * (lane >> 5) + 131071 * sub + (131071 * rows * owner + 65599 * group0)
    keepers = (
        (((owner_y & 2) | (y & 1)) * 4 + x, 0),
        (((owner_y & 2) | (1 - (y & 1))) * 4 + x, 0),
        (owner_y * 4 + x, 1),
        (owner_y * 4 + ((owner_x & 2) | (x & 1)), 2),
        (owner, 3),
    )
    for at, (keeper, step) in enumerate(keepers):
        base_ref[at] = words_ref[pl.ds(keeper, 1), :] + shared + 7919 * step

    def columns(at, carry):
        first = pl.multiple_of(at * tile, tile)
        for row in range(0, rows, 16):
            for col in range(0, tile, 128):
                halves = ([], [])
                for top in (row, row + 8):
                    offset = (at * (tile // 128) + col // 128) * (4 * 65599) + 131071 * top
                    f = [factor(base_ref[n], offset) for n in range(5)]
                    later = (f[2] * (2.0**-38)) * ((f[3] * (2.0**-38)) * f[4])
                    for pair in range(2):
                        halves[pair].append(f[pair] * later - 1.0)
                for pair in range(2):
                    block = jnp.concatenate(halves[pair], axis=0).astype(jnp.bfloat16)
                    out_ref[pair, row : row + 16, pl.ds(pl.multiple_of(first + col, 128), 128)] = block
        return carry

    lax.fori_loop(0, width // tile, columns, 0)


def factors(place, words, rows_all, width):
    rows = rows_all // OWNERS

    def body(*refs):
        factor_kernel(*refs, tile=min(512, width))

    return pl.pallas_call(
        body,
        grid_spec=pltpu.PrefetchScalarGridSpec(
            num_scalar_prefetch=1,
            grid=(OWNERS,),
            in_specs=[pl.BlockSpec(words.shape, lambda i, p: (0, 0))],
            out_specs=pl.BlockSpec((2, rows, width), lambda i, p: (0, i, 0)),
            scratch_shapes=[pltpu.VMEM((5, 8, 128), jnp.int32)],
        ),
        out_shape=jax.ShapeDtypeStruct((2, rows_all, width), jnp.bfloat16),
        compiler_params=pltpu.CompilerParams(vmem_limit_bytes=8 * 2**20),
        cost_estimate=pl.CostEstimate(
            flops=1000 * rows_all * width * 10, bytes_accessed=2 * rows_all * width * 2, transcendentals=0
        ),
    )(place, words)


def pairs_kernel(place, h0, h2a, h2b, h1, h3, g0, g2, g1, g3, f_ref, *refs):
    more_ref, out_ref = refs if len(refs) == 2 else (None, *refs)

    def product(h, g):
        return jnp.dot(h, g[0], preferred_element_type=jnp.float32)

    facing = jnp.concatenate([h2a[...], h2b[...]], axis=1)
    near = product(h0[...], g0) + product(facing, g2)
    far = product(h1[...], g1) + product(h3[...], g3)
    total = near + near * f_ref[0].astype(jnp.float32) + (far + far * f_ref[1].astype(jnp.float32))
    if more_ref is not None:
        total = total + more_ref[...].astype(jnp.float32)
    out_ref[...] = total.astype(jnp.bfloat16)


def pairs(place, h, g, scale, more=None):
    rows_all, tokens = h[0].shape
    width = g.shape[2] // 2
    rows = rows_all // SIDE
    cell = pl.BlockSpec((rows, width), lambda i, p: (i, 0))

    def source(at):
        return pl.BlockSpec((1, tokens, width), lambda i, p: (p[at], 0, p[4]))

    specs = [pl.BlockSpec((rows, block.shape[1]), lambda i, p: (i, 0)) for block in h]
    specs += [source(0), source(2), source(1), source(3)]
    specs.append(pl.BlockSpec((2, rows, width), lambda i, p: (0, i, p[4])))
    args = [*h, g, g, g, g, scale]
    if more is not None:
        specs.append(cell)
        args.append(more)
    return pl.pallas_call(
        pairs_kernel,
        grid_spec=pltpu.PrefetchScalarGridSpec(num_scalar_prefetch=1, grid=(SIDE,), in_specs=specs, out_specs=cell),
        out_shape=jax.ShapeDtypeStruct((rows_all, width), jnp.bfloat16),
        compiler_params=pltpu.CompilerParams(vmem_limit_bytes=24 * 2**20),
        cost_estimate=pl.CostEstimate(
            flops=8 * rows_all * tokens * width, bytes_accessed=3 * rows_all * width * 2, transcendentals=0
        ),
    )(place, *args)


def exchange(blocks, axes):
    return lax.all_to_all(blocks, axes, 0, 0, tiled=True)


def added(blocks, axis=0):
    return jnp.sum(blocks.astype(jnp.float32), axis=axis).astype(jnp.bfloat16)


def along_y(block, step):
    return lax.ppermute(block, "y", [(at, (at + step) % SIDE) for at in range(SIDE)])


def per_device(hidden, grad_out, seed_table):
    depth = lax.axis_size("z")
    x, y, core = lax.axis_index("x"), lax.axis_index("y"), lax.axis_index("core")
    tokens, columns = grad_out.shape[1:]
    quarter = columns // SIDE
    half = quarter // 2
    words = exchange(jnp.broadcast_to(jnp.tile(seed_table[0, 0], (1, 4)), (OWNERS, 128)), ("y", "x"))

    h_own = hidden[0].T
    h_low = along_y(h_own, 1)
    h_high = along_y(h_own, -1)
    h_facing_a = along_y(h_low[:, : tokens // 2], 1)
    h_facing_b = along_y(h_high[:, tokens // 2 :], -1)
    h = [h_own, h_facing_a, h_facing_b, h_high, h_low]

    g = grad_out[0].reshape(tokens, SIDE, quarter).transpose(1, 0, 2)
    g, words = lax.optimization_barrier((g, words))
    g = exchange(g, "y")

    rows_all = h_own.shape[0]
    scale = factors(jnp.stack([x, y, y * quarter // 32]).astype(jnp.int32), words, rows_all, quarter)

    def place(which):
        return jnp.stack([y, (y + 1) % SIDE, (y + 2) % SIDE, (y + 3) % SIDE, which]).astype(jnp.int32)

    sent = pairs(place(1 - core), h, g, scale)
    received = lax.ppermute(sent, "core", SWAP)
    both = pairs(place(core), h, g, scale, received)

    rows = rows_all // OWNERS
    got = exchange(both.reshape(OWNERS, rows, half), ("y", "x"))
    owned = added(got.reshape(SIDE, SIDE, rows, half), 1)
    lanes = half // SIDE
    cells = owned.reshape(SIDE, rows, SIDE, lanes).transpose(0, 2, 1, 3).reshape(depth, OWNERS // depth, rows, lanes)
    cell = added(exchange(cells, "z"))
    everyone = exchange(jnp.broadcast_to(cell, cells.shape), "z")
    here = everyone.reshape(SIDE, SIDE, rows, lanes).transpose(2, 0, 1, 3).reshape(rows, SIDE, half)
    there = lax.ppermute(here, "core", SWAP)
    first = core == 0
    result = jnp.stack([jnp.where(first, here, there), jnp.where(first, there, here)], axis=2)
    return result.reshape(1, rows, columns)


def solution(mesh):
    devices = mesh.devices
    zero, dp = devices.shape
    split = Mesh(devices.reshape(SIDE, zero // SIDE, dp // 2, 2), ("y", "x", "z", "core"))
    return jax.shard_map(
        per_device,
        mesh=split,
        in_specs=(
            P(("z", "core"), ("y", "x"), None),
            P(("z", "core"), ("y", "x"), None),
            P(("z", "core"), ("y", "x"), None, None),
        ),
        out_specs=P(None, ("y", "x"), None),
        check_vma=False,
    )
```

time: 223 us -> 193 us (0.87)
  waiting for transfers between devices: 57.9 us -> 13.2 us
  starting transfers between devices: 25.5 us -> 39.2 us
  between operations: 13.6 us -> 0.22 us
  local copies, waits for them, and re-layouts: 13.2 us -> 24.2 us
  blocking collectives: 83.7 us -> 88.1 us
    all_gather x1 -> x0, waiting for transfers between devices: 52 us -> none  [per_device(): h = lax.all_gather(hidden[0].T, 'y')]
    ppermute x0 -> x4, starting transfers between devices: none -> 13.9 us  [along_y(): lax.ppermute(block, 'y', [(at, (at + step) % SIDE) for at in range(SIDE)])]
    unnamed x1 -> x14, local copies, waits for them, and re-layouts: 3.28 us -> 15.6 us
    all_to_all x3, blocking collectives: 83.7 us -> 88.1 us  [exchange(): return lax.all_to_all(blocks, axes, 0, 0, tiled=True)]
    ppermute x0 -> x4, waiting for transfers between devices: none -> 4.33 us  [along_y(): lax.ppermute(block, 'y', [(at, (at + step) % SIDE) for at in range(SIDE)])]
    all_to_all x2, waiting for transfers between devices: 0.54 us -> 4.25 us  [exchange(): return lax.all_to_all(blocks, axes, 0, 0, tiled=True)]
    all_gather x1 -> x0, local copies, waits for them, and re-layouts: 3.17 us -> none  [per_device(): h = lax.all_gather(hidden[0].T, 'y')]
    ppermute x1, starting transfers between devices: 2.35 us -> 5.41 us  [per_device(): received = lax.ppermute(sent, 'core', SWAP)]
  transfers between devices with their start and end apart: 5 -> 8, of which waited for: 4 -> 5; matrix products, arithmetic and copies ran while one was open for 5% -> 5% of each run, Pallas kernels for 0% -> 8%
where the time goes in v3:
time: 193 us; the launch traced here: 192 us
  blocking collectives  88.1 us (46%)
  starting transfers between devices  39.2 us (20%)
  Pallas kernels  26.8 us (14%)
  local copies, waits for them, and re-layouts  24.2 us (13%)
  waiting for transfers between devices  13.2 us (7%)
    all_to_all x3, blocking collectives, exchange(): return lax.all_to_all(blocks, axes, 0, 0, tiled=True)  88.1 us
    pallas_call x1, Pallas kernels, factors(): pl.pallas_call(body, grid_spec=pltpu.PrefetchScalarGridSpec(num_scalar_pr...  16.3 us
    unnamed x14, local copies, waits for them, and re-layouts  15.6 us
    ppermute x4, starting transfers between devices, along_y(): lax.ppermute(block, 'y', [(at, (at + step) % SIDE) for at in range(SIDE)])  13.9 us
    pallas_call x2, Pallas kernels, pairs(): pl.pallas_call(pairs_kernel, grid_spec=pltpu.PrefetchScalarGridSpec(num_s...  10.6 us
    all_to_all x2, starting transfers between devices, exchange(): return lax.all_to_all(blocks, axes, 0, 0, tiled=True)  10.1 us
    ppermute x1, starting transfers between devices, per_device(): there = lax.ppermute(here, 'core', SWAP)  9.79 us
    ppermute x1, starting transfers between devices, per_device(): received = lax.ppermute(sent, 'core', SWAP)  5.41 us
  transfers between devices with their start and end apart: 8, of which 5 were waited for; matrix products, arithmetic and copies ran while one was open for 5% of the time, Pallas kernels for 8%

profile of v3, /device:TPU:1, one launch (start us, length us, event | category | flops | bytes accessed | tf_op | source)
XLA Modules:
  0.0 192.2 jit_solution(9369876310772636187)
XLA Ops:
  0.0 1.4 copy.21
  1.4 5.5 %collective-permute-start.2 = (bf16[1536,256]{1,0:T(8,128)(2,1)S(1)}, bf16[1536,256]{1,0:T(8,128)(2,1)}, u32[]{:S(2)}, u32[]{:S(2)}) collective-permute-start(bf16[1536,256]{1,0:T(8,128)(2,1)S(1)} %bitcast.39), channel_id=1, source_target_pairs={{0,384},{128,0},{256,128},{384,256},{1,385},{129,1},{257,129},{385... | collective-permute-start | bytes 2359304 | tf_op jit(solution)/shard_map/ppermute | solution.py:135
  6.9 1.9 collective-permute-start
  8.8 0.7 tile.11
  9.5 0.1 tile.12
  9.6 0.6 broadcast_in_dim.8
  10.2 6.5 %all-to-all-start = ((s32[16,1,128]{2,1,0:T(1,128)}), s32[16,1,128]{2,1,0:T(1,128)S(1)}, u32[]{:S(2)}, u32[]{:S(2)}) async-start(s32[16,1,128]{2,1,0:T(1,128)} %broadcast_in_dim.8), calls=%async_computation | async-start | bytes 16384 | tf_op jit(solution)/shard_map/all_to_all | solution.py:127
  16.7 3.3 %copy.22 = bf16[1,256,4096]{1,2,0:T(8,128)(2,1)S(1)} copy(bf16[1,256,4096]{2,1,0:T(8,128)(2,1)} %param.4) | data formatting | bytes 4194304 | tf_op args[1]
  20.0 2.5 %copy.23 = bf16[256,4,1024]{2,0,1:T(8,128)(2,1)} copy(bf16[256,4,1024]{0,2,1:T(8,128)(2,1)S(1)} %bitcast.46) | data formatting | bytes 4194304 | tf_op jit(solution)/shard_map/reshape;squeeze | solution.py:153
  22.5 0.1 stack.57.place
  22.6 4.2 %all-to-all-done = s32[16,1,128]{2,1,0:T(1,128)S(1)} async-done(((s32[16,1,128]{2,1,0:T(1,128)}), s32[16,1,128]{2,1,0:T(1,128)S(1)}, u32[]{:S(2)}, u32[]{:S(2)}) %all-to-all-start) | async-done | bytes 8224 | tf_op jit(solution)/shard_map/all_to_all | solution.py:127
  26.8 3.6 %all-to-all-start.1 = ((bf16[4,256,1024]{2,1,0:T(8,128)(2,1)}), bf16[4,256,1024]{2,1,0:T(8,128)(2,1)S(1)}, u32[]{:S(2)}, u32[]{:S(2)}) async-start(bf16[4,256,1024]{2,1,0:T(8,128)(2,1)} %bitcast.45), calls=%async_computation.1 | async-start | bytes 4194304 | tf_op jit(solution)/shard_map/all_to_all | solution.py:127
  30.4 0.1 pad_add_fusion.refs_0_
  30.5 0.0 collective-permute-done.2.h1
  30.5 1.0 slice.9
  31.5 4.5 %collective-permute-start.3 = (bf16[1536,128]{1,0:T(8,128)(2,1)S(1)}, bf16[1536,128]{1,0:T(8,128)(2,1)S(1)}, u32[]{:S(2)}, u32[]{:S(2)}) collective-permute-start(bf16[1536,128]{1,0:T(8,128)(2,1)S(1)} %slice.9), channel_id=1, source_target_pairs={{0,384},{128,0},{256,128},{384,256},{1,385},{129,1},{257,129},{385... | collective-permute-start | bytes 1179656 | tf_op jit(solution)/shard_map/ppermute | solution.py:135
  36.1 0.0 collective-permute-done.h3
  36.1 1.0 slice.8
  37.1 1.9 collective-permute-start.1
  39.1 16.3 %shard_map.37.f_ref = bf16[2,1536,1024]{2,1,0:T(8,128)(2,1)S(1)} custom-call(s32[3]{0:T(128)S(1)} %pad_add_fusion.refs_0_, s32[16,128]{1,0:T(8,128)S(1)} %bitcast.44), custom_call_target="tpu_custom_call" | custom-call | flops 15728640000 | bytes 6291456 | tf_op jit(solution)/shard_map/pallas_call | solution.py:67
  55.3 0.0 copy-start
  55.3 2.6 %copy-done = bf16[2,1536,1024]{2,1,0:T(8,128)(2,1)} copy-done((bf16[2,1536,1024]{2,1,0:T(8,128)(2,1)}, bf16[2,1536,1024]{2,1,0:T(8,128)(2,1)S(1)}, u32[]{:S(2)}) %copy-start) | copy-done | bytes 6291480
  58.0 2.4 %collective-permute-done.3.h2b = bf16[1536,128]{1,0:T(8,128)(2,1)S(1)} collective-permute-done((bf16[1536,128]{1,0:T(8,128)(2,1)S(1)}, bf16[1536,128]{1,0:T(8,128)(2,1)S(1)}, u32[]{:S(2)}, u32[]{:S(2)}) %collective-permute-start.3) | collective-permute-done | bytes 393248 | tf_op jit(solution)/shard_map/ppermute | solution.py:135
  60.4 1.9 collective-permute-done.1.h2a
  62.3 0.0 copy-start.3
  62.3 0.7 copy-done.3
  63.1 0.0 all-to-all-done.1.g0.g2.g1.g3
  63.1 0.0 copy-start.1
  63.1 2.8 %copy-done.1 = bf16[2,1536,1024]{2,1,0:T(8,128)(2,1)S(1)} copy-done((bf16[2,1536,1024]{2,1,0:T(8,128)(2,1)S(1)}, bf16[2,1536,1024]{2,1,0:T(8,128)(2,1)}, u32[]{:S(2)}) %copy-start.1) | copy-done | bytes 6291480
  65.8 0.0 copy-start.4
  65.9 1.0 copy-done.4
  66.8 5.5 %shard_map.38 = bf16[1536,512]{1,0:T(8,128)(2,1)} custom-call(s32[5]{0:T(128)S(1)} %stack.57.place, bf16[1536,256]{1,0:T(8,128)(2,1)S(1)} %bitcast.41, bf16[1536,128]{1,0:T(8,128)(2,1)S(1)} %copy-done.4, bf16[1536,128]{1,0:T(8,128)(2,1)S(1)} %collective-permute-done.3.h2b, bf16[1536,256]{1,0:T(8,128)(2,1)} %collective-permute-done.2.h1, ...), custom_call_target="tpu_custom_call" | custom-call | flops 1610612736 | bytes 4718592 | tf_op jit(solution)/shard_map/pallas_call | solution.py:115
  72.3 5.4 %collective-permute-start.4 = (bf16[1536,512]{1,0:T(8,128)(2,1)}, bf16[1536,512]{1,0:T(8,128)(2,1)}, u32[]{:S(2)}, u32[]{:S(2)}) collective-permute-start(bf16[1536,512]{1,0:T(8,128)(2,1)} %shard_map.38), channel_id=1, source_target_pairs={{0,1},{1,0},{2,3},{3,2},{4,5},{5,4},{6,7},{7,6},{8,9},{9,8},{10,11... | collective-permute-start | bytes 4718600 | tf_op jit(solution)/shard_map/ppermute | solution.py:164
  77.8 0.1 stack.52.place
  77.8 3.3 %collective-permute-done.4.refs_0_ = bf16[1536,512]{1,0:T(8,128)(2,1)} collective-permute-done((bf16[1536,512]{1,0:T(8,128)(2,1)}, bf16[1536,512]{1,0:T(8,128)(2,1)}, u32[]{:S(2)}, u32[]{:S(2)}) %collective-permute-start.4) | collective-permute-done | bytes 1572896 | tf_op jit(solution)/shard_map/ppermute | solution.py:164
  81.1 0.0 copy-start.2
  81.1 2.8 %copy-done.2 = bf16[2,1536,1024]{2,1,0:T(8,128)(2,1)S(1)} copy-done((bf16[2,1536,1024]{2,1,0:T(8,128)(2,1)S(1)}, bf16[2,1536,1024]{2,1,0:T(8,128)(2,1)}, u32[]{:S(2)}) %copy-start.2) | copy-done | bytes 6291480
  83.9 0.0 copy-start.5
  83.9 1.0 copy-done.5
  84.9 5.1 %shard_map.39 = bf16[1536,512]{1,0:T(8,128)(2,1)S(1)} custom-call(s32[5]{0:T(128)S(1)} %stack.52.place, bf16[1536,256]{1,0:T(8,128)(2,1)S(1)} %bitcast.42, bf16[1536,128]{1,0:T(8,128)(2,1)S(1)} %copy-done.5, bf16[1536,128]{1,0:T(8,128)(2,1)S(1)} %collective-permute-done.3.h2b, bf16[1536,256]{1,0:T(8,128)(2,1)} %collective-permute-done.2.h1, ...), custom_call_target="tpu_custom_call" | custom-call | flops 1610612736 | bytes 4718592 | tf_op jit(solution)/shard_map/pallas_call | solution.py:115
  90.0 28.3 %all_to_all.29 = bf16[16,96,512]{2,1,0:T(8,128)(2,1)S(1)} all-to-all(bf16[16,96,512]{2,1,0:T(8,128)(2,1)S(1)} %bitcast.43), channel_id=1, replica_groups=mesh['y'=4,'x'=4,'z'=16,'core'=2] {'y','x'}, dimensions={0} | all-to-all | bytes 3145728 | tf_op jit(solution)/shard_map/all_to_all | solution.py:127
  118.3 0.2 bitcast_reduce_fusion
  118.5 0.1 reshape.36
  118.6 0.1 copy.24
  118.7 31.2 %all_to_all.30 = bf16[16,1,96,128]{3,2,1,0:T(8,128)(2,1)S(1)} all-to-all(bf16[16,1,96,128]{3,2,1,0:T(8,128)(2,1)S(1)} %bitcast.50), channel_id=1, replica_groups=mesh['y'=4,'x'=4,'z'=16,'core'=2] {'z'}, dimensions={0} | all-to-all | bytes 786432 | tf_op jit(solution)/shard_map/all_to_all | solution.py:127
  149.9 0.1 reduce_sum.25
  149.9 0.1 broadcast_in_dim.9
  150.0 28.6 %all_to_all.31 = bf16[16,1,96,128]{3,2,1,0:T(8,128)(2,1)S(1)} all-to-all(bf16[16,1,96,128]{3,2,1,0:T(8,128)(2,1)S(1)} %broadcast_in_dim.9), channel_id=1, replica_groups=mesh['y'=4,'x'=4,'z'=16,'core'=2] {'z'}, dimensions={0} | all-to-all | bytes 786432 | tf_op jit(solution)/shard_map/all_to_all | solution.py:127
  178.6 0.1 copy.35
  178.7 9.8 %collective-permute-start.5 = (bf16[96,4,512]{2,0,1:T(8,128)(2,1)S(1)}, bf16[96,4,512]{2,0,1:T(8,128)(2,1)S(1)}, u32[]{:S(2)}, u32[]{:S(2)}) collective-permute-start(bf16[96,4,512]{2,0,1:T(8,128)(2,1)S(1)} %bitcast.51), channel_id=1, source_target_pairs={{0,1},{1,0},{2,3},{3,2},{4,5},{5,4},{6,7},{7,6},{8,9},{9,8},{10,11... | collective-permute-start | bytes 1179656 | tf_op jit(solution)/shard_map/ppermute | solution.py:175
  188.5 1.3 collective-permute-done.5
  189.8 0.1 select_bitcast_fusion.1
  189.9 0.1 pad_maximum_fusion
  189.9 0.8 copy.28
  190.8 1.5 reshape.40
Async XLA Ops:
  1.4 29.1 %collective-permute-start.2 = (bf16[1536,256]{1,0:T(8,128)(2,1)S(1)}, bf16[1536,256]{1,0:T(8,128)(2,1)}, u32[]{:S(2)}, u32[]{:S(2)}) collective-permute-start(bf16[1536,256]{1,0:T(8,128)(2,1)S(1)} %bitcast.39), channel_id=1, source_target_pairs={{0,384},{128,0},{256,128},{384,256},{1,385},{129,1},{257,129},{385... | collective-permute-start | bytes 2359304 | tf_op jit(solution)/shard_map/ppermute | solution.py:135
  6.9 29.2 %collective-permute-start = (bf16[1536,256]{1,0:T(8,128)(2,1)S(1)}, bf16[1536,256]{1,0:T(8,128)(2,1)}, u32[]{:S(2)}, u32[]{:S(2)}) collective-permute-start(bf16[1536,256]{1,0:T(8,128)(2,1)S(1)} %bitcast.40), channel_id=1, source_target_pairs={{0,128},{128,256},{256,384},{384,0},{1,129},{129,257},{257,385},{3... | collective-permute-start | bytes 2359304 | tf_op jit(solution)/shard_map/ppermute | solution.py:135
  10.2 16.7 %all-to-all-start = ((s32[16,1,128]{2,1,0:T(1,128)}), s32[16,1,128]{2,1,0:T(1,128)S(1)}, u32[]{:S(2)}, u32[]{:S(2)}) async-start(s32[16,1,128]{2,1,0:T(1,128)} %broadcast_in_dim.8), calls=%async_computation | async-start | bytes 16384 | tf_op jit(solution)/shard_map/all_to_all | solution.py:127
  26.8 36.2 %all-to-all-start.1 = ((bf16[4,256,1024]{2,1,0:T(8,128)(2,1)}), bf16[4,256,1024]{2,1,0:T(8,128)(2,1)S(1)}, u32[]{:S(2)}, u32[]{:S(2)}) async-start(bf16[4,256,1024]{2,1,0:T(8,128)(2,1)} %bitcast.45), calls=%async_computation.1 | async-start | bytes 4194304 | tf_op jit(solution)/shard_map/all_to_all | solution.py:127
  31.5 28.9 %collective-permute-start.3 = (bf16[1536,128]{1,0:T(8,128)(2,1)S(1)}, bf16[1536,128]{1,0:T(8,128)(2,1)S(1)}, u32[]{:S(2)}, u32[]{:S(2)}) collective-permute-start(bf16[1536,128]{1,0:T(8,128)(2,1)S(1)} %slice.9), channel_id=1, source_target_pairs={{0,384},{128,0},{256,128},{384,256},{1,385},{129,1},{257,129},{385... | collective-permute-start | bytes 1179656 | tf_op jit(solution)/shard_map/ppermute | solution.py:135
  37.1 25.2 %collective-permute-start.1 = (bf16[1536,128]{1,0:T(8,128)(2,1)S(1)}, bf16[1536,128]{1,0:T(8,128)(2,1)S(1)}, u32[]{:S(2)}, u32[]{:S(2)}) collective-permute-start(bf16[1536,128]{1,0:T(8,128)(2,1)S(1)} %slice.8), channel_id=1, source_target_pairs={{0,128},{128,256},{256,384},{384,0},{1,129},{129,257},{257,385},{3... | collective-permute-start | bytes 1179656 | tf_op jit(solution)/shard_map/ppermute | solution.py:135
  55.3 2.7 %copy-start = (bf16[2,1536,1024]{2,1,0:T(8,128)(2,1)}, bf16[2,1536,1024]{2,1,0:T(8,128)(2,1)S(1)}, u32[]{:S(2)}) copy-start(bf16[2,1536,1024]{2,1,0:T(8,128)(2,1)S(1)} %shard_map.37.f_ref) | copy-start | bytes 18874372
  62.3 0.7 copy-start.3
  63.1 2.8 %copy-start.1 = (bf16[2,1536,1024]{2,1,0:T(8,128)(2,1)S(1)}, bf16[2,1536,1024]{2,1,0:T(8,128)(2,1)}, u32[]{:S(2)}) copy-start(bf16[2,1536,1024]{2,1,0:T(8,128)(2,1)} %copy-done) | copy-start | bytes 18874372
  65.8 1.0 copy-start.4
  72.3 8.8 %collective-permute-start.4 = (bf16[1536,512]{1,0:T(8,128)(2,1)}, bf16[1536,512]{1,0:T(8,128)(2,1)}, u32[]{:S(2)}, u32[]{:S(2)}) collective-permute-start(bf16[1536,512]{1,0:T(8,128)(2,1)} %shard_map.38), channel_id=1, source_target_pairs={{0,1},{1,0},{2,3},{3,2},{4,5},{5,4},{6,7},{7,6},{8,9},{9,8},{10,11... | collective-permute-start | bytes 4718600 | tf_op jit(solution)/shard_map/ppermute | solution.py:164
  81.1 2.8 %copy-start.2 = (bf16[2,1536,1024]{2,1,0:T(8,128)(2,1)S(1)}, bf16[2,1536,1024]{2,1,0:T(8,128)(2,1)}, u32[]{:S(2)}) copy-start(bf16[2,1536,1024]{2,1,0:T(8,128)(2,1)} %copy-done) | copy-start | bytes 18874372
  83.9 1.0 copy-start.5
  178.7 11.1 %collective-permute-start.5 = (bf16[96,4,512]{2,0,1:T(8,128)(2,1)S(1)}, bf16[96,4,512]{2,0,1:T(8,128)(2,1)S(1)}, u32[]{:S(2)}, u32[]{:S(2)}) collective-permute-start(bf16[96,4,512]{2,0,1:T(8,128)(2,1)S(1)} %bitcast.51), channel_id=1, source_target_pairs={{0,1},{1,0},{2,3},{3,2},{4,5},{5,4},{6,7},{7,6},{8,9},{9,8},{10,11... | collective-permute-start | bytes 1179656 | tf_op jit(solution)/shard_map/ppermute | solution.py:175

commit v4 on v3

--- a/solution.py
+++ b/solution.py
@@ -81,22 +81,19 @@
     )(place, words)
 
 
-def pairs_kernel(place, h0, h2a, h2b, h1, h3, g0, g2, g1, g3, f_ref, *refs):
-    more_ref, out_ref = refs if len(refs) == 2 else (None, *refs)
+def pairs_kernel(place, h0, h2a, h2b, h1, h3, g0, g2, g1, g3, f_ref, out_ref):
+    def product(left, right):
+        left = jnp.concatenate([part[...] for part in left], axis=1)
+        right = jnp.concatenate([part[0] for part in right], axis=0)
+        return jnp.dot(left, right, preferred_element_type=jnp.float32)
 
-    def product(h, g):
-        return jnp.dot(h, g[0], preferred_element_type=jnp.float32)
-
-    facing = jnp.concatenate([h2a[...], h2b[...]], axis=1)
-    near = product(h0[...], g0) + product(facing, g2)
-    far = product(h1[...], g1) + product(h3[...], g3)
+    near = product((h0, h2a, h2b), (g0, g2))
+    far = product((h1, h3), (g1, g3))
     total = near + near * f_ref[0].astype(jnp.float32) + (far + far * f_ref[1].astype(jnp.float32))
-    if more_ref is not None:
-        total = total + more_ref[...].astype(jnp.float32)
     out_ref[...] = total.astype(jnp.bfloat16)
 
 
-def pairs(place, h, g, scale, more=None):
+def pairs(place, h, g, scale):
     rows_all, tokens = h[0].shape
     width = g.shape[2] // 2
     rows = rows_all // SIDE
@@ -108,19 +105,15 @@
     specs = [pl.BlockSpec((rows, block.shape[1]), lambda i, p: (i, 0)) for block in h]
     specs += [source(0), source(2), source(1), source(3)]
     specs.append(pl.BlockSpec((2, rows, width), lambda i, p: (0, i, p[4])))
-    args = [*h, g, g, g, g, scale]
-    if more is not None:
-        specs.append(cell)
-        args.append(more)
     return pl.pallas_call(
         pairs_kernel,
         grid_spec=pltpu.PrefetchScalarGridSpec(num_scalar_prefetch=1, grid=(SIDE,), in_specs=specs, out_specs=cell),
         out_shape=jax.ShapeDtypeStruct((rows_all, width), jnp.bfloat16),
-        compiler_params=pltpu.CompilerParams(vmem_limit_bytes=24 * 2**20),
+        compiler_params=pltpu.CompilerParams(vmem_limit_bytes=56 * 2**20),
         cost_estimate=pl.CostEstimate(
             flops=8 * rows_all * tokens * width, bytes_accessed=3 * rows_all * width * 2, transcendentals=0
         ),
-    )(place, *args)
+    )(place, *h, g, g, g, g, scale)
 
 
 def exchange(blocks, axes):
@@ -162,7 +155,8 @@
 
     sent = pairs(place(1 - core), h, g, scale)
     received = lax.ppermute(sent, "core", SWAP)
-    both = pairs(place(core), h, g, scale, received)
+    both = pairs(place(core), h, g, scale).astype(jnp.float32) + received.astype(jnp.float32)
+    both = both.astype(jnp.bfloat16)
 
     rows = rows_all // OWNERS
     got = exchange(both.reshape(OWNERS, rows, half), ("y", "x"))

time: 193 us -> 190 us (0.984)
  local copies, waits for them, and re-layouts: 24.2 us -> 18.5 us
  waiting for transfers between devices: 13.2 us -> 9.95 us
  Pallas kernels: 26.8 us -> 30 us
  blocking collectives: 88.1 us -> 90.3 us
    unnamed x14, local copies, waits for them, and re-layouts: 15.6 us -> 9.45 us
    ppermute x1, waiting for transfers between devices: 3.27 us -> 0.01 us  [per_device(): received = lax.ppermute(sent, 'core', SWAP)]
    pallas_call x2, Pallas kernels: 10.6 us -> 13.8 us  [pairs(): pl.pallas_call(pairs_kernel, grid_spec=pltpu.PrefetchScalarGridSpec(num_s...]
    all_to_all x3, blocking collectives: 88.1 us -> 90.3 us  [exchange(): return lax.all_to_all(blocks, axes, 0, 0, tiled=True)]
  transfers between devices with their start and end apart: 8 -> 8, of which waited for: 5 -> 4; matrix products, arithmetic and copies ran while one was open for 5% -> 5% of each run, Pallas kernels for 8% -> 12%
where the time goes in v4:
time: 190 us; the launch traced here: 189 us
  blocking collectives  90.3 us (48%)
  starting transfers between devices  37.8 us (20%)
  Pallas kernels  30 us (16%)
  local copies, waits for them, and re-layouts  18.5 us (10%)
  waiting for transfers between devices  9.95 us (5%)
  other arithmetic  2.36 us (1%)
    all_to_all x3, blocking collectives, exchange(): return lax.all_to_all(blocks, axes, 0, 0, tiled=True)  90.3 us
    pallas_call x1, Pallas kernels, factors(): pl.pallas_call(body, grid_spec=pltpu.PrefetchScalarGridSpec(num_scalar_pr...  16.3 us
    ppermute x4, starting transfers between devices, along_y(): lax.ppermute(block, 'y', [(at, (at + step) % SIDE) for at in range(SIDE)])  13.9 us
    pallas_call x2, Pallas kernels, pairs(): pl.pallas_call(pairs_kernel, grid_spec=pltpu.PrefetchScalarGridSpec(num_s...  13.8 us
    all_to_all x2, starting transfers between devices, exchange(): return lax.all_to_all(blocks, axes, 0, 0, tiled=True)  10.1 us
    unnamed x14, local copies, waits for them, and re-layouts  9.45 us
    ppermute x1, starting transfers between devices, per_device(): there = lax.ppermute(here, 'core', SWAP)  8.43 us
    ppermute x1, starting transfers between devices, per_device(): received = lax.ppermute(sent, 'core', SWAP)  5.4 us
  transfers between devices with their start and end apart: 8, of which 4 were waited for; matrix products, arithmetic and copies ran while one was open for 5% of the time, Pallas kernels for 12%

profile of v4, /device:TPU:1, one launch (start us, length us, event | category | flops | bytes accessed | tf_op | source)
XLA Modules:
  0.0 189.2 jit_solution(8764660172936683548)
XLA Ops:
  0.0 0.0 copy-start.5
  0.0 1.4 copy.21
  1.4 0.0 copy-start.2
  1.4 5.5 %collective-permute-start.2 = (bf16[1536,256]{1,0:T(8,128)(2,1)S(1)}, bf16[1536,256]{1,0:T(8,128)(2,1)}, u32[]{:S(2)}, u32[]{:S(2)}) collective-permute-start(bf16[1536,256]{1,0:T(8,128)(2,1)S(1)} %bitcast.42), channel_id=1, source_target_pairs={{0,384},{128,0},{256,128},{384,256},{1,385},{129,1},{257,129},{385... | collective-permute-start | bytes 2359304 | tf_op jit(solution)/shard_map/ppermute | solution.py:128
  6.9 1.9 %collective-permute-start = (bf16[1536,256]{1,0:T(8,128)(2,1)S(1)}, bf16[1536,256]{1,0:T(8,128)(2,1)}, u32[]{:S(2)}, u32[]{:S(2)}) collective-permute-start(bf16[1536,256]{1,0:T(8,128)(2,1)S(1)} %bitcast.43), channel_id=1, source_target_pairs={{0,128},{128,256},{256,384},{384,0},{1,129},{129,257},{257,385},{3... | collective-permute-start | bytes 2359304 | tf_op jit(solution)/shard_map/ppermute | solution.py:128
  8.8 0.0 copy-done.5
  8.9 0.1 tile.12
  8.9 0.6 broadcast_in_dim.8
  9.6 6.5 %all-to-all-start = ((s32[16,1,128]{2,1,0:T(1,128)}), s32[16,1,128]{2,1,0:T(1,128)S(1)}, u32[]{:S(2)}, u32[]{:S(2)}) async-start(s32[16,1,128]{2,1,0:T(1,128)} %broadcast_in_dim.8), calls=%async_computation | async-start | bytes 16384 | tf_op jit(solution)/shard_map/all_to_all | solution.py:120
  16.1 3.3 %copy.22 = bf16[1,256,4096]{1,2,0:T(8,128)(2,1)S(1)} copy(bf16[1,256,4096]{2,1,0:T(8,128)(2,1)} %param.4) | data formatting | bytes 4194304 | tf_op args[1]
  19.4 0.0 copy-done.2
  19.4 2.5 %copy.23 = bf16[256,4,1024]{2,0,1:T(8,128)(2,1)} copy(bf16[256,4,1024]{0,2,1:T(8,128)(2,1)S(1)} %bitcast.41) | data formatting | bytes 4194304 | tf_op jit(solution)/shard_map/reshape;squeeze | solution.py:146
  21.9 0.7 stack.57.place
  22.6 4.3 %all-to-all-done = s32[16,1,128]{2,1,0:T(1,128)S(1)} async-done(((s32[16,1,128]{2,1,0:T(1,128)}), s32[16,1,128]{2,1,0:T(1,128)S(1)}, u32[]{:S(2)}, u32[]{:S(2)}) %all-to-all-start) | async-done | bytes 8224 | tf_op jit(solution)/shard_map/all_to_all | solution.py:120
  26.9 3.6 %all-to-all-start.1 = ((bf16[4,256,1024]{2,1,0:T(8,128)(2,1)}), bf16[4,256,1024]{2,1,0:T(8,128)(2,1)S(1)}, u32[]{:S(2)}, u32[]{:S(2)}) async-start(bf16[4,256,1024]{2,1,0:T(8,128)(2,1)} %bitcast.40), calls=%async_computation.1 | async-start | bytes 4194304 | tf_op jit(solution)/shard_map/all_to_all | solution.py:120
  30.5 0.1 pad_add_fusion.refs_0_
  30.5 0.0 collective-permute-done.2.h1
  30.5 1.0 slice.9
  31.6 4.5 %collective-permute-start.3 = (bf16[1536,128]{1,0:T(8,128)(2,1)S(1)}, bf16[1536,128]{1,0:T(8,128)(2,1)S(1)}, u32[]{:S(2)}, u32[]{:S(2)}) collective-permute-start(bf16[1536,128]{1,0:T(8,128)(2,1)S(1)} %slice.9), channel_id=1, source_target_pairs={{0,384},{128,0},{256,128},{384,256},{1,385},{129,1},{257,129},{385... | collective-permute-start | bytes 1179656 | tf_op jit(solution)/shard_map/ppermute | solution.py:128
  36.1 0.0 collective-permute-done.h3
  36.1 1.0 slice.8
  37.2 1.9 %collective-permute-start.1 = (bf16[1536,128]{1,0:T(8,128)(2,1)S(1)}, bf16[1536,128]{1,0:T(8,128)(2,1)S(1)}, u32[]{:S(2)}, u32[]{:S(2)}) collective-permute-start(bf16[1536,128]{1,0:T(8,128)(2,1)S(1)} %slice.8), channel_id=1, source_target_pairs={{0,128},{128,256},{256,384},{384,0},{1,129},{129,257},{257,385},{3... | collective-permute-start | bytes 1179656 | tf_op jit(solution)/shard_map/ppermute | solution.py:128
  39.1 16.3 %shard_map.37.f_ref = bf16[2,1536,1024]{2,1,0:T(8,128)(2,1)S(1)} custom-call(s32[3]{0:T(128)S(1)} %pad_add_fusion.refs_0_, s32[16,128]{1,0:T(8,128)S(1)} %bitcast.39), custom_call_target="tpu_custom_call" | custom-call | flops 15728640000 | bytes 6291456 | tf_op jit(solution)/shard_map/pallas_call | solution.py:67
  55.4 0.0 copy-start
  55.4 2.6 %copy-done = bf16[2,1536,1024]{2,1,0:T(8,128)(2,1)} copy-done((bf16[2,1536,1024]{2,1,0:T(8,128)(2,1)}, bf16[2,1536,1024]{2,1,0:T(8,128)(2,1)S(1)}, u32[]{:S(2)}) %copy-start) | copy-done | bytes 6291480
  58.0 2.4 %collective-permute-done.3.h2b = bf16[1536,128]{1,0:T(8,128)(2,1)S(1)} collective-permute-done((bf16[1536,128]{1,0:T(8,128)(2,1)S(1)}, bf16[1536,128]{1,0:T(8,128)(2,1)S(1)}, u32[]{:S(2)}, u32[]{:S(2)}) %collective-permute-start.3) | collective-permute-done | bytes 393248 | tf_op jit(solution)/shard_map/ppermute | solution.py:128
  60.4 0.0 copy-start.3
  60.4 1.9 %collective-permute-done.1.h2a = bf16[1536,128]{1,0:T(8,128)(2,1)S(1)} collective-permute-done((bf16[1536,128]{1,0:T(8,128)(2,1)S(1)}, bf16[1536,128]{1,0:T(8,128)(2,1)S(1)}, u32[]{:S(2)}, u32[]{:S(2)}) %collective-permute-start.1) | collective-permute-done | bytes 393248 | tf_op jit(solution)/shard_map/ppermute | solution.py:128
  62.3 0.0 copy-start.4
  62.3 0.0 all-to-all-done.1.g0.g2.g1.g3
  62.3 0.0 copy-done.3
  62.4 0.7 copy-done.4
  63.1 0.0 copy-start.1
  63.1 1.3 copy-done.1
  64.4 6.9 %shard_map.39 = bf16[1536,512]{1,0:T(8,128)(2,1)} custom-call(s32[5]{0:T(128)} %stack.57.place, bf16[1536,256]{1,0:T(8,128)(2,1)} %bitcast.44, bf16[1536,128]{1,0:T(8,128)(2,1)} %copy-done.4, bf16[1536,128]{1,0:T(8,128)(2,1)} %copy-done.3, bf16[1536,256]{1,0:T(8,128)(2,1)} %collective-permute-done.2.h1, bf16[1536,256]{1,0:T(8,128)(2,1)} %collective-permute-done.h3, ...), custom_call_target="tpu_custom_call" | custom-call | flops 1610612736 | bytes 4718592 | tf_op jit(solution)/shard_map/pallas_call | solution.py:108
  71.3 5.4 %collective-permute-start.4 = (bf16[1536,512]{1,0:T(8,128)(2,1)}, bf16[1536,512]{1,0:T(8,128)(2,1)S(1)}, u32[]{:S(2)}, u32[]{:S(2)}) collective-permute-start(bf16[1536,512]{1,0:T(8,128)(2,1)} %shard_map.39), channel_id=1, source_target_pairs={{0,1},{1,0},{2,3},{3,2},{4,5},{5,4},{6,7},{7,6},{8,9},{9,8},{10,11... | collective-permute-start | bytes 4718600 | tf_op jit(solution)/shard_map/ppermute | solution.py:157
  76.7 0.6 stack.52.place
  77.4 6.9 %shard_map.38 = bf16[1536,512]{1,0:T(8,128)(2,1)} custom-call(s32[5]{0:T(128)} %stack.52.place, bf16[1536,256]{1,0:T(8,128)(2,1)} %bitcast.45, bf16[1536,128]{1,0:T(8,128)(2,1)} %copy-done.4, bf16[1536,128]{1,0:T(8,128)(2,1)} %copy-done.3, bf16[1536,256]{1,0:T(8,128)(2,1)} %collective-permute-done.2.h1, bf16[1536,256]{1,0:T(8,128)(2,1)} %collective-permute-done.h3, ...), custom_call_target="tpu_custom_call" | custom-call | flops 1610612736 | bytes 4718592 | tf_op jit(solution)/shard_map/pallas_call | solution.py:108
  84.2 0.0 collective-permute-done.4
  84.2 1.8 add_convert_fusion
  86.1 28.8 %all_to_all.29 = bf16[16,96,512]{2,1,0:T(8,128)(2,1)S(1)} all-to-all(bf16[16,96,512]{2,1,0:T(8,128)(2,1)S(1)} %bitcast.46), channel_id=1, replica_groups=mesh['y'=4,'x'=4,'z'=16,'core'=2] {'y','x'}, dimensions={0} | all-to-all | bytes 3145728 | tf_op jit(solution)/shard_map/all_to_all | solution.py:120
  114.9 0.2 bitcast_reduce_fusion
  115.1 0.1 reshape.36
  115.2 0.1 copy.24
  115.3 31.0 %all_to_all.30 = bf16[16,1,96,128]{3,2,1,0:T(8,128)(2,1)S(1)} all-to-all(bf16[16,1,96,128]{3,2,1,0:T(8,128)(2,1)S(1)} %bitcast.50), channel_id=1, replica_groups=mesh['y'=4,'x'=4,'z'=16,'core'=2] {'z'}, dimensions={0} | all-to-all | bytes 786432 | tf_op jit(solution)/shard_map/all_to_all | solution.py:120
  146.3 0.1 reduce_sum.25
  146.4 0.1 broadcast_in_dim.9
  146.4 30.5 %all_to_all.31 = bf16[16,1,96,128]{3,2,1,0:T(8,128)(2,1)S(1)} all-to-all(bf16[16,1,96,128]{3,2,1,0:T(8,128)(2,1)S(1)} %broadcast_in_dim.9), channel_id=1, replica_groups=mesh['y'=4,'x'=4,'z'=16,'core'=2] {'z'}, dimensions={0} | all-to-all | bytes 786432 | tf_op jit(solution)/shard_map/all_to_all | solution.py:120
  176.9 0.1 copy.35
  177.0 8.4 %collective-permute-start.5 = (bf16[96,4,512]{2,0,1:T(8,128)(2,1)S(1)}, bf16[96,4,512]{2,0,1:T(8,128)(2,1)S(1)}, u32[]{:S(2)}, u32[]{:S(2)}) collective-permute-start(bf16[96,4,512]{2,0,1:T(8,128)(2,1)S(1)} %bitcast.51), channel_id=1, source_target_pairs={{0,1},{1,0},{2,3},{3,2},{4,5},{5,4},{6,7},{7,6},{8,9},{9,8},{10,11... | collective-permute-start | bytes 1179656 | tf_op jit(solution)/shard_map/ppermute | solution.py:169
  185.5 1.3 collective-permute-done.5
  186.8 0.1 select_bitcast_fusion.1
  186.8 0.1 pad_maximum_fusion
  186.9 0.8 copy.28
  187.7 1.5 reshape.40
  (1 shorter events, 0.0 us)
Async XLA Ops:
  0.0 8.8 %copy-start.5 = (s32[1,1,1,32]{3,2,1,0:T(1,128)S(1)}, s32[1,1,1,32]{3,2,1,0:T(1,128)}, u32[]{:S(2)}) copy-start(s32[1,1,1,32]{3,2,1,0:T(1,128)} %param.5) | copy-start | bytes 388
  1.4 18.0 %copy-start.2 = (bf16[1,256,1536]{1,2,0:T(8,128)(2,1)}, bf16[1,256,1536]{1,2,0:T(8,128)(2,1)S(1)}, u32[]{:S(2)}) copy-start(bf16[1,256,1536]{1,2,0:T(8,128)(2,1)S(1)} %copy.21) | copy-start | bytes 2359300
  1.4 29.1 %collective-permute-start.2 = (bf16[1536,256]{1,0:T(8,128)(2,1)S(1)}, bf16[1536,256]{1,0:T(8,128)(2,1)}, u32[]{:S(2)}, u32[]{:S(2)}) collective-permute-start(bf16[1536,256]{1,0:T(8,128)(2,1)S(1)} %bitcast.42), channel_id=1, source_target_pairs={{0,384},{128,0},{256,128},{384,256},{1,385},{129,1},{257,129},{385... | collective-permute-start | bytes 2359304 | tf_op jit(solution)/shard_map/ppermute | solution.py:128
  6.9 29.2 %collective-permute-start = (bf16[1536,256]{1,0:T(8,128)(2,1)S(1)}, bf16[1536,256]{1,0:T(8,128)(2,1)}, u32[]{:S(2)}, u32[]{:S(2)}) collective-permute-start(bf16[1536,256]{1,0:T(8,128)(2,1)S(1)} %bitcast.43), channel_id=1, source_target_pairs={{0,128},{128,256},{256,384},{384,0},{1,129},{129,257},{257,385},{3... | collective-permute-start | bytes 2359304 | tf_op jit(solution)/shard_map/ppermute | solution.py:128
  9.6 17.3 %all-to-all-start = ((s32[16,1,128]{2,1,0:T(1,128)}), s32[16,1,128]{2,1,0:T(1,128)S(1)}, u32[]{:S(2)}, u32[]{:S(2)}) async-start(s32[16,1,128]{2,1,0:T(1,128)} %broadcast_in_dim.8), calls=%async_computation | async-start | bytes 16384 | tf_op jit(solution)/shard_map/all_to_all | solution.py:120
  26.9 35.5 %all-to-all-start.1 = ((bf16[4,256,1024]{2,1,0:T(8,128)(2,1)}), bf16[4,256,1024]{2,1,0:T(8,128)(2,1)S(1)}, u32[]{:S(2)}, u32[]{:S(2)}) async-start(bf16[4,256,1024]{2,1,0:T(8,128)(2,1)} %bitcast.40), calls=%async_computation.1 | async-start | bytes 4194304 | tf_op jit(solution)/shard_map/all_to_all | solution.py:120
  31.6 28.9 %collective-permute-start.3 = (bf16[1536,128]{1,0:T(8,128)(2,1)S(1)}, bf16[1536,128]{1,0:T(8,128)(2,1)S(1)}, u32[]{:S(2)}, u32[]{:S(2)}) collective-permute-start(bf16[1536,128]{1,0:T(8,128)(2,1)S(1)} %slice.9), channel_id=1, source_target_pairs={{0,384},{128,0},{256,128},{384,256},{1,385},{129,1},{257,129},{385... | collective-permute-start | bytes 1179656 | tf_op jit(solution)/shard_map/ppermute | solution.py:128
  37.2 25.2 %collective-permute-start.1 = (bf16[1536,128]{1,0:T(8,128)(2,1)S(1)}, bf16[1536,128]{1,0:T(8,128)(2,1)S(1)}, u32[]{:S(2)}, u32[]{:S(2)}) collective-permute-start(bf16[1536,128]{1,0:T(8,128)(2,1)S(1)} %slice.8), channel_id=1, source_target_pairs={{0,128},{128,256},{256,384},{384,0},{1,129},{129,257},{257,385},{3... | collective-permute-start | bytes 1179656 | tf_op jit(solution)/shard_map/ppermute | solution.py:128
  55.4 2.7 %copy-start = (bf16[2,1536,1024]{2,1,0:T(8,128)(2,1)}, bf16[2,1536,1024]{2,1,0:T(8,128)(2,1)S(1)}, u32[]{:S(2)}) copy-start(bf16[2,1536,1024]{2,1,0:T(8,128)(2,1)S(1)} %shard_map.37.f_ref) | copy-start | bytes 18874372
  60.4 1.9 %copy-start.3 = (bf16[1536,128]{1,0:T(8,128)(2,1)}, bf16[1536,128]{1,0:T(8,128)(2,1)S(1)}, u32[]{:S(2)}) copy-start(bf16[1536,128]{1,0:T(8,128)(2,1)S(1)} %collective-permute-done.3.h2b) | copy-start | bytes 1179652
  62.3 0.8 copy-start.4
  63.1 1.3 copy-start.1
  71.3 12.9 %collective-permute-start.4 = (bf16[1536,512]{1,0:T(8,128)(2,1)}, bf16[1536,512]{1,0:T(8,128)(2,1)S(1)}, u32[]{:S(2)}, u32[]{:S(2)}) collective-permute-start(bf16[1536,512]{1,0:T(8,128)(2,1)} %shard_map.39), channel_id=1, source_target_pairs={{0,1},{1,0},{2,3},{3,2},{4,5},{5,4},{6,7},{7,6},{8,9},{9,8},{10,11... | collective-permute-start | bytes 4718600 | tf_op jit(solution)/shard_map/ppermute | solution.py:157
  177.0 9.8 %collective-permute-start.5 = (bf16[96,4,512]{2,0,1:T(8,128)(2,1)S(1)}, bf16[96,4,512]{2,0,1:T(8,128)(2,1)S(1)}, u32[]{:S(2)}, u32[]{:S(2)}) collective-permute-start(bf16[96,4,512]{2,0,1:T(8,128)(2,1)S(1)} %bitcast.51), channel_id=1, source_target_pairs={{0,1},{1,0},{2,3},{3,2},{4,5},{5,4},{6,7},{7,6},{8,9},{9,8},{10,11... | collective-permute-start | bytes 1179656 | tf_op jit(solution)/shard_map/ppermute | solution.py:169

commit v5 on v4

v5 whole, which is shorter than its diff:
```python
import jax
import jax.numpy as jnp
from jax import lax
from jax.experimental import pallas as pl
from jax.experimental.pallas import tpu as pltpu
from jax.sharding import Mesh, PartitionSpec as P

SWAP = [(0, 1), (1, 0)]
MIX = 73244475
SIDE = 4
OWNERS = SIDE * SIDE


def factor(base, offset):
    k = base + offset
    k = k ^ lax.shift_right_logical(k, 16)
    k = k * MIX
    k = k ^ lax.shift_right_logical(k, 16)
    k = k * MIX
    k = (k ^ lax.shift_right_logical(k, 16)) & 65535
    return k.astype(jnp.float32) + 491520.0


def factor_kernel(place, words_ref, out_ref, base_ref, *, tile, part):
    owner = pl.program_id(0)
    x, y, group0 = place[0], place[1], place[2 + part]
    owner_y, owner_x = owner >> 2, owner & 3
    rows, width = out_ref.shape[1:]
    lane = lax.broadcasted_iota(jnp.int32, (8, 128), 1)
    sub = lax.broadcasted_iota(jnp.int32, (8, 128), 0)
    shared = 65599 * (lane >> 5) + 131071 * sub + (131071 * rows * owner + 65599 * group0)
    keepers = (
        (((owner_y & 2) | (y & 1)) * 4 + x, 0),
        (((owner_y & 2) | (1 - (y & 1))) * 4 + x, 0),
        (owner_y * 4 + x, 1),
        (owner_y * 4 + ((owner_x & 2) | (x & 1)), 2),
        (owner, 3),
    )
    for at, (keeper, step) in enumerate(keepers):
        base_ref[at] = words_ref[pl.ds(keeper, 1), :] + shared + 7919 * step

    def columns(at, carry):
        first = pl.multiple_of(at * tile, tile)
        for row in range(0, rows, 16):
            for col in range(0, tile, 128):
                halves = ([], [])
                for top in (row, row + 8):
                    offset = (at * (tile // 128) + col // 128) * (4 * 65599) + 131071 * top
                    f = [factor(base_ref[n], offset) for n in range(5)]
                    later = (f[2] * (2.0**-38)) * ((f[3] * (2.0**-38)) * f[4])
                    for pair in range(2):
                        halves[pair].append(f[pair] * later - 1.0)
                for pair in range(2):
                    block = jnp.concatenate(halves[pair], axis=0).astype(jnp.bfloat16)
                    out_ref[pair, row : row + 16, pl.ds(pl.multiple_of(first + col, 128), 128)] = block
        return carry

    lax.fori_loop(0, width // tile, columns, 0)


def factors(place, words, rows_all, width, part):
    rows = rows_all // OWNERS

    def body(*refs):
        factor_kernel(*refs, tile=min(512, width), part=part)

    return pl.pallas_call(
        body,
        grid_spec=pltpu.PrefetchScalarGridSpec(
            num_scalar_prefetch=1,
            grid=(OWNERS,),
            in_specs=[pl.BlockSpec(words.shape, lambda i, p: (0, 0))],
            out_specs=pl.BlockSpec((2, rows, width), lambda i, p: (0, i, 0)),
            scratch_shapes=[pltpu.VMEM((5, 8, 128), jnp.int32)],
        ),
        out_shape=jax.ShapeDtypeStruct((2, rows_all, width), jnp.bfloat16),
        compiler_params=pltpu.CompilerParams(vmem_limit_bytes=8 * 2**20),
        cost_estimate=pl.CostEstimate(
            flops=10000 * rows_all * width, bytes_accessed=2 * rows_all * width * 2, transcendentals=0
        ),
    )(place, words)


def pairs_kernel(place, h0, h2a, h2b, h1, h3, g0, g2, g1, g3, f_ref, out_ref):
    def product(left, right):
        left = jnp.concatenate([part[...] for part in left], axis=1)
        right = jnp.concatenate([part[...] for part in right], axis=0)
        return jnp.dot(left, right, preferred_element_type=jnp.float32)

    near = product((h0, h2a, h2b), (g0, g2))
    far = product((h1, h3), (g1, g3))
    total = near + near * f_ref[0].astype(jnp.float32) + (far + far * f_ref[1].astype(jnp.float32))
    out_ref[...] = total.astype(jnp.bfloat16)


def pairs(place, h, g, scale, part):
    rows_all, tokens = h[0].shape
    width = scale.shape[2]
    rows = rows_all // SIDE
    specs = [pl.BlockSpec((rows, block.shape[1]), lambda i, p: (i, 0)) for block in h]
    specs.append(pl.BlockSpec((tokens, width), lambda i, p: (0, p[4 + part])))
    specs += [pl.BlockSpec((tokens, width), lambda i, p: (0, p[6 + part]))] * 3
    specs.append(pl.BlockSpec((2, rows, width), lambda i, p: (0, i, 0)))
    return pl.pallas_call(
        pairs_kernel,
        grid_spec=pltpu.PrefetchScalarGridSpec(
            num_scalar_prefetch=1,
            grid=(SIDE,),
            in_specs=specs,
            out_specs=pl.BlockSpec((rows, width), lambda i, p: (i, 0)),
        ),
        out_shape=jax.ShapeDtypeStruct((rows_all, width), jnp.bfloat16),
        compiler_params=pltpu.CompilerParams(vmem_limit_bytes=16 * 2**20),
        cost_estimate=pl.CostEstimate(
            flops=8 * rows_all * tokens * width, bytes_accessed=3 * rows_all * width * 2, transcendentals=0
        ),
    )(place, *h, *g, scale)


def weave_kernel(place, here_ref, there_ref, out_ref):
    width = here_ref.shape[2]
    first = place[7] == 0
    here, there = here_ref[0], there_ref[0]
    out_ref[:, :width] = jnp.where(first, here, there)
    out_ref[:, width:] = jnp.where(first, there, here)


def weave(place, here, there):
    sides, rows, width = here.shape
    cell = pl.BlockSpec((1, rows, width), lambda i, p: (i, 0, 0))
    return pl.pallas_call(
        weave_kernel,
        grid_spec=pltpu.PrefetchScalarGridSpec(
            num_scalar_prefetch=1,
            grid=(sides,),
            in_specs=[cell, cell],
            out_specs=pl.BlockSpec((rows, 2 * width), lambda i, p: (0, i)),
        ),
        out_shape=jax.ShapeDtypeStruct((rows, sides * 2 * width), here.dtype),
        compiler_params=pltpu.CompilerParams(vmem_limit_bytes=8 * 2**20),
    )(place, here, there)


def exchange(blocks, axes):
    return lax.all_to_all(blocks, axes, 0, 0, tiled=True)


def added(blocks, axis=0):
    return jnp.sum(blocks.astype(jnp.float32), axis=axis).astype(jnp.bfloat16)


def along_y(block, step):
    return lax.ppermute(block, "y", [(at, (at + step) % SIDE) for at in range(SIDE)])


def per_device(hidden, grad_out, seed_table):
    depth = lax.axis_size("zh")
    x, y, core = lax.axis_index("x"), lax.axis_index("y"), lax.axis_index("core")
    tokens, columns = grad_out.shape[1:]
    quarter = columns // SIDE
    half = quarter // 2
    words = exchange(jnp.broadcast_to(jnp.tile(seed_table[0, 0], (1, 4)), (OWNERS, 128)), ("y", "x"))
    other = 1 - core
    groups = half // 32
    place = [x, y, (y * 2 + other) * groups, (y * 2 + core) * groups, y * 2 + other, y * 2 + core, other, core]
    place = jnp.stack(place).astype(jnp.int32)

    h_own = hidden[0].T
    h_low = along_y(h_own, 1)
    h_high = along_y(h_own, -1)
    h_facing_a = along_y(h_low[:, : tokens // 2], 1)
    h_facing_b = along_y(h_high[:, tokens // 2 :], -1)
    h = [h_own, h_facing_a, h_facing_b, h_high, h_low]

    def quarter_for(step):
        return lax.dynamic_slice_in_dim(grad_out[0], (y + step) % SIDE * quarter, quarter, 1)

    g_low, g_high, g_facing = (along_y(quarter_for(step), step) for step in (1, -1, 2))
    g = [grad_out[0], g_facing, g_high, g_low]

    rows_all = h_own.shape[0]
    scale = [factors(place, words, rows_all, half, part) for part in range(2)]
    sent = pairs(place, h, g, scale[0], 0)
    received = lax.ppermute(sent, "core", SWAP)
    both = pairs(place, h, g, scale[1], 1).astype(jnp.float32) + received.astype(jnp.float32)

    rows = rows_all // OWNERS
    got = exchange(both.astype(jnp.bfloat16).reshape(OWNERS, rows, half), ("y", "x"))
    owned = added(got.reshape(SIDE, SIDE, rows, half), 1)
    near = added(exchange(owned, "zl"))
    total = added(exchange(jnp.broadcast_to(near, (depth, *near.shape)), "zh"))
    here = lax.all_gather(total, "zl")
    there = lax.ppermute(here, "core", SWAP)
    return weave(place, here, there)[None]


def solution(mesh):
    devices = mesh.devices
    zero, dp = devices.shape
    split = Mesh(devices.reshape(SIDE, zero // SIDE, dp // 2 // SIDE, SIDE, 2), ("y", "x", "zh", "zl", "core"))
    return jax.shard_map(
        per_device,
        mesh=split,
        in_specs=(
            P(("zh", "zl", "core"), ("y", "x"), None),
            P(("zh", "zl", "core"), ("y", "x"), None),
            P(("zh", "zl", "core"), ("y", "x"), None, None),
        ),
        out_specs=P(None, ("y", "x"), None),
        check_vma=False,
    )
```

time: 190 us -> 183 us (0.963)
  local copies, waits for them, and re-layouts: 18.5 us -> 6.34 us
  starting transfers between devices: 37.8 us -> 43.8 us
  waiting for transfers between devices: 9.95 us -> 15.3 us
  blocking collectives: 90.3 us -> 87.8 us
  Pallas kernels: 30 us -> 27.6 us
    all_to_all x3, blocking collectives: 90.3 us -> 75.4 us  [exchange(): return lax.all_to_all(blocks, axes, 0, 0, tiled=True)]
    all_gather x0 -> x1, blocking collectives: none -> 12.3 us  [per_device(): here = lax.all_gather(total, 'zl')]
    ppermute x4 -> x7, waiting for transfers between devices: 4.32 us -> 14 us  [along_y(): lax.ppermute(block, 'y', [(at, (at + step) % SIDE) for at in range(SIDE)])]
    ppermute x4 -> x7, starting transfers between devices: 13.9 us -> 23.2 us  [along_y(): lax.ppermute(block, 'y', [(at, (at + step) % SIDE) for at in range(SIDE)])]
    unnamed x14 -> x5, local copies, waits for them, and re-layouts: 9.45 us -> 1.43 us
    pallas_call x2, Pallas kernels: 13.8 us -> 9.15 us  [pairs(): pl.pallas_call(pairs_kernel, grid_spec=pltpu.PrefetchScalarGridSpec(num_s...]
    another operation x4 -> x1, local copies, waits for them, and re-layouts: 4.58 us -> 0.09 us  [per_device(): place = jnp.stack(place).astype(jnp.int32)]
    all_to_all x2 -> x1, waiting for transfers between devices: 4.3 us -> 0.01 us  [exchange(): return lax.all_to_all(blocks, axes, 0, 0, tiled=True)]
  transfers between devices with their start and end apart: 8 -> 10, of which waited for: 4 -> 4; matrix products, arithmetic and copies ran while one was open for 5% -> 3% of each run, Pallas kernels for 12% -> 12%
where the time goes in v5:
time: 183 us; the launch traced here: 182 us
  blocking collectives  87.8 us (48%)
  starting transfers between devices  43.8 us (24%)
  Pallas kernels  27.6 us (15%)
  waiting for transfers between devices  15.3 us (8%)
  local copies, waits for them, and re-layouts  6.34 us (3%)
    all_to_all x3, blocking collectives, exchange(): return lax.all_to_all(blocks, axes, 0, 0, tiled=True)  75.4 us
    ppermute x7, starting transfers between devices, along_y(): lax.ppermute(block, 'y', [(at, (at + step) % SIDE) for at in range(SIDE)])  23.2 us
    pallas_call x2, Pallas kernels, factors(): pl.pallas_call(body, grid_spec=pltpu.PrefetchScalarGridSpec(num_scalar_pr...  16.4 us
    ppermute x7, waiting for transfers between devices, along_y(): lax.ppermute(block, 'y', [(at, (at + step) % SIDE) for at in range(SIDE)])  14 us
    all_gather x1, blocking collectives, per_device(): here = lax.all_gather(total, 'zl')  12.3 us
    ppermute x1, starting transfers between devices, per_device(): there = lax.ppermute(here, 'core', SWAP)  9.52 us
    pallas_call x2, Pallas kernels, pairs(): pl.pallas_call(pairs_kernel, grid_spec=pltpu.PrefetchScalarGridSpec(num_s...  9.15 us
    all_to_all x1, starting transfers between devices, exchange(): return lax.all_to_all(blocks, axes, 0, 0, tiled=True)  6.5 us
  transfers between devices with their start and end apart: 10, of which 4 were waited for; matrix products, arithmetic and copies ran while one was open for 3% of the time, Pallas kernels for 12%

profile of v5, /device:TPU:1, one launch (start us, length us, event | category | flops | bytes accessed | tf_op | source)
XLA Modules:
  0.0 181.9 jit_solution(3260468542342507452)
XLA Ops:
  0.0 0.0 copy-start.1
  0.0 1.4 copy.6
  1.4 5.5 %collective-permute-start.2 = (bf16[1536,256]{1,0:T(8,128)(2,1)S(1)}, bf16[1536,256]{1,0:T(8,128)(2,1)S(1)}, u32[]{:S(2)}, u32[]{:S(2)}) collective-permute-start(bf16[1536,256]{1,0:T(8,128)(2,1)S(1)} %bitcast.27), channel_id=1, source_target_pairs={{0,384},{128,0},{256,128},{384,256},{1,385},{129,1},{257,129},{385... | collective-permute-start | bytes 2359304 | tf_op jit(solution)/shard_map/ppermute | solution.py:153
  6.9 1.9 %collective-permute-start = (bf16[1536,256]{1,0:T(8,128)(2,1)S(1)}, bf16[1536,256]{1,0:T(8,128)(2,1)S(1)}, u32[]{:S(2)}, u32[]{:S(2)}) collective-permute-start(bf16[1536,256]{1,0:T(8,128)(2,1)S(1)} %bitcast.28), channel_id=1, source_target_pairs={{0,128},{128,256},{256,384},{384,0},{1,129},{129,257},{257,385},{3... | collective-permute-start | bytes 2359304 | tf_op jit(solution)/shard_map/ppermute | solution.py:153
  8.8 0.0 copy-done.1
  8.9 0.1 tile.12
  8.9 0.6 broadcast_in_dim.11
  9.5 6.5 %all-to-all-start = ((s32[16,1,128]{2,1,0:T(1,128)}), s32[16,1,128]{2,1,0:T(1,128)S(1)}, u32[]{:S(2)}, u32[]{:S(2)}) async-start(s32[16,1,128]{2,1,0:T(1,128)} %broadcast_in_dim.11), calls=%async_computation | async-start | bytes 16384 | tf_op jit(solution)/shard_map/all_to_all | solution.py:145
  16.1 2.6 %dynamic-slice_bitcast_fusion = (bf16[256,1024]{1,0:T(8,128)(2,1)}, bf16[256,1024]{1,0:T(8,128)(2,1)}, bf16[256,1024]{1,0:T(8,128)(2,1)}) fusion(bf16[1,256,4096]{2,1,0:T(8,128)(2,1)} %param.4, s32[]{:T(128)S(6)} %select_n.29, s32[]{:T(128)S(6)} %select_n.25, s32[]{:T(128)S(6)} %select_n.27), kind=kLoop, calls=%fused_computation.2 | loop fusion | bytes 3145740 | tf_op jit(solution)/shard_map/dynamic_slice | solution.py:176
  18.7 3.2 %collective-permute-start.6 = (bf16[256,1024]{1,0:T(8,128)(2,1)}, bf16[256,1024]{1,0:T(8,128)(2,1)S(1)}, u32[]{:S(2)}, u32[]{:S(2)}) collective-permute-start(bf16[256,1024]{1,0:T(8,128)(2,1)} %get-tuple-element.5), channel_id=1, source_target_pairs={{0,128},{128,256},{256,384},{384,0},{1,129},{129,257},{257,385},{3... | collective-permute-start | bytes 1572872 | tf_op jit(solution)/shard_map/ppermute | solution.py:153
  21.9 4.3 %collective-permute-start.4 = (bf16[256,1024]{1,0:T(8,128)(2,1)}, bf16[256,1024]{1,0:T(8,128)(2,1)S(1)}, u32[]{:S(2)}, u32[]{:S(2)}) collective-permute-start(bf16[256,1024]{1,0:T(8,128)(2,1)} %get-tuple-element.6), channel_id=1, source_target_pairs={{0,256},{128,384},{256,0},{384,128},{1,257},{129,385},{257,1},{385... | collective-permute-start | bytes 1572872 | tf_op jit(solution)/shard_map/ppermute | solution.py:153
  26.2 3.1 %collective-permute-start.5 = (bf16[256,1024]{1,0:T(8,128)(2,1)}, bf16[256,1024]{1,0:T(8,128)(2,1)}, u32[]{:S(2)}, u32[]{:S(2)}) collective-permute-start(bf16[256,1024]{1,0:T(8,128)(2,1)} %get-tuple-element.7), channel_id=1, source_target_pairs={{0,384},{128,0},{256,128},{384,256},{1,385},{129,1},{257,129},{385... | collective-permute-start | bytes 1572872 | tf_op jit(solution)/shard_map/ppermute | solution.py:153
  29.3 0.1 stack.35.refs_0_.place
  29.4 0.0 collective-permute-done.2.h1
  29.4 0.8 slice.9
  30.2 1.9 %collective-permute-start.3 = (bf16[1536,128]{1,0:T(8,128)(2,1)}, bf16[1536,128]{1,0:T(8,128)(2,1)}, u32[]{:S(2)}, u32[]{:S(2)}) collective-permute-start(bf16[1536,128]{1,0:T(8,128)(2,1)} %slice.9), channel_id=1, source_target_pairs={{0,384},{128,0},{256,128},{384,256},{1,385},{129,1},{257,129},{385... | collective-permute-start | bytes 1179656 | tf_op jit(solution)/shard_map/ppermute | solution.py:153
  32.1 0.0 collective-permute-done.h3
  32.1 0.8 slice.8
  32.9 3.4 %collective-permute-start.1 = (bf16[1536,128]{1,0:T(8,128)(2,1)}, bf16[1536,128]{1,0:T(8,128)(2,1)}, u32[]{:S(2)}, u32[]{:S(2)}) collective-permute-start(bf16[1536,128]{1,0:T(8,128)(2,1)} %slice.8), channel_id=1, source_target_pairs={{0,128},{128,256},{256,384},{384,0},{1,129},{129,257},{257,385},{3... | collective-permute-start | bytes 1179656 | tf_op jit(solution)/shard_map/ppermute | solution.py:153
  36.2 0.0 all-to-all-done
  36.2 0.0 copy-start
  36.3 8.2 %shard_map.39.f_ref = bf16[2,1536,512]{2,1,0:T(8,128)(2,1)S(1)} custom-call(s32[8]{0:T(128)S(1)} %stack.35.refs_0_.place, s32[16,128]{1,0:T(8,128)S(1)} %bitcast.33), custom_call_target="tpu_custom_call" | custom-call | flops 7864320000 | bytes 3145728 | tf_op jit(solution)/shard_map/pallas_call | solution.py:67
  44.5 0.0 collective-permute-done.6.g3
  44.5 5.2 %collective-permute-done.4.g2 = bf16[256,1024]{1,0:T(8,128)(2,1)S(1)} collective-permute-done((bf16[256,1024]{1,0:T(8,128)(2,1)}, bf16[256,1024]{1,0:T(8,128)(2,1)S(1)}, u32[]{:S(2)}, u32[]{:S(2)}) %collective-permute-start.4) | collective-permute-done | bytes 524320 | tf_op jit(solution)/shard_map/ppermute | solution.py:153
  49.7 0.0 collective-permute-done.5.g1
  49.7 7.4 %collective-permute-done.3.h2b = bf16[1536,128]{1,0:T(8,128)(2,1)} collective-permute-done((bf16[1536,128]{1,0:T(8,128)(2,1)}, bf16[1536,128]{1,0:T(8,128)(2,1)}, u32[]{:S(2)}, u32[]{:S(2)}) %collective-permute-start.3) | collective-permute-done | bytes 393248 | tf_op jit(solution)/shard_map/ppermute | solution.py:153
  57.0 1.4 collective-permute-done.1.h2a
  58.5 0.0 copy-done
  58.5 4.6 %shard_map.40 = bf16[1536,512]{1,0:T(8,128)(2,1)S(1)} custom-call(s32[8]{0:T(128)S(1)} %stack.35.refs_0_.place, bf16[1536,256]{1,0:T(8,128)(2,1)S(1)} %bitcast.29, bf16[1536,128]{1,0:T(8,128)(2,1)} %collective-permute-done.1.h2a, bf16[1536,128]{1,0:T(8,128)(2,1)} %collective-permute-done.3.h2b, bf16[1536,256]{1,0:T(8,128)(2,1)S(1)} %collective-permute-done.2.h1, ...), custom_call_target="tpu_custom_call" | custom-call | flops 1610612736 | bytes 4718592 | tf_op jit(solution)/shard_map/pallas_call | solution.py:104
  63.1 4.5 %collective-permute-start.7 = (bf16[1536,512]{1,0:T(8,128)(2,1)S(1)}, bf16[1536,512]{1,0:T(8,128)(2,1)S(1)}, u32[]{:S(2)}, u32[]{:S(2)}) collective-permute-start(bf16[1536,512]{1,0:T(8,128)(2,1)S(1)} %shard_map.40), channel_id=1, source_target_pairs={{0,1},{1,0},{2,3},{3,2},{4,5},{5,4},{6,7},{7,6},{8,9},{9,8},{10,11... | collective-permute-start | bytes 4718600 | tf_op jit(solution)/shard_map/ppermute | solution.py:184
  67.6 8.2 %shard_map.37.f_ref = bf16[2,1536,512]{2,1,0:T(8,128)(2,1)S(1)} custom-call(s32[8]{0:T(128)S(1)} %stack.35.refs_0_.place, s32[16,128]{1,0:T(8,128)S(1)} %bitcast.34), custom_call_target="tpu_custom_call" | custom-call | flops 7864320000 | bytes 3145728 | tf_op jit(solution)/shard_map/pallas_call | solution.py:67
  75.8 4.6 %shard_map.38 = bf16[1536,512]{1,0:T(8,128)(2,1)S(1)} custom-call(s32[8]{0:T(128)S(1)} %stack.35.refs_0_.place, bf16[1536,256]{1,0:T(8,128)(2,1)S(1)} %bitcast.30, bf16[1536,128]{1,0:T(8,128)(2,1)} %collective-permute-done.1.h2a, bf16[1536,128]{1,0:T(8,128)(2,1)} %collective-permute-done.3.h2b, bf16[1536,256]{1,0:T(8,128)(2,1)S(1)} %collective-permute-done.2.h1, ...), custom_call_target="tpu_custom_call" | custom-call | flops 1610612736 | bytes 4718592 | tf_op jit(solution)/shard_map/pallas_call | solution.py:104
  80.3 0.0 collective-permute-done.7
  80.3 0.5 add_convert_fusion
  80.9 26.3 %all_to_all.23 = bf16[16,96,512]{2,1,0:T(8,128)(2,1)S(1)} all-to-all(bf16[16,96,512]{2,1,0:T(8,128)(2,1)S(1)} %bitcast.35), channel_id=1, replica_groups=mesh['y'=4,'x'=4,'zh'=4,'zl'=4,'core'=2] {'y','x'}, dimensions={0} | all-to-all | bytes 3145728 | tf_op jit(solution)/shard_map/all_to_all | solution.py:145
  107.2 0.2 bitcast_reduce_fusion
  107.4 15.8 %all_to_all.24 = bf16[4,96,512]{2,1,0:T(8,128)(2,1)S(1)} all-to-all(bf16[4,96,512]{2,1,0:T(8,128)(2,1)S(1)} %bitcast_reduce_fusion), channel_id=1, replica_groups=mesh['y'=4,'x'=4,'zh'=4,'zl'=4,'core'=2] {'zl'}, dimensions={0} | all-to-all | bytes 786432 | tf_op jit(solution)/shard_map/all_to_all | solution.py:145
  123.3 0.1 reduce_sum.37
  123.4 33.3 %all_to_all.25 = bf16[4,96,512]{2,1,0:T(8,128)(2,1)S(1)} all-to-all(bf16[4,96,512]{2,1,0:T(8,128)(2,1)S(1)} %broadcast_in_dim.12), channel_id=1, replica_groups=mesh['y'=4,'x'=4,'zh'=4,'zl'=4,'core'=2] {'zh'}, dimensions={0} | all-to-all | bytes 786432 | tf_op jit(solution)/shard_map/all_to_all | solution.py:145
  156.6 0.1 reduce_sum.38
  156.7 12.3 %all-gather = bf16[384,512]{1,0:T(8,128)(2,1)S(1)} all-gather(bf16[96,512]{1,0:T(8,128)(2,1)S(1)} %reduce_sum.38), channel_id=2, replica_groups=mesh['y'=4,'x'=4,'zh'=4,'zl'=4,'core'=2] {'zl'}, dimensions={0}, use_global_device_ids=true | all-gather | bytes 491520 | tf_op jit(solution)/shard_map/all_gather | solution.py:192
  169.0 9.5 %collective-permute-start.8 = (bf16[4,96,512]{2,1,0:T(8,128)(2,1)S(1)}, bf16[4,96,512]{2,1,0:T(8,128)(2,1)S(1)}, u32[]{:S(2)}, u32[]{:S(2)}) collective-permute-start(bf16[4,96,512]{2,1,0:T(8,128)(2,1)S(1)} %bitcast.31), channel_id=1, source_target_pairs={{0,1},{1,0},{2,3},{3,2},{4,5},{5,4},{6,7},{7,6},{8,9},{9,8},{10,11... | collective-permute-start | bytes 1179656 | tf_op jit(solution)/shard_map/ppermute | solution.py:193
  178.6 1.3 collective-permute-done.8.there_ref
  179.9 2.0 %shard_map.41 = bf16[96,4096]{1,0:T(8,128)(2,1)} custom-call(s32[8]{0:T(128)S(1)} %stack.35.refs_0_.place, bf16[4,96,512]{2,1,0:T(8,128)(2,1)S(1)} %bitcast.32, bf16[4,96,512]{2,1,0:T(8,128)(2,1)S(1)} %collective-permute-done.8.there_ref), custom_call_target="tpu_custom_call" | custom-call | tf_op jit(solution)/shard_map/pallas_call | solution.py:131
  (2 shorter events, 0.0 us)
Async XLA Ops:
  0.0 8.8 %copy-start.1 = (s32[1,1,1,32]{3,2,1,0:T(1,128)S(1)}, s32[1,1,1,32]{3,2,1,0:T(1,128)}, u32[]{:S(2)}) copy-start(s32[1,1,1,32]{3,2,1,0:T(1,128)} %param.5) | copy-start | bytes 388
  1.4 28.0 %collective-permute-start.2 = (bf16[1536,256]{1,0:T(8,128)(2,1)S(1)}, bf16[1536,256]{1,0:T(8,128)(2,1)S(1)}, u32[]{:S(2)}, u32[]{:S(2)}) collective-permute-start(bf16[1536,256]{1,0:T(8,128)(2,1)S(1)} %bitcast.27), channel_id=1, source_target_pairs={{0,384},{128,0},{256,128},{384,256},{1,385},{129,1},{257,129},{385... | collective-permute-start | bytes 2359304 | tf_op jit(solution)/shard_map/ppermute | solution.py:153
  6.9 25.2 %collective-permute-start = (bf16[1536,256]{1,0:T(8,128)(2,1)S(1)}, bf16[1536,256]{1,0:T(8,128)(2,1)S(1)}, u32[]{:S(2)}, u32[]{:S(2)}) collective-permute-start(bf16[1536,256]{1,0:T(8,128)(2,1)S(1)} %bitcast.28), channel_id=1, source_target_pairs={{0,128},{128,256},{256,384},{384,0},{1,129},{129,257},{257,385},{3... | collective-permute-start | bytes 2359304 | tf_op jit(solution)/shard_map/ppermute | solution.py:153
  9.5 26.7 %all-to-all-start = ((s32[16,1,128]{2,1,0:T(1,128)}), s32[16,1,128]{2,1,0:T(1,128)S(1)}, u32[]{:S(2)}, u32[]{:S(2)}) async-start(s32[16,1,128]{2,1,0:T(1,128)} %broadcast_in_dim.11), calls=%async_computation | async-start | bytes 16384 | tf_op jit(solution)/shard_map/all_to_all | solution.py:145
  18.7 25.8 %collective-permute-start.6 = (bf16[256,1024]{1,0:T(8,128)(2,1)}, bf16[256,1024]{1,0:T(8,128)(2,1)S(1)}, u32[]{:S(2)}, u32[]{:S(2)}) collective-permute-start(bf16[256,1024]{1,0:T(8,128)(2,1)} %get-tuple-element.5), channel_id=1, source_target_pairs={{0,128},{128,256},{256,384},{384,0},{1,129},{129,257},{257,385},{3... | collective-permute-start | bytes 1572872 | tf_op jit(solution)/shard_map/ppermute | solution.py:153
  21.9 27.8 %collective-permute-start.4 = (bf16[256,1024]{1,0:T(8,128)(2,1)}, bf16[256,1024]{1,0:T(8,128)(2,1)S(1)}, u32[]{:S(2)}, u32[]{:S(2)}) collective-permute-start(bf16[256,1024]{1,0:T(8,128)(2,1)} %get-tuple-element.6), channel_id=1, source_target_pairs={{0,256},{128,384},{256,0},{384,128},{1,257},{129,385},{257,1},{385... | collective-permute-start | bytes 1572872 | tf_op jit(solution)/shard_map/ppermute | solution.py:153
  26.2 23.5 %collective-permute-start.5 = (bf16[256,1024]{1,0:T(8,128)(2,1)}, bf16[256,1024]{1,0:T(8,128)(2,1)}, u32[]{:S(2)}, u32[]{:S(2)}) collective-permute-start(bf16[256,1024]{1,0:T(8,128)(2,1)} %get-tuple-element.7), channel_id=1, source_target_pairs={{0,384},{128,0},{256,128},{384,256},{1,385},{129,1},{257,129},{385... | collective-permute-start | bytes 1572872 | tf_op jit(solution)/shard_map/ppermute | solution.py:153
  30.2 26.9 %collective-permute-start.3 = (bf16[1536,128]{1,0:T(8,128)(2,1)}, bf16[1536,128]{1,0:T(8,128)(2,1)}, u32[]{:S(2)}, u32[]{:S(2)}) collective-permute-start(bf16[1536,128]{1,0:T(8,128)(2,1)} %slice.9), channel_id=1, source_target_pairs={{0,384},{128,0},{256,128},{384,256},{1,385},{129,1},{257,129},{385... | collective-permute-start | bytes 1179656 | tf_op jit(solution)/shard_map/ppermute | solution.py:153
  32.9 25.6 %collective-permute-start.1 = (bf16[1536,128]{1,0:T(8,128)(2,1)}, bf16[1536,128]{1,0:T(8,128)(2,1)}, u32[]{:S(2)}, u32[]{:S(2)}) collective-permute-start(bf16[1536,128]{1,0:T(8,128)(2,1)} %slice.8), channel_id=1, source_target_pairs={{0,128},{128,256},{256,384},{384,0},{1,129},{129,257},{257,385},{3... | collective-permute-start | bytes 1179656 | tf_op jit(solution)/shard_map/ppermute | solution.py:153
  36.2 22.2 %copy-start = (bf16[1,256,4096]{2,1,0:T(8,128)(2,1)S(1)}, bf16[1,256,4096]{2,1,0:T(8,128)(2,1)}, u32[]{:S(2)}) copy-start(bf16[1,256,4096]{2,1,0:T(8,128)(2,1)} %param.4) | copy-start | bytes 6291460
  63.1 17.3 %collective-permute-start.7 = (bf16[1536,512]{1,0:T(8,128)(2,1)S(1)}, bf16[1536,512]{1,0:T(8,128)(2,1)S(1)}, u32[]{:S(2)}, u32[]{:S(2)}) collective-permute-start(bf16[1536,512]{1,0:T(8,128)(2,1)S(1)} %shard_map.40), channel_id=1, source_target_pairs={{0,1},{1,0},{2,3},{3,2},{4,5},{5,4},{6,7},{7,6},{8,9},{9,8},{10,11... | collective-permute-start | bytes 4718600 | tf_op jit(solution)/shard_map/ppermute | solution.py:184
  169.0 10.9 %collective-permute-start.8 = (bf16[4,96,512]{2,1,0:T(8,128)(2,1)S(1)}, bf16[4,96,512]{2,1,0:T(8,128)(2,1)S(1)}, u32[]{:S(2)}, u32[]{:S(2)}) collective-permute-start(bf16[4,96,512]{2,1,0:T(8,128)(2,1)S(1)} %bitcast.31), channel_id=1, source_target_pairs={{0,1},{1,0},{2,3},{3,2},{4,5},{5,4},{6,7},{7,6},{8,9},{9,8},{10,11... | collective-permute-start | bytes 1179656 | tf_op jit(solution)/shard_map/ppermute | solution.py:193

commit v6 on v5

--- a/solution.py
+++ b/solution.py
@@ -21,14 +21,15 @@
     return k.astype(jnp.float32) + 491520.0
 
 
-def factor_kernel(place, words_ref, out_ref, base_ref, *, tile, part):
+def factor_kernel(place, words_ref, *refs):
+    outs, base_ref = refs[:2], refs[2]
     owner = pl.program_id(0)
-    x, y, group0 = place[0], place[1], place[2 + part]
+    x, y = place[0], place[1]
     owner_y, owner_x = owner >> 2, owner & 3
-    rows, width = out_ref.shape[1:]
+    rows, width = outs[0].shape[1:]
     lane = lax.broadcasted_iota(jnp.int32, (8, 128), 1)
     sub = lax.broadcasted_iota(jnp.int32, (8, 128), 0)
-    shared = 65599 * (lane >> 5) + 131071 * sub + (131071 * rows * owner + 65599 * group0)
+    shared = 65599 * (lane >> 5) + 131071 * sub + 131071 * rows * owner
     keepers = (
         (((owner_y & 2) | (y & 1)) * 4 + x, 0),
         (((owner_y & 2) | (1 - (y & 1))) * 4 + x, 0),
@@ -39,78 +40,82 @@
     for at, (keeper, step) in enumerate(keepers):
         base_ref[at] = words_ref[pl.ds(keeper, 1), :] + shared + 7919 * step
 
-    def columns(at, carry):
-        first = pl.multiple_of(at * tile, tile)
+    def fill(out_ref, group0):
         for row in range(0, rows, 16):
-            for col in range(0, tile, 128):
+            for col in range(0, width, 128):
                 halves = ([], [])
                 for top in (row, row + 8):
-                    offset = (at * (tile // 128) + col // 128) * (4 * 65599) + 131071 * top
+                    offset = 65599 * (group0 + col // 32) + 131071 * top
                     f = [factor(base_ref[n], offset) for n in range(5)]
                     later = (f[2] * (2.0**-38)) * ((f[3] * (2.0**-38)) * f[4])
                     for pair in range(2):
                         halves[pair].append(f[pair] * later - 1.0)
                 for pair in range(2):
                     block = jnp.concatenate(halves[pair], axis=0).astype(jnp.bfloat16)
-                    out_ref[pair, row : row + 16, pl.ds(pl.multiple_of(first + col, 128), 128)] = block
-        return carry
-
-    lax.fori_loop(0, width // tile, columns, 0)
-
-
-def factors(place, words, rows_all, width, part):
+                    out_ref[pair, row : row + 16, col : col + 128] = block
+
+    for part in range(2):
+        fill(outs[part], place[2 + part])
+
+
+def factors(place, words, rows_all, width):
     rows = rows_all // OWNERS
-
-    def body(*refs):
-        factor_kernel(*refs, tile=min(512, width), part=part)
-
+    spec = pl.BlockSpec((2, rows, width), lambda i, p: (0, i, 0))
+    shape = jax.ShapeDtypeStruct((2, rows_all, width), jnp.bfloat16)
     return pl.pallas_call(
-        body,
+        factor_kernel,
         grid_spec=pltpu.PrefetchScalarGridSpec(
             num_scalar_prefetch=1,
             grid=(OWNERS,),
             in_specs=[pl.BlockSpec(words.shape, lambda i, p: (0, 0))],
-            out_specs=pl.BlockSpec((2, rows, width), lambda i, p: (0, i, 0)),
+            out_specs=[spec, spec],
             scratch_shapes=[pltpu.VMEM((5, 8, 128), jnp.int32)],
         ),
-        out_shape=jax.ShapeDtypeStruct((2, rows_all, width), jnp.bfloat16),
+        out_shape=[shape, shape],
         compiler_params=pltpu.CompilerParams(vmem_limit_bytes=8 * 2**20),
         cost_estimate=pl.CostEstimate(
-            flops=10000 * rows_all * width, bytes_accessed=2 * rows_all * width * 2, transcendentals=0
+            flops=20000 * rows_all * width, bytes_accessed=4 * rows_all * width * 2, transcendentals=0
         ),
     )(place, words)
 
 
-def pairs_kernel(place, h0, h2a, h2b, h1, h3, g0, g2, g1, g3, f_ref, out_ref):
-    def product(left, right):
-        left = jnp.concatenate([part[...] for part in left], axis=1)
-        right = jnp.concatenate([part[...] for part in right], axis=0)
-        return jnp.dot(left, right, preferred_element_type=jnp.float32)
-
-    near = product((h0, h2a, h2b), (g0, g2))
-    far = product((h1, h3), (g1, g3))
-    total = near + near * f_ref[0].astype(jnp.float32) + (far + far * f_ref[1].astype(jnp.float32))
-    out_ref[...] = total.astype(jnp.bfloat16)
+def pairs_kernel(place, h0, h2a, h2b, h1, h3, g0, g2, g1, g3, f_ref, out_ref, *, part):
+    rows_all, width = out_ref.shape
+    rows = rows_all // SIDE
+    first = pl.multiple_of(place[6 + part] * width, width)
+
+    def right(parts):
+        return jnp.concatenate([ref[:, pl.ds(first, width)] for ref in parts], axis=0)
+
+    sides = (((h0, h2a, h2b), (g0, g2)), ((h1, h3), (g1, g3)))
+
+    def block(at, carry):
+        here = pl.ds(pl.multiple_of(at * rows, rows), rows)
+        total = None
+        for pair, (left, own) in enumerate(sides):
+            left = jnp.concatenate([ref[here, :] for ref in left], axis=1)
+            value = jnp.dot(left, right(own), preferred_element_type=jnp.float32)
+            value = value + value * f_ref[pair, here, :].astype(jnp.float32)
+            total = value if total is None else total + value
+        out_ref[here, :] = total.astype(jnp.bfloat16)
+        return carry
+
+    lax.fori_loop(0, SIDE, block, 0)
 
 
 def pairs(place, h, g, scale, part):
     rows_all, tokens = h[0].shape
     width = scale.shape[2]
-    rows = rows_all // SIDE
-    specs = [pl.BlockSpec((rows, block.shape[1]), lambda i, p: (i, 0)) for block in h]
-    specs.append(pl.BlockSpec((tokens, width), lambda i, p: (0, p[4 + part])))
-    specs += [pl.BlockSpec((tokens, width), lambda i, p: (0, p[6 + part]))] * 3
-    specs.append(pl.BlockSpec((2, rows, width), lambda i, p: (0, i, 0)))
+
+    def body(*refs):
+        pairs_kernel(*refs, part=part)
+
     return pl.pallas_call(
-        pairs_kernel,
-        grid_spec=pltpu.PrefetchScalarGridSpec(
-            num_scalar_prefetch=1,
-            grid=(SIDE,),
-            in_specs=specs,
-            out_specs=pl.BlockSpec((rows, width), lambda i, p: (i, 0)),
-        ),
+        body,
+        in_specs=[pl.BlockSpec(memory_space=pltpu.SMEM)] + [pl.BlockSpec(memory_space=pltpu.VMEM)] * (len(h) + len(g) + 1),
+        out_specs=pl.BlockSpec(memory_space=pltpu.VMEM),
         out_shape=jax.ShapeDtypeStruct((rows_all, width), jnp.bfloat16),
-        compiler_params=pltpu.CompilerParams(vmem_limit_bytes=16 * 2**20),
+        compiler_params=pltpu.CompilerParams(vmem_limit_bytes=24 * 2**20),
         cost_estimate=pl.CostEstimate(
             flops=8 * rows_all * tokens * width, bytes_accessed=3 * rows_all * width * 2, transcendentals=0
         ),
@@ -154,7 +159,6 @@
 
 
 def per_device(hidden, grad_out, seed_table):
-    depth = lax.axis_size("zh")
     x, y, core = lax.axis_index("x"), lax.axis_index("y"), lax.axis_index("core")
     tokens, columns = grad_out.shape[1:]
     quarter = columns // SIDE
@@ -176,10 +180,10 @@
         return lax.dynamic_slice_in_dim(grad_out[0], (y + step) % SIDE * quarter, quarter, 1)
 
     g_low, g_high, g_facing = (along_y(quarter_for(step), step) for step in (1, -1, 2))
-    g = [grad_out[0], g_facing, g_high, g_low]
+    g = [quarter_for(0), g_facing, g_high, g_low]
 
     rows_all = h_own.shape[0]
-    scale = [factors(place, words, rows_all, half, part) for part in range(2)]
+    scale = factors(place, words, rows_all, half)
     sent = pairs(place, h, g, scale[0], 0)
     received = lax.ppermute(sent, "core", SWAP)
     both = pairs(place, h, g, scale[1], 1).astype(jnp.float32) + received.astype(jnp.float32)
@@ -188,7 +192,7 @@
     got = exchange(both.astype(jnp.bfloat16).reshape(OWNERS, rows, half), ("y", "x"))
     owned = added(got.reshape(SIDE, SIDE, rows, half), 1)
     near = added(exchange(owned, "zl"))
-    total = added(exchange(jnp.broadcast_to(near, (depth, *near.shape)), "zh"))
+    total = added(lax.all_gather(near, "zh"))
     here = lax.all_gather(total, "zl")
     there = lax.ppermute(here, "core", SWAP)
     return weave(place, here, there)[None]

time: 183 us -> 166 us (0.907)
  waiting for transfers between devices: 15.3 us -> 7.9 us
  blocking collectives: 87.8 us -> 81.5 us
  Pallas kernels: 27.6 us -> 25.4 us
    all_to_all x3 -> x2, blocking collectives: 75.4 us -> 42.3 us  [exchange(): return lax.all_to_all(blocks, axes, 0, 0, tiled=True)]
    all_gather x0 -> x1, blocking collectives: none -> 24 us  [per_device(): total = added(lax.all_gather(near, 'zh'))]
    ppermute x7, waiting for transfers between devices: 14 us -> 6.57 us  [along_y(): lax.ppermute(block, 'y', [(at, (at + step) % SIDE) for at in range(SIDE)])]
    all_gather x1, blocking collectives: 12.3 us -> 15.2 us  [per_device(): here = lax.all_gather(total, 'zl')]
    pallas_call x4 -> x3, Pallas kernels: 25.5 us -> 23.4 us  [the longest x1 15.6 us: factors(): pl.pallas_call(factor_kernel, grid_spec=pltpu.PrefetchScalarGridSpec(num_...]
  transfers between devices with their start and end apart: 10 -> 10, of which waited for: 4 -> 3; matrix products, arithmetic and copies ran while one was open for 3% -> 3% of each run, Pallas kernels for 12% -> 12%
where the time goes in v6:
time: 166 us
  blocking collectives  81.5 us (49%)
  starting transfers between devices  43.2 us (26%)
  Pallas kernels  25.4 us (15%)
  waiting for transfers between devices  7.9 us (5%)
  local copies, waits for them, and re-layouts  6.47 us (4%)
    all_to_all x2, blocking collectives, exchange(): return lax.all_to_all(blocks, axes, 0, 0, tiled=True)  42.3 us
    all_gather x1, blocking collectives, per_device(): total = added(lax.all_gather(near, 'zh'))  24 us
    ppermute x7, starting transfers between devices, along_y(): lax.ppermute(block, 'y', [(at, (at + step) % SIDE) for at in range(SIDE)])  23.2 us
    pallas_call x1, Pallas kernels, factors(): pl.pallas_call(factor_kernel, grid_spec=pltpu.PrefetchScalarGridSpec(num_...  15.6 us
    all_gather x1, blocking collectives, per_device(): here = lax.all_gather(total, 'zl')  15.2 us
    ppermute x1, starting transfers between devices, per_device(): there = lax.ppermute(here, 'core', SWAP)  9.03 us
    pallas_call x2, Pallas kernels, pairs(): pl.pallas_call(body, in_specs=[pl.BlockSpec(memory_space=pltpu.SMEM)] + [...  7.82 us
    ppermute x7, waiting for transfers between devices, along_y(): lax.ppermute(block, 'y', [(at, (at + step) % SIDE) for at in range(SIDE)])  6.57 us
  transfers between devices with their start and end apart: 10, of which 3 were waited for; matrix products, arithmetic and copies ran while one was open for 3% of the time, Pallas kernels for 12%

profile of v6, /device:TPU:1, one launch (start us, length us, event | category | flops | bytes accessed | tf_op | source)
XLA Modules:
  0.0 165.6 jit_solution(18408439131906418011)
XLA Ops:
  0.0 0.0 copy-start
  0.0 1.4 copy.6
  1.4 5.5 %collective-permute-start.2 = (bf16[1536,256]{1,0:T(8,128)(2,1)S(1)}, bf16[1536,256]{1,0:T(8,128)(2,1)S(1)}, u32[]{:S(2)}, u32[]{:S(2)}) collective-permute-start(bf16[1536,256]{1,0:T(8,128)(2,1)S(1)} %bitcast.27), channel_id=1, source_target_pairs={{0,384},{128,0},{256,128},{384,256},{1,385},{129,1},{257,129},{385... | collective-permute-start | bytes 2359304 | tf_op jit(solution)/shard_map/ppermute | solution.py:158
  6.9 1.9 %collective-permute-start = (bf16[1536,256]{1,0:T(8,128)(2,1)S(1)}, bf16[1536,256]{1,0:T(8,128)(2,1)S(1)}, u32[]{:S(2)}, u32[]{:S(2)}) collective-permute-start(bf16[1536,256]{1,0:T(8,128)(2,1)S(1)} %bitcast.28), channel_id=1, source_target_pairs={{0,128},{128,256},{256,384},{384,0},{1,129},{129,257},{257,385},{3... | collective-permute-start | bytes 2359304 | tf_op jit(solution)/shard_map/ppermute | solution.py:158
  8.8 0.0 copy-done
  8.9 0.1 tile.12
  8.9 0.6 broadcast_in_dim.8
  9.5 6.5 %all-to-all-start = ((s32[16,1,128]{2,1,0:T(1,128)}), s32[16,1,128]{2,1,0:T(1,128)S(1)}, u32[]{:S(2)}, u32[]{:S(2)}) async-start(s32[16,1,128]{2,1,0:T(1,128)} %broadcast_in_dim.8), calls=%async_computation | async-start | bytes 16384 | tf_op jit(solution)/shard_map/all_to_all | solution.py:150
  16.1 2.7 %dynamic-slice_bitcast_fusion = (bf16[256,1024]{1,0:T(8,128)(2,1)}, bf16[256,1024]{1,0:T(8,128)(2,1)}, bf16[256,1024]{1,0:T(8,128)(2,1)S(1)}, bf16[256,1024]{1,0:T(8,128)(2,1)}) fusion(bf16[1,256,4096]{2,1,0:T(8,128)(2,1)} %param.4, s32[]{:T(128)S(6)} %select_n.38, s32[]{:T(128)S(6)} %select_n.34, s32[]{:T(128)S(6)} %select_n.32, s32[]{:T(128)S(6)} %select_n.36), kind=kLoop, calls=%fused_computation.2 | loop fusion | bytes 4194320 | tf_op jit(solution)/shard_map/dynamic_slice | solution.py:180
  18.8 3.2 %collective-permute-start.6 = (bf16[256,1024]{1,0:T(8,128)(2,1)}, bf16[256,1024]{1,0:T(8,128)(2,1)S(1)}, u32[]{:S(2)}, u32[]{:S(2)}) collective-permute-start(bf16[256,1024]{1,0:T(8,128)(2,1)} %get-tuple-element.9), channel_id=1, source_target_pairs={{0,128},{128,256},{256,384},{384,0},{1,129},{129,257},{257,385},{3... | collective-permute-start | bytes 1572872 | tf_op jit(solution)/shard_map/ppermute | solution.py:158
  22.0 4.3 %collective-permute-start.4 = (bf16[256,1024]{1,0:T(8,128)(2,1)}, bf16[256,1024]{1,0:T(8,128)(2,1)}, u32[]{:S(2)}, u32[]{:S(2)}) collective-permute-start(bf16[256,1024]{1,0:T(8,128)(2,1)} %get-tuple-element.10), channel_id=1, source_target_pairs={{0,256},{128,384},{256,0},{384,128},{1,257},{129,385},{257,1},{385... | collective-permute-start | bytes 1572872 | tf_op jit(solution)/shard_map/ppermute | solution.py:158
  26.3 3.1 %collective-permute-start.5 = (bf16[256,1024]{1,0:T(8,128)(2,1)}, bf16[256,1024]{1,0:T(8,128)(2,1)}, u32[]{:S(2)}, u32[]{:S(2)}) collective-permute-start(bf16[256,1024]{1,0:T(8,128)(2,1)} %get-tuple-element.12), channel_id=1, source_target_pairs={{0,384},{128,0},{256,128},{384,256},{1,385},{129,1},{257,129},{385... | collective-permute-start | bytes 1572872 | tf_op jit(solution)/shard_map/ppermute | solution.py:158
  29.4 0.1 stack.35.place.refs_0_
  29.5 0.0 collective-permute-done.2.refs_4_
  29.5 0.8 slice.9
  30.3 1.9 %collective-permute-start.3 = (bf16[1536,128]{1,0:T(8,128)(2,1)}, bf16[1536,128]{1,0:T(8,128)(2,1)}, u32[]{:S(2)}, u32[]{:S(2)}) collective-permute-start(bf16[1536,128]{1,0:T(8,128)(2,1)} %slice.9), channel_id=1, source_target_pairs={{0,384},{128,0},{256,128},{384,256},{1,385},{129,1},{257,129},{385... | collective-permute-start | bytes 1179656 | tf_op jit(solution)/shard_map/ppermute | solution.py:158
  32.2 0.0 collective-permute-done.refs_5_
  32.2 0.8 slice.8
  33.0 3.4 %collective-permute-start.1 = (bf16[1536,128]{1,0:T(8,128)(2,1)}, bf16[1536,128]{1,0:T(8,128)(2,1)}, u32[]{:S(2)}, u32[]{:S(2)}) collective-permute-start(bf16[1536,128]{1,0:T(8,128)(2,1)} %slice.8), channel_id=1, source_target_pairs={{0,128},{128,256},{256,384},{384,0},{1,129},{129,257},{257,385},{3... | collective-permute-start | bytes 1179656 | tf_op jit(solution)/shard_map/ppermute | solution.py:158
  36.4 0.0 all-to-all-done
  36.4 15.6 %shard_map.37 = (bf16[2,1536,512]{2,1,0:T(8,128)(2,1)S(1)}, bf16[2,1536,512]{2,1,0:T(8,128)(2,1)S(1)}) custom-call(s32[8]{0:T(128)S(1)} %stack.35.place.refs_0_, s32[16,128]{1,0:T(8,128)S(1)} %bitcast.33), custom_call_target="tpu_custom_call" | custom-call | flops 15728640000 | bytes 6291456 | tf_op jit(solution)/shard_map/pallas_call | solution.py:65
  52.0 0.0 collective-permute-done.6.refs_9_
  52.0 0.0 collective-permute-done.4.refs_7_
  52.0 0.0 collective-permute-done.5.refs_8_
  52.0 5.2 %collective-permute-done.3.refs_3_ = bf16[1536,128]{1,0:T(8,128)(2,1)} collective-permute-done((bf16[1536,128]{1,0:T(8,128)(2,1)}, bf16[1536,128]{1,0:T(8,128)(2,1)}, u32[]{:S(2)}, u32[]{:S(2)}) %collective-permute-start.3) | collective-permute-done | bytes 393248 | tf_op jit(solution)/shard_map/ppermute | solution.py:158
  57.2 1.3 collective-permute-done.1.refs_2_
  58.6 3.9 %shard_map.39 = bf16[1536,512]{1,0:T(8,128)(2,1)S(1)} custom-call(s32[8]{0:T(128)S(1)} %stack.35.place.refs_0_, bf16[1536,256]{1,0:T(8,128)(2,1)S(1)} %bitcast.29, bf16[1536,128]{1,0:T(8,128)(2,1)} %collective-permute-done.1.refs_2_, bf16[1536,128]{1,0:T(8,128)(2,1)} %collective-permute-done.3.refs_3_, bf16[1536,256]{1,0:T(8,128)(2,1)S(1)} %collective-permute-done.2.refs_4_, ...), custom_call_target="tpu_custom_call" | custom-call | flops 1610612736 | bytes 4718592 | tf_op jit(solution)/shard_map/pallas_call | solution.py:113
  62.5 4.4 %collective-permute-start.7 = (bf16[1536,512]{1,0:T(8,128)(2,1)S(1)}, bf16[1536,512]{1,0:T(8,128)(2,1)S(1)}, u32[]{:S(2)}, u32[]{:S(2)}) collective-permute-start(bf16[1536,512]{1,0:T(8,128)(2,1)S(1)} %shard_map.39), channel_id=1, source_target_pairs={{0,1},{1,0},{2,3},{3,2},{4,5},{5,4},{6,7},{7,6},{8,9},{9,8},{10,11... | collective-permute-start | bytes 4718600 | tf_op jit(solution)/shard_map/ppermute | solution.py:188
  66.9 3.9 %shard_map.38 = bf16[1536,512]{1,0:T(8,128)(2,1)S(1)} custom-call(s32[8]{0:T(128)S(1)} %stack.35.place.refs_0_, bf16[1536,256]{1,0:T(8,128)(2,1)S(1)} %bitcast.30, bf16[1536,128]{1,0:T(8,128)(2,1)} %collective-permute-done.1.refs_2_, bf16[1536,128]{1,0:T(8,128)(2,1)} %collective-permute-done.3.refs_3_, bf16[1536,256]{1,0:T(8,128)(2,1)S(1)} %collective-permute-done.2.refs_4_, ...), custom_call_target="tpu_custom_call" | custom-call | flops 1610612736 | bytes 4718592 | tf_op jit(solution)/shard_map/pallas_call | solution.py:113
  70.8 0.0 collective-permute-done.7
  70.8 0.4 add_convert_fusion
  71.3 26.5 %all_to_all.18 = bf16[16,96,512]{2,1,0:T(8,128)(2,1)S(1)} all-to-all(bf16[16,96,512]{2,1,0:T(8,128)(2,1)S(1)} %bitcast.34), channel_id=1, replica_groups=mesh['y'=4,'x'=4,'zh'=4,'zl'=4,'core'=2] {'y','x'}, dimensions={0} | all-to-all | bytes 3145728 | tf_op jit(solution)/shard_map/all_to_all | solution.py:150
  97.8 0.2 bitcast_reduce_fusion
  98.0 15.8 %all_to_all.19 = bf16[4,96,512]{2,1,0:T(8,128)(2,1)S(1)} all-to-all(bf16[4,96,512]{2,1,0:T(8,128)(2,1)S(1)} %bitcast_reduce_fusion), channel_id=1, replica_groups=mesh['y'=4,'x'=4,'zh'=4,'zl'=4,'core'=2] {'zl'}, dimensions={0} | all-to-all | bytes 786432 | tf_op jit(solution)/shard_map/all_to_all | solution.py:150
  113.8 0.1 reduce_sum.37
  113.9 24.0 %all-gather = bf16[384,512]{1,0:T(8,128)(2,1)S(1)} all-gather(bf16[96,512]{1,0:T(8,128)(2,1)S(1)} %reduce_sum.37), channel_id=2, replica_groups=mesh['y'=4,'x'=4,'zh'=4,'zl'=4,'core'=2] {'zh'}, dimensions={0}, use_global_device_ids=true | all-gather | bytes 491520 | tf_op jit(solution)/shard_map/all_gather | solution.py:195
  137.9 0.1 reduce_sum.38
  138.0 15.2 %all-gather.1 = bf16[384,512]{1,0:T(8,128)(2,1)S(1)} all-gather(bf16[96,512]{1,0:T(8,128)(2,1)S(1)} %reduce_sum.38), channel_id=3, replica_groups=mesh['y'=4,'x'=4,'zh'=4,'zl'=4,'core'=2] {'zl'}, dimensions={0}, use_global_device_ids=true | all-gather | bytes 491520 | tf_op jit(solution)/shard_map/all_gather | solution.py:196
  153.2 9.0 %collective-permute-start.8 = (bf16[4,96,512]{2,1,0:T(8,128)(2,1)S(1)}, bf16[4,96,512]{2,1,0:T(8,128)(2,1)S(1)}, u32[]{:S(2)}, u32[]{:S(2)}) collective-permute-start(bf16[4,96,512]{2,1,0:T(8,128)(2,1)S(1)} %bitcast.31), channel_id=1, source_target_pairs={{0,1},{1,0},{2,3},{3,2},{4,5},{5,4},{6,7},{7,6},{8,9},{9,8},{10,11... | collective-permute-start | bytes 1179656 | tf_op jit(solution)/shard_map/ppermute | solution.py:197
  162.2 1.3 collective-permute-done.8.there_ref
  163.5 2.0 %shard_map.40 = bf16[96,4096]{1,0:T(8,128)(2,1)} custom-call(s32[8]{0:T(128)S(1)} %stack.35.place.refs_0_, bf16[4,96,512]{2,1,0:T(8,128)(2,1)S(1)} %bitcast.32, bf16[4,96,512]{2,1,0:T(8,128)(2,1)S(1)} %collective-permute-done.8.there_ref), custom_call_target="tpu_custom_call" | custom-call | tf_op jit(solution)/shard_map/pallas_call | solution.py:136
  (1 shorter events, 0.0 us)
Async XLA Ops:
  0.0 8.8 %copy-start = (s32[1,1,1,32]{3,2,1,0:T(1,128)S(1)}, s32[1,1,1,32]{3,2,1,0:T(1,128)}, u32[]{:S(2)}) copy-start(s32[1,1,1,32]{3,2,1,0:T(1,128)} %param.5) | copy-start | bytes 388
  1.4 28.1 %collective-permute-start.2 = (bf16[1536,256]{1,0:T(8,128)(2,1)S(1)}, bf16[1536,256]{1,0:T(8,128)(2,1)S(1)}, u32[]{:S(2)}, u32[]{:S(2)}) collective-permute-start(bf16[1536,256]{1,0:T(8,128)(2,1)S(1)} %bitcast.27), channel_id=1, source_target_pairs={{0,384},{128,0},{256,128},{384,256},{1,385},{129,1},{257,129},{385... | collective-permute-start | bytes 2359304 | tf_op jit(solution)/shard_map/ppermute | solution.py:158
  6.9 25.3 %collective-permute-start = (bf16[1536,256]{1,0:T(8,128)(2,1)S(1)}, bf16[1536,256]{1,0:T(8,128)(2,1)S(1)}, u32[]{:S(2)}, u32[]{:S(2)}) collective-permute-start(bf16[1536,256]{1,0:T(8,128)(2,1)S(1)} %bitcast.28), channel_id=1, source_target_pairs={{0,128},{128,256},{256,384},{384,0},{1,129},{129,257},{257,385},{3... | collective-permute-start | bytes 2359304 | tf_op jit(solution)/shard_map/ppermute | solution.py:158
  9.5 26.9 %all-to-all-start = ((s32[16,1,128]{2,1,0:T(1,128)}), s32[16,1,128]{2,1,0:T(1,128)S(1)}, u32[]{:S(2)}, u32[]{:S(2)}) async-start(s32[16,1,128]{2,1,0:T(1,128)} %broadcast_in_dim.8), calls=%async_computation | async-start | bytes 16384 | tf_op jit(solution)/shard_map/all_to_all | solution.py:150
  18.8 33.1 %collective-permute-start.6 = (bf16[256,1024]{1,0:T(8,128)(2,1)}, bf16[256,1024]{1,0:T(8,128)(2,1)S(1)}, u32[]{:S(2)}, u32[]{:S(2)}) collective-permute-start(bf16[256,1024]{1,0:T(8,128)(2,1)} %get-tuple-element.9), channel_id=1, source_target_pairs={{0,128},{128,256},{256,384},{384,0},{1,129},{129,257},{257,385},{3... | collective-permute-start | bytes 1572872 | tf_op jit(solution)/shard_map/ppermute | solution.py:158
  22.0 30.0 %collective-permute-start.4 = (bf16[256,1024]{1,0:T(8,128)(2,1)}, bf16[256,1024]{1,0:T(8,128)(2,1)}, u32[]{:S(2)}, u32[]{:S(2)}) collective-permute-start(bf16[256,1024]{1,0:T(8,128)(2,1)} %get-tuple-element.10), channel_id=1, source_target_pairs={{0,256},{128,384},{256,0},{384,128},{1,257},{129,385},{257,1},{385... | collective-permute-start | bytes 1572872 | tf_op jit(solution)/shard_map/ppermute | solution.py:158
  26.3 25.7 %collective-permute-start.5 = (bf16[256,1024]{1,0:T(8,128)(2,1)}, bf16[256,1024]{1,0:T(8,128)(2,1)}, u32[]{:S(2)}, u32[]{:S(2)}) collective-permute-start(bf16[256,1024]{1,0:T(8,128)(2,1)} %get-tuple-element.12), channel_id=1, source_target_pairs={{0,384},{128,0},{256,128},{384,256},{1,385},{129,1},{257,129},{385... | collective-permute-start | bytes 1572872 | tf_op jit(solution)/shard_map/ppermute | solution.py:158
  30.3 26.9 %collective-permute-start.3 = (bf16[1536,128]{1,0:T(8,128)(2,1)}, bf16[1536,128]{1,0:T(8,128)(2,1)}, u32[]{:S(2)}, u32[]{:S(2)}) collective-permute-start(bf16[1536,128]{1,0:T(8,128)(2,1)} %slice.9), channel_id=1, source_target_pairs={{0,384},{128,0},{256,128},{384,256},{1,385},{129,1},{257,129},{385... | collective-permute-start | bytes 1179656 | tf_op jit(solution)/shard_map/ppermute | solution.py:158
  33.0 25.5 %collective-permute-start.1 = (bf16[1536,128]{1,0:T(8,128)(2,1)}, bf16[1536,128]{1,0:T(8,128)(2,1)}, u32[]{:S(2)}, u32[]{:S(2)}) collective-permute-start(bf16[1536,128]{1,0:T(8,128)(2,1)} %slice.8), channel_id=1, source_target_pairs={{0,128},{128,256},{256,384},{384,0},{1,129},{129,257},{257,385},{3... | collective-permute-start | bytes 1179656 | tf_op jit(solution)/shard_map/ppermute | solution.py:158
  62.5 8.3 %collective-permute-start.7 = (bf16[1536,512]{1,0:T(8,128)(2,1)S(1)}, bf16[1536,512]{1,0:T(8,128)(2,1)S(1)}, u32[]{:S(2)}, u32[]{:S(2)}) collective-permute-start(bf16[1536,512]{1,0:T(8,128)(2,1)S(1)} %shard_map.39), channel_id=1, source_target_pairs={{0,1},{1,0},{2,3},{3,2},{4,5},{5,4},{6,7},{7,6},{8,9},{9,8},{10,11... | collective-permute-start | bytes 4718600 | tf_op jit(solution)/shard_map/ppermute | solution.py:188
  153.2 10.4 %collective-permute-start.8 = (bf16[4,96,512]{2,1,0:T(8,128)(2,1)S(1)}, bf16[4,96,512]{2,1,0:T(8,128)(2,1)S(1)}, u32[]{:S(2)}, u32[]{:S(2)}) collective-permute-start(bf16[4,96,512]{2,1,0:T(8,128)(2,1)S(1)} %bitcast.31), channel_id=1, source_target_pairs={{0,1},{1,0},{2,3},{3,2},{4,5},{5,4},{6,7},{7,6},{8,9},{9,8},{10,11... | collective-permute-start | bytes 1179656 | tf_op jit(solution)/shard_map/ppermute | solution.py:197

commit v7 on v6

v7 whole, which is shorter than its diff:
```python
import itertools

import jax
import jax.numpy as jnp
from jax import lax
from jax.experimental import pallas as pl
from jax.experimental.pallas import tpu as pltpu
from jax.sharding import Mesh, PartitionSpec as P

SWAP = [(0, 1), (1, 0)]
MIX = 73244475
SIDE = 4
OWNERS = SIDE * SIDE


def factor(base, offset):
    k = base + offset
    k = k ^ lax.shift_right_logical(k, 16)
    k = k * MIX
    k = k ^ lax.shift_right_logical(k, 16)
    k = k * MIX
    k = (k ^ lax.shift_right_logical(k, 16)) & 65535
    return k.astype(jnp.float32) + 491520.0


def factor_kernel(place, words_ref, *refs):
    outs, base_ref = refs[:2], refs[2]
    owner = pl.program_id(0)
    x, y = place[0], place[1]
    owner_y, owner_x = owner >> 2, owner & 3
    rows, width = outs[0].shape[1:]
    lane = lax.broadcasted_iota(jnp.int32, (8, 128), 1)
    sub = lax.broadcasted_iota(jnp.int32, (8, 128), 0)
    shared = 65599 * (lane >> 5) + 131071 * sub + 131071 * rows * owner
    keepers = (
        (((owner_y & 2) | (y & 1)) * 4 + x, 0),
        (((owner_y & 2) | (1 - (y & 1))) * 4 + x, 0),
        (owner_y * 4 + x, 1),
        (owner_y * 4 + ((owner_x & 2) | (x & 1)), 2),
        (owner, 3),
    )
    for at, (keeper, step) in enumerate(keepers):
        base_ref[at] = words_ref[pl.ds(keeper, 1), :] + shared + 7919 * step

    def fill(out_ref, group0):
        for row in range(0, rows, 16):
            for col in range(0, width, 128):
                halves = ([], [])
                for top in (row, row + 8):
                    offset = 65599 * (group0 + col // 32) + 131071 * top
                    f = [factor(base_ref[n], offset) for n in range(5)]
                    later = (f[2] * f[3] * f[4]) * (2.0**-76)
                    for pair in range(2):
                        halves[pair].append(f[pair] * later - 1.0)
                for pair in range(2):
                    block = jnp.concatenate(halves[pair], axis=0).astype(jnp.bfloat16)
                    out_ref[pair, row : row + 16, col : col + 128] = block

    for part in range(2):
        fill(outs[part], place[2 + part])


def factors(place, words, rows_all, width):
    rows = rows_all // OWNERS
    spec = pl.BlockSpec((2, rows, width), lambda i, p: (0, i, 0))
    shape = jax.ShapeDtypeStruct((2, rows_all, width), jnp.bfloat16)
    return pl.pallas_call(
        factor_kernel,
        grid_spec=pltpu.PrefetchScalarGridSpec(
            num_scalar_prefetch=1,
            grid=(OWNERS,),
            in_specs=[pl.BlockSpec(words.shape, lambda i, p: (0, 0))],
            out_specs=[spec, spec],
            scratch_shapes=[pltpu.VMEM((5, 8, 128), jnp.int32)],
        ),
        out_shape=[shape, shape],
        compiler_params=pltpu.CompilerParams(vmem_limit_bytes=8 * 2**20),
        cost_estimate=pl.CostEstimate(
            flops=20000 * rows_all * width, bytes_accessed=4 * rows_all * width * 2, transcendentals=0
        ),
    )(place, words)


def product(left, right):
    return jnp.dot(left, right, preferred_element_type=jnp.float32)


def early_kernel(place, h0, h1, h3, g0, g1, g3, fa_ref, fb_ref, outa_ref, outb_ref):
    rows_all, width = outa_ref.shape
    rows = rows_all // SIDE

    def block(at, carry):
        here = pl.ds(pl.multiple_of(at * rows, rows), rows)
        both = jnp.concatenate([h1[here, :], h3[here, :]], axis=1)
        for part, (f_ref, out_ref) in enumerate(((fa_ref, outa_ref), (fb_ref, outb_ref))):
            cut = pl.ds(pl.multiple_of(place[6 + part] * width, width), width)
            near = product(h0[here, :], g0[:, cut])
            far = product(both, jnp.concatenate([g1[:, cut], g3[:, cut]], axis=0))
            near = near + near * f_ref[0, here, :].astype(jnp.float32)
            out_ref[here, :] = near + (far + far * f_ref[1, here, :].astype(jnp.float32))
        return carry

    lax.fori_loop(0, SIDE, block, 0)


def late_kernel(place, h2a, h2b, g2, f_ref, more_ref, out_ref, *, part):
    rows_all, width = more_ref.shape
    rows = rows_all // SIDE
    cell_rows, cell_width = out_ref.shape[1:]
    cut = pl.ds(pl.multiple_of(place[6 + part] * width, width), width)

    def block(at, carry):
        here = pl.ds(pl.multiple_of(at * rows, rows), rows)
        left = jnp.concatenate([h2a[here, :], h2b[here, :]], axis=1)
        value = product(left, g2[:, cut])
        value = value + value * f_ref[0, here, :].astype(jnp.float32) + more_ref[here, :]
        value = value.astype(jnp.bfloat16)
        for x in range(SIDE):
            for side in range(2):
                cell = value[x * cell_rows : (x + 1) * cell_rows, side * cell_width : (side + 1) * cell_width]
                out_ref[(at * SIDE + x) * 2 + side] = cell
        return carry

    lax.fori_loop(0, SIDE, block, 0)


def in_vmem(body, place, args, shape, flops):
    return pl.pallas_call(
        body,
        in_specs=[pl.BlockSpec(memory_space=pltpu.SMEM)] + [pl.BlockSpec(memory_space=pltpu.VMEM)] * len(args),
        out_specs=jax.tree.map(lambda _: pl.BlockSpec(memory_space=pltpu.VMEM), shape),
        out_shape=shape,
        compiler_params=pltpu.CompilerParams(vmem_limit_bytes=24 * 2**20),
        cost_estimate=pl.CostEstimate(flops=flops, bytes_accessed=2**22, transcendentals=0),
    )(place, *args)


def early(place, h, g, scale):
    rows_all, tokens = h[0].shape
    width = scale[0].shape[2]
    shape = jax.ShapeDtypeStruct((rows_all, width), jnp.float32)
    return in_vmem(early_kernel, place, [*h, *g, *scale], [shape, shape], 12 * rows_all * tokens * width)


def late(place, h, g, scale, more, part):
    rows_all, width = more.shape

    def body(*refs):
        late_kernel(*refs, part=part)

    shape = jax.ShapeDtypeStruct((2 * OWNERS, rows_all // OWNERS, width // 2), jnp.bfloat16)
    return in_vmem(body, place, [*h, g, scale, more], shape, 8 * rows_all * g.shape[0] * width)


def weave_kernel(place, blocks_ref, out_ref):
    width = blocks_ref.shape[3]
    for z1, z0, core, low in itertools.product(range(2), repeat=4):
        first = (((z1 * 2 + low) * 2 + core) * 2 + z0) * width
        out_ref[:, first : first + width] = blocks_ref[z1 * 4 + z0 * 2 + core, low]


def weave(place, blocks, columns):
    rows, width = blocks.shape[2:]
    shape = jax.ShapeDtypeStruct((rows, columns), blocks.dtype)
    return in_vmem(weave_kernel, place, [blocks], shape, 1)


def exchange(blocks, axes):
    return lax.all_to_all(blocks, axes, 0, 0, tiled=True)


def added(blocks, axis=0):
    return jnp.sum(blocks.astype(jnp.float32), axis=axis).astype(jnp.bfloat16)


def along_y(block, step):
    return lax.ppermute(block, "y", [(at, (at + step) % SIDE) for at in range(SIDE)])


def per_device(hidden, grad_out, seed_table):
    x, y, core = lax.axis_index("x"), lax.axis_index("y"), lax.axis_index("core")
    tokens, columns = grad_out.shape[1:]
    quarter = columns // SIDE
    half = quarter // 2
    words = exchange(jnp.tile(seed_table[0, 0], (OWNERS, 4)), ("y", "x"))
    other = 1 - core
    groups = half // 32
    place = [x, y, (y * 2 + other) * groups, (y * 2 + core) * groups, y * 2 + other, y * 2 + core, other, core]
    place = jnp.stack(place).astype(jnp.int32)

    h_own = hidden[0].T
    h_low = along_y(h_own, 1)
    h_high = along_y(h_own, -1)
    h_facing_a = along_y(h_low[:, : tokens // 2], 1)
    h_facing_b = along_y(h_high[:, tokens // 2 :], -1)
    def quarter_for(step):
        return lax.dynamic_slice_in_dim(grad_out[0], (y + step) % SIDE * quarter, quarter, 1)

    g_low, g_high, g_facing = (along_y(quarter_for(step), step) for step in (1, -1, 2))

    rows_all = h_own.shape[0]
    scale = factors(place, words, rows_all, half)
    three = early(place, [h_own, h_high, h_low], [quarter_for(0), g_high, g_low], scale)
    facing = [h_facing_a, h_facing_b]
    sent = late(place, facing, g_facing, scale[0], three[0], 0)
    received = lax.ppermute(sent, "core", SWAP)
    both = late(place, facing, g_facing, scale[1], three[1], 1).astype(jnp.float32) + received.astype(jnp.float32)

    got = exchange(both.astype(jnp.bfloat16), ("y", "x", "z0"))
    owned = added(got.reshape(SIDE, 2 * SIDE, *got.shape[1:]), 1)
    near = added(exchange(owned, "z1").reshape(2, 2, *got.shape[1:]))
    total = added(lax.all_gather(near, "zh"))
    return weave(place, lax.all_gather(total, ("z1", "z0", "core")), columns)[None]


def solution(mesh):
    devices = mesh.devices
    zero, dp = devices.shape
    names = ("y", "x", "zh", "z1", "z0", "core")
    split = Mesh(devices.reshape(SIDE, zero // SIDE, dp // 8, 2, 2, 2), names)
    dp_parts = ("zh", "z1", "z0", "core")
    return jax.shard_map(
        per_device,
        mesh=split,
        in_specs=(
            P(dp_parts, ("y", "x"), None),
            P(dp_parts, ("y", "x"), None),
            P(dp_parts, ("y", "x"), None, None),
        ),
        out_specs=P(None, ("y", "x"), None),
        check_vma=False,
    )
```

time: 166 us -> 157 us (0.946)
  waiting for transfers between devices: 7.9 us -> 0.75 us
  starting transfers between devices: 43.2 us -> 37.4 us
  blocking collectives: 81.5 us -> 83.8 us
    ppermute x1 -> x0, starting transfers between devices: 9.03 us -> none  [per_device(): there = lax.ppermute(here, 'core', SWAP)]
    all_gather x1, blocking collectives: 15.2 us -> 23.1 us  [per_device(): lax.all_gather(total, ('z1', 'z0', 'core'))]
    all_to_all x2, blocking collectives: 42.3 us -> 35.7 us  [exchange(): return lax.all_to_all(blocks, axes, 0, 0, tiled=True)]
    ppermute x7, waiting for transfers between devices: 6.57 us -> 0.02 us  [along_y(): lax.ppermute(block, 'y', [(at, (at + step) % SIDE) for at in range(SIDE)])]
    ppermute x1, starting transfers between devices: 4.41 us -> 8.11 us  [per_device(): received = lax.ppermute(sent, 'core', SWAP)]
    pallas_call x3 -> x4, Pallas kernels: 9.83 us -> 10.7 us  [in_vmem(): pl.pallas_call(body, in_specs=[pl.BlockSpec(memory_space=pltpu.SMEM)] + [...]
  transfers between devices with their start and end apart: 10 -> 9, of which waited for: 3 -> 1; matrix products, arithmetic and copies ran while one was open for 3% -> 4% of each run, Pallas kernels for 12% -> 14%
where the time goes in v7:
time: 157 us; the launch traced here: 156 us
  blocking collectives  83.8 us (53%)
  starting transfers between devices  37.4 us (24%)
  Pallas kernels  26.1 us (17%)
  local copies, waits for them, and re-layouts  7.08 us (5%)
    all_to_all x2, blocking collectives, exchange(): return lax.all_to_all(blocks, axes, 0, 0, tiled=True)  35.7 us
    all_gather x1, blocking collectives, per_device(): total = added(lax.all_gather(near, 'zh'))  24.9 us
    ppermute x7, starting transfers between devices, along_y(): lax.ppermute(block, 'y', [(at, (at + step) % SIDE) for at in range(SIDE)])  23.8 us
    all_gather x1, blocking collectives, per_device(): lax.all_gather(total, ('z1', 'z0', 'core'))  23.1 us
    pallas_call x1, Pallas kernels, factors(): pl.pallas_call(factor_kernel, grid_spec=pltpu.PrefetchScalarGridSpec(num_...  15.4 us
    pallas_call x4, Pallas kernels, in_vmem(): pl.pallas_call(body, in_specs=[pl.BlockSpec(memory_space=pltpu.SMEM)] + [...  10.7 us
    ppermute x1, starting transfers between devices, per_device(): received = lax.ppermute(sent, 'core', SWAP)  8.11 us
    all_to_all x1, starting transfers between devices, exchange(): return lax.all_to_all(blocks, axes, 0, 0, tiled=True)  5.47 us
  transfers between devices with their start and end apart: 9, of which 1 were waited for; matrix products, arithmetic and copies ran while one was open for 4% of the time, Pallas kernels for 14%

profile of v7, /device:TPU:1, one launch (start us, length us, event | category | flops | bytes accessed | tf_op | source)
XLA Modules:
  0.0 156.3 jit_solution(7841233964195003973)
XLA Ops:
  0.0 1.4 copy.6
  1.4 4.0 %collective-permute-start = (bf16[1536,256]{1,0:T(8,128)(2,1)S(1)}, bf16[1536,256]{1,0:T(8,128)(2,1)S(1)}, u32[]{:S(2)}, u32[]{:S(2)}) collective-permute-start(bf16[1536,256]{1,0:T(8,128)(2,1)S(1)} %bitcast.27), channel_id=1, source_target_pairs={{0,128},{128,256},{256,384},{384,0},{1,129},{129,257},{257,385},{3... | collective-permute-start | bytes 2359304 | tf_op jit(solution)/shard_map/ppermute | solution.py:177
  5.4 3.4 %collective-permute-start.2 = (bf16[1536,256]{1,0:T(8,128)(2,1)S(1)}, bf16[1536,256]{1,0:T(8,128)(2,1)S(1)}, u32[]{:S(2)}, u32[]{:S(2)}) collective-permute-start(bf16[1536,256]{1,0:T(8,128)(2,1)S(1)} %bitcast.28), channel_id=1, source_target_pairs={{0,384},{128,0},{256,128},{384,256},{1,385},{129,1},{257,129},{385... | collective-permute-start | bytes 2359304 | tf_op jit(solution)/shard_map/ppermute | solution.py:177
  8.8 0.7 tile.13
  9.5 0.1 tile.14
  9.6 0.6 tile.15
  10.2 5.5 %all-to-all-start = ((s32[16,1,128]{2,1,0:T(1,128)}), s32[16,1,128]{2,1,0:T(1,128)S(1)}, u32[]{:S(2)}, u32[]{:S(2)}) async-start(s32[16,1,128]{2,1,0:T(1,128)} %tile.15), calls=%async_computation | async-start | bytes 16384 | tf_op jit(solution)/shard_map/all_to_all | solution.py:169
  15.7 2.7 %dynamic-slice_bitcast_fusion = (bf16[256,1024]{1,0:T(8,128)(2,1)}, bf16[256,1024]{1,0:T(8,128)(2,1)S(1)}, bf16[256,1024]{1,0:T(8,128)(2,1)}, bf16[256,1024]{1,0:T(8,128)(2,1)}) fusion(bf16[1,256,4096]{2,1,0:T(8,128)(2,1)} %param.4, s32[]{:T(128)S(6)} %select_n.38, s32[]{:T(128)S(6)} %select_n.34, s32[]{:T(128)S(6)} %select_n.32, s32[]{:T(128)S(6)} %select_n.36), kind=kLoop, calls=%fused_computation.2 | loop fusion | bytes 4194320 | tf_op jit(solution)/shard_map/dynamic_slice | solution.py:197
  18.4 4.4 %collective-permute-start.5 = (bf16[256,1024]{1,0:T(8,128)(2,1)}, bf16[256,1024]{1,0:T(8,128)(2,1)}, u32[]{:S(2)}, u32[]{:S(2)}) collective-permute-start(bf16[256,1024]{1,0:T(8,128)(2,1)} %get-tuple-element.16), channel_id=1, source_target_pairs={{0,384},{128,0},{256,128},{384,256},{1,385},{129,1},{257,129},{385... | collective-permute-start | bytes 1572872 | tf_op jit(solution)/shard_map/ppermute | solution.py:177
  22.8 1.9 %collective-permute-start.6 = (bf16[256,1024]{1,0:T(8,128)(2,1)}, bf16[256,1024]{1,0:T(8,128)(2,1)}, u32[]{:S(2)}, u32[]{:S(2)}) collective-permute-start(bf16[256,1024]{1,0:T(8,128)(2,1)} %get-tuple-element.13), channel_id=1, source_target_pairs={{0,128},{128,256},{256,384},{384,0},{1,129},{129,257},{257,385},{3... | collective-permute-start | bytes 1572872 | tf_op jit(solution)/shard_map/ppermute | solution.py:177
  24.8 3.7 %collective-permute-start.4 = (bf16[256,1024]{1,0:T(8,128)(2,1)}, bf16[256,1024]{1,0:T(8,128)(2,1)S(1)}, u32[]{:S(2)}, u32[]{:S(2)}) collective-permute-start(bf16[256,1024]{1,0:T(8,128)(2,1)} %get-tuple-element.15), channel_id=1, source_target_pairs={{0,256},{128,384},{256,0},{384,128},{1,257},{129,385},{257,1},{385... | collective-permute-start | bytes 1572872 | tf_op jit(solution)/shard_map/ppermute | solution.py:177
  28.4 0.1 stack.35.place.refs_0_
  28.5 0.0 collective-permute-done.h3
  28.5 0.8 slice.8
  29.3 3.4 %collective-permute-start.1 = (bf16[1536,128]{1,0:T(8,128)(2,1)}, bf16[1536,128]{1,0:T(8,128)(2,1)}, u32[]{:S(2)}, u32[]{:S(2)}) collective-permute-start(bf16[1536,128]{1,0:T(8,128)(2,1)} %slice.8), channel_id=1, source_target_pairs={{0,128},{128,256},{256,384},{384,0},{1,129},{129,257},{257,385},{3... | collective-permute-start | bytes 1179656 | tf_op jit(solution)/shard_map/ppermute | solution.py:177
  32.7 0.0 collective-permute-done.2.h1
  32.7 0.8 slice.9
  33.5 3.1 %collective-permute-start.3 = (bf16[1536,128]{1,0:T(8,128)(2,1)}, bf16[1536,128]{1,0:T(8,128)(2,1)}, u32[]{:S(2)}, u32[]{:S(2)}) collective-permute-start(bf16[1536,128]{1,0:T(8,128)(2,1)} %slice.9), channel_id=1, source_target_pairs={{0,384},{128,0},{256,128},{384,256},{1,385},{129,1},{257,129},{385... | collective-permute-start | bytes 1179656 | tf_op jit(solution)/shard_map/ppermute | solution.py:177
  36.6 0.0 all-to-all-done
  36.6 15.4 %shard_map.37 = (bf16[2,1536,512]{2,1,0:T(8,128)(2,1)S(1)}, bf16[2,1536,512]{2,1,0:T(8,128)(2,1)S(1)}) custom-call(s32[8]{0:T(128)S(1)} %stack.35.place.refs_0_, s32[16,128]{1,0:T(8,128)S(1)} %bitcast.31), custom_call_target="tpu_custom_call" | custom-call | flops 15728640000 | bytes 6291456 | tf_op jit(solution)/shard_map/pallas_call | solution.py:67
  51.9 0.0 collective-permute-done.5.g1
  51.9 0.0 collective-permute-done.6.g3
  52.0 4.7 %shard_map.38 = (f32[1536,512]{1,0:T(8,128)S(1)}, f32[1536,512]{1,0:T(8,128)S(1)}) custom-call(s32[8]{0:T(128)S(1)} %stack.35.place.refs_0_, bf16[1536,256]{1,0:T(8,128)(2,1)S(1)} %bitcast.29, bf16[1536,256]{1,0:T(8,128)(2,1)S(1)} %collective-permute-done.2.h1, bf16[1536,256]{1,0:T(8,128)(2,1)S(1)} %collective-permute-done.h3, ...), custom_call_target="tpu_custom_call" | custom-call | flops 2415919104 | bytes 4194304 | tf_op jit(solution)/shard_map/pallas_call | solution.py:128
  56.7 0.0 collective-permute-done.4.refs_3_
  56.7 0.0 collective-permute-done.1.refs_1_
  56.7 0.0 collective-permute-done.3.refs_2_
  56.7 2.2 %shard_map.40 = bf16[32,96,256]{2,1,0:T(8,128)(2,1)S(1)} custom-call(s32[8]{0:T(128)S(1)} %stack.35.place.refs_0_, bf16[1536,128]{1,0:T(8,128)(2,1)} %collective-permute-done.1.refs_1_, bf16[1536,128]{1,0:T(8,128)(2,1)} %collective-permute-done.3.refs_2_, bf16[256,1024]{1,0:T(8,128)(2,1)S(1)} %collective-permute-done.4.refs_3_, ...), custom_call_target="tpu_custom_call" | custom-call | flops 1610612736 | bytes 4194304 | tf_op jit(solution)/shard_map/pallas_call | solution.py:128
  59.0 8.1 %collective-permute-start.7 = (bf16[32,96,256]{2,1,0:T(8,128)(2,1)S(1)}, bf16[32,96,256]{2,1,0:T(8,128)(2,1)S(1)}, u32[]{:S(2)}, u32[]{:S(2)}) collective-permute-start(bf16[32,96,256]{2,1,0:T(8,128)(2,1)S(1)} %shard_map.40), channel_id=1, source_target_pairs={{0,1},{1,0},{2,3},{3,2},{4,5},{5,4},{6,7},{7,6},{8,9},{9,8},{10,11... | collective-permute-start | bytes 4718600 | tf_op jit(solution)/shard_map/ppermute | solution.py:206
  67.1 2.3 %shard_map.39 = bf16[32,96,256]{2,1,0:T(8,128)(2,1)S(1)} custom-call(s32[8]{0:T(128)S(1)} %stack.35.place.refs_0_, bf16[1536,128]{1,0:T(8,128)(2,1)} %collective-permute-done.1.refs_1_, bf16[1536,128]{1,0:T(8,128)(2,1)} %collective-permute-done.3.refs_2_, bf16[256,1024]{1,0:T(8,128)(2,1)S(1)} %collective-permute-done.4.refs_3_, ...), custom_call_target="tpu_custom_call" | custom-call | flops 1610612736 | bytes 4194304 | tf_op jit(solution)/shard_map/pallas_call | solution.py:128
  69.4 0.7 collective-permute-done.7
  70.1 0.6 add_convert_fusion
  70.7 26.8 %all_to_all.18 = bf16[32,96,256]{2,1,0:T(8,128)(2,1)S(1)} all-to-all(bf16[32,96,256]{2,1,0:T(8,128)(2,1)S(1)} %add_convert_fusion), channel_id=1, replica_groups=mesh['y'=4,'x'=4,'zh'=4,'z1'=2,'z0'=2,'core'=2] {'y','x','z0'}, dimensions={0} | all-to-all | bytes 3145728 | tf_op jit(solution)/shard_map/all_to_all | solution.py:169
  97.5 0.2 bitcast_reduce_fusion
  97.7 8.9 %all_to_all.19 = bf16[4,96,256]{2,1,0:T(8,128)(2,1)S(1)} all-to-all(bf16[4,96,256]{2,1,0:T(8,128)(2,1)S(1)} %bitcast_reduce_fusion), channel_id=1, replica_groups=mesh['y'=4,'x'=4,'zh'=4,'z1'=2,'z0'=2,'core'=2] {'z1'}, dimensions={0} | all-to-all | bytes 393216 | tf_op jit(solution)/shard_map/all_to_all | solution.py:169
  106.7 24.9 %all-gather = bf16[8,96,256]{2,1,0:T(8,128)(2,1)S(1)} all-gather(bf16[2,96,256]{2,1,0:T(8,128)(2,1)S(1)} %reduce_sum.37), channel_id=2, replica_groups=mesh['y'=4,'x'=4,'zh'=4,'z1'=2,'z0'=2,'core'=2] {'zh'}, dimensions={0}, use_global_device_ids=true | all-gather | bytes 491520 | tf_op jit(solution)/shard_map/all_gather | solution.py:212
  131.6 0.1 reduce_sum.38
  131.7 23.1 %all-gather.1 = bf16[16,96,256]{2,1,0:T(8,128)(2,1)S(1)} all-gather(bf16[2,96,256]{2,1,0:T(8,128)(2,1)S(1)} %reduce_sum.38), channel_id=3, replica_groups=mesh['y'=4,'x'=4,'zh'=4,'z1'=2,'z0'=2,'core'=2] {'z1','z0','core'}, dimensions={0}, use_global_device_ids=true | all-gather | bytes 884736 | tf_op jit(solution)/shard_map/all_gather | solution.py:213
  154.8 1.5 shard_map.41
  (1 shorter events, 0.0 us)
Async XLA Ops:
  1.4 27.1 %collective-permute-start = (bf16[1536,256]{1,0:T(8,128)(2,1)S(1)}, bf16[1536,256]{1,0:T(8,128)(2,1)S(1)}, u32[]{:S(2)}, u32[]{:S(2)}) collective-permute-start(bf16[1536,256]{1,0:T(8,128)(2,1)S(1)} %bitcast.27), channel_id=1, source_target_pairs={{0,128},{128,256},{256,384},{384,0},{1,129},{129,257},{257,385},{3... | collective-permute-start | bytes 2359304 | tf_op jit(solution)/shard_map/ppermute | solution.py:177
  5.4 27.2 %collective-permute-start.2 = (bf16[1536,256]{1,0:T(8,128)(2,1)S(1)}, bf16[1536,256]{1,0:T(8,128)(2,1)S(1)}, u32[]{:S(2)}, u32[]{:S(2)}) collective-permute-start(bf16[1536,256]{1,0:T(8,128)(2,1)S(1)} %bitcast.28), channel_id=1, source_target_pairs={{0,384},{128,0},{256,128},{384,256},{1,385},{129,1},{257,129},{385... | collective-permute-start | bytes 2359304 | tf_op jit(solution)/shard_map/ppermute | solution.py:177
  10.2 26.4 %all-to-all-start = ((s32[16,1,128]{2,1,0:T(1,128)}), s32[16,1,128]{2,1,0:T(1,128)S(1)}, u32[]{:S(2)}, u32[]{:S(2)}) async-start(s32[16,1,128]{2,1,0:T(1,128)} %tile.15), calls=%async_computation | async-start | bytes 16384 | tf_op jit(solution)/shard_map/all_to_all | solution.py:169
  18.4 33.5 %collective-permute-start.5 = (bf16[256,1024]{1,0:T(8,128)(2,1)}, bf16[256,1024]{1,0:T(8,128)(2,1)}, u32[]{:S(2)}, u32[]{:S(2)}) collective-permute-start(bf16[256,1024]{1,0:T(8,128)(2,1)} %get-tuple-element.16), channel_id=1, source_target_pairs={{0,384},{128,0},{256,128},{384,256},{1,385},{129,1},{257,129},{385... | collective-permute-start | bytes 1572872 | tf_op jit(solution)/shard_map/ppermute | solution.py:177
  22.8 29.1 %collective-permute-start.6 = (bf16[256,1024]{1,0:T(8,128)(2,1)}, bf16[256,1024]{1,0:T(8,128)(2,1)}, u32[]{:S(2)}, u32[]{:S(2)}) collective-permute-start(bf16[256,1024]{1,0:T(8,128)(2,1)} %get-tuple-element.13), channel_id=1, source_target_pairs={{0,128},{128,256},{256,384},{384,0},{1,129},{129,257},{257,385},{3... | collective-permute-start | bytes 1572872 | tf_op jit(solution)/shard_map/ppermute | solution.py:177
  24.8 31.9 %collective-permute-start.4 = (bf16[256,1024]{1,0:T(8,128)(2,1)}, bf16[256,1024]{1,0:T(8,128)(2,1)S(1)}, u32[]{:S(2)}, u32[]{:S(2)}) collective-permute-start(bf16[256,1024]{1,0:T(8,128)(2,1)} %get-tuple-element.15), channel_id=1, source_target_pairs={{0,256},{128,384},{256,0},{384,128},{1,257},{129,385},{257,1},{385... | collective-permute-start | bytes 1572872 | tf_op jit(solution)/shard_map/ppermute | solution.py:177
  29.3 27.4 %collective-permute-start.1 = (bf16[1536,128]{1,0:T(8,128)(2,1)}, bf16[1536,128]{1,0:T(8,128)(2,1)}, u32[]{:S(2)}, u32[]{:S(2)}) collective-permute-start(bf16[1536,128]{1,0:T(8,128)(2,1)} %slice.8), channel_id=1, source_target_pairs={{0,128},{128,256},{256,384},{384,0},{1,129},{129,257},{257,385},{3... | collective-permute-start | bytes 1179656 | tf_op jit(solution)/shard_map/ppermute | solution.py:177
  33.5 23.2 %collective-permute-start.3 = (bf16[1536,128]{1,0:T(8,128)(2,1)}, bf16[1536,128]{1,0:T(8,128)(2,1)}, u32[]{:S(2)}, u32[]{:S(2)}) collective-permute-start(bf16[1536,128]{1,0:T(8,128)(2,1)} %slice.9), channel_id=1, source_target_pairs={{0,384},{128,0},{256,128},{384,256},{1,385},{129,1},{257,129},{385... | collective-permute-start | bytes 1179656 | tf_op jit(solution)/shard_map/ppermute | solution.py:177
  59.0 11.1 %collective-permute-start.7 = (bf16[32,96,256]{2,1,0:T(8,128)(2,1)S(1)}, bf16[32,96,256]{2,1,0:T(8,128)(2,1)S(1)}, u32[]{:S(2)}, u32[]{:S(2)}) collective-permute-start(bf16[32,96,256]{2,1,0:T(8,128)(2,1)S(1)} %shard_map.40), channel_id=1, source_target_pairs={{0,1},{1,0},{2,3},{3,2},{4,5},{5,4},{6,7},{7,6},{8,9},{9,8},{10,11... | collective-permute-start | bytes 4718600 | tf_op jit(solution)/shard_map/ppermute | solution.py:206

commit v8 on v7

--- a/solution.py
+++ b/solution.py
@@ -40,15 +40,17 @@
         (owner, 3),
     )
     for at, (keeper, step) in enumerate(keepers):
-        base_ref[at] = words_ref[pl.ds(keeper, 1), :] + shared + 7919 * step
-
-    def fill(out_ref, group0):
+        base = words_ref[pl.ds(keeper, 1), :] + shared + 7919 * step
+        for part in range(2):
+            base_ref[part, at] = base + 65599 * place[2 + part]
+
+    def fill(out_ref, bases):
         for row in range(0, rows, 16):
             for col in range(0, width, 128):
                 halves = ([], [])
                 for top in (row, row + 8):
-                    offset = 65599 * (group0 + col // 32) + 131071 * top
-                    f = [factor(base_ref[n], offset) for n in range(5)]
+                    offset = 65599 * (col // 32) + 131071 * top
+                    f = [factor(bases[n], offset) for n in range(5)]
                     later = (f[2] * f[3] * f[4]) * (2.0**-76)
                     for pair in range(2):
                         halves[pair].append(f[pair] * later - 1.0)
@@ -57,7 +59,7 @@
                     out_ref[pair, row : row + 16, col : col + 128] = block
 
     for part in range(2):
-        fill(outs[part], place[2 + part])
+        fill(outs[part], [base_ref[part, n] for n in range(5)])
 
 
 def factors(place, words, rows_all, width):
@@ -71,7 +73,7 @@
             grid=(OWNERS,),
             in_specs=[pl.BlockSpec(words.shape, lambda i, p: (0, 0))],
             out_specs=[spec, spec],
-            scratch_shapes=[pltpu.VMEM((5, 8, 128), jnp.int32)],
+            scratch_shapes=[pltpu.VMEM((2, 5, 8, 128), jnp.int32)],
         ),
         out_shape=[shape, shape],
         compiler_params=pltpu.CompilerParams(vmem_limit_bytes=8 * 2**20),
@@ -82,7 +84,7 @@
 
 
 def product(left, right):
-    return jnp.dot(left, right, preferred_element_type=jnp.float32)
+    return lax.dot_general(left, right, (((0,), (0,)), ((), ())), preferred_element_type=jnp.float32)
 
 
 def early_kernel(place, h0, h1, h3, g0, g1, g3, fa_ref, fb_ref, outa_ref, outb_ref):
@@ -91,16 +93,17 @@
 
     def block(at, carry):
         here = pl.ds(pl.multiple_of(at * rows, rows), rows)
-        both = jnp.concatenate([h1[here, :], h3[here, :]], axis=1)
+        both = jnp.concatenate([h1[:, here], h3[:, here]], axis=0)
         for part, (f_ref, out_ref) in enumerate(((fa_ref, outa_ref), (fb_ref, outb_ref))):
             cut = pl.ds(pl.multiple_of(place[6 + part] * width, width), width)
-            near = product(h0[here, :], g0[:, cut])
+            mine = pl.ds(pl.multiple_of(place[4 + part] * width, width), width)
+            near = product(h0[:, here], g0[:, mine])
             far = product(both, jnp.concatenate([g1[:, cut], g3[:, cut]], axis=0))
             near = near + near * f_ref[0, here, :].astype(jnp.float32)
             out_ref[here, :] = near + (far + far * f_ref[1, here, :].astype(jnp.float32))
         return carry
 
-    lax.fori_loop(0, SIDE, block, 0)
+    lax.fori_loop(0, SIDE, block, 0, unroll=True)
 
 
 def late_kernel(place, h2a, h2b, g2, f_ref, more_ref, out_ref, *, part):
@@ -111,7 +114,7 @@
 
     def block(at, carry):
         here = pl.ds(pl.multiple_of(at * rows, rows), rows)
-        left = jnp.concatenate([h2a[here, :], h2b[here, :]], axis=1)
+        left = jnp.concatenate([h2a[:, here], h2b[:, here]], axis=0)
         value = product(left, g2[:, cut])
         value = value + value * f_ref[0, here, :].astype(jnp.float32) + more_ref[here, :]
         value = value.astype(jnp.bfloat16)
@@ -121,7 +124,7 @@
                 out_ref[(at * SIDE + x) * 2 + side] = cell
         return carry
 
-    lax.fori_loop(0, SIDE, block, 0)
+    lax.fori_loop(0, SIDE, block, 0, unroll=True)
 
 
 def in_vmem(body, place, args, shape, flops):
@@ -136,7 +139,7 @@
 
 
 def early(place, h, g, scale):
-    rows_all, tokens = h[0].shape
+    tokens, rows_all = h[0].shape
     width = scale[0].shape[2]
     shape = jax.ShapeDtypeStruct((rows_all, width), jnp.float32)
     return in_vmem(early_kernel, place, [*h, *g, *scale], [shape, shape], 12 * rows_all * tokens * width)
@@ -188,19 +191,19 @@
     place = [x, y, (y * 2 + other) * groups, (y * 2 + core) * groups, y * 2 + other, y * 2 + core, other, core]
     place = jnp.stack(place).astype(jnp.int32)
 
-    h_own = hidden[0].T
+    h_own = hidden[0]
     h_low = along_y(h_own, 1)
     h_high = along_y(h_own, -1)
-    h_facing_a = along_y(h_low[:, : tokens // 2], 1)
-    h_facing_b = along_y(h_high[:, tokens // 2 :], -1)
+    h_facing_a = along_y(h_low[: tokens // 2], 1)
+    h_facing_b = along_y(h_high[tokens // 2 :], -1)
     def quarter_for(step):
         return lax.dynamic_slice_in_dim(grad_out[0], (y + step) % SIDE * quarter, quarter, 1)
 
     g_low, g_high, g_facing = (along_y(quarter_for(step), step) for step in (1, -1, 2))
 
-    rows_all = h_own.shape[0]
+    rows_all = h_own.shape[1]
     scale = factors(place, words, rows_all, half)
-    three = early(place, [h_own, h_high, h_low], [quarter_for(0), g_high, g_low], scale)
+    three = early(place, [h_own, h_high, h_low], [grad_out[0], g_high, g_low], scale)
     facing = [h_facing_a, h_facing_b]
     sent = late(place, facing, g_facing, scale[0], three[0], 0)
     received = lax.ppermute(sent, "core", SWAP)

time: 157 us -> 154 us (0.981)
  Pallas kernels: 26.1 us -> 23.7 us
    pallas_call x4, Pallas kernels: 10.7 us -> 8.28 us  [in_vmem(): pl.pallas_call(body, in_specs=[pl.BlockSpec(memory_space=pltpu.SMEM)] + [...]
where the time goes in v8:
time: 154 us
  blocking collectives  84.5 us (55%)
  starting transfers between devices  37.3 us (24%)
  Pallas kernels  23.7 us (15%)
  local copies, waits for them, and re-layouts  5.59 us (4%)
  waiting for transfers between devices  1.75 us (1%)
    all_to_all x2, blocking collectives, exchange(): return lax.all_to_all(blocks, axes, 0, 0, tiled=True)  36.4 us
    all_gather x1, blocking collectives, per_device(): total = added(lax.all_gather(near, 'zh'))  24.9 us
    ppermute x7, starting transfers between devices, along_y(): lax.ppermute(block, 'y', [(at, (at + step) % SIDE) for at in range(SIDE)])  23.8 us
    all_gather x1, blocking collectives, per_device(): lax.all_gather(total, ('z1', 'z0', 'core'))  23.1 us
    pallas_call x1, Pallas kernels, factors(): pl.pallas_call(factor_kernel, grid_spec=pltpu.PrefetchScalarGridSpec(num_...  15.4 us
    pallas_call x4, Pallas kernels, in_vmem(): pl.pallas_call(body, in_specs=[pl.BlockSpec(memory_space=pltpu.SMEM)] + [...  8.28 us
    ppermute x1, starting transfers between devices, per_device(): received = lax.ppermute(sent, 'core', SWAP)  7.98 us
    all_to_all x1, starting transfers between devices, exchange(): return lax.all_to_all(blocks, axes, 0, 0, tiled=True)  5.47 us
  transfers between devices with their start and end apart: 9, of which 1 were waited for; matrix products, arithmetic and copies ran while one was open for 4% of the time, Pallas kernels for 14%

profile of v8, /device:TPU:1, one launch (start us, length us, event | category | flops | bytes accessed | tf_op | source)
XLA Modules:
  0.0 154.0 jit_solution(17241420101398567619)
XLA Ops:
  0.0 4.0 %collective-permute-start = (bf16[256,1536]{1,0:T(8,128)(2,1)}, bf16[256,1536]{1,0:T(8,128)(2,1)S(1)}, u32[]{:S(2)}, u32[]{:S(2)}) collective-permute-start(bf16[256,1536]{1,0:T(8,128)(2,1)} %bitcast.26), channel_id=1, source_target_pairs={{0,128},{128,256},{256,384},{384,0},{1,129},{129,257},{257,385},{3... | collective-permute-start | bytes 2359304 | tf_op jit(solution)/shard_map/ppermute | solution.py:180
  4.0 3.4 %collective-permute-start.2 = (bf16[256,1536]{1,0:T(8,128)(2,1)}, bf16[256,1536]{1,0:T(8,128)(2,1)S(1)}, u32[]{:S(2)}, u32[]{:S(2)}) collective-permute-start(bf16[256,1536]{1,0:T(8,128)(2,1)} %bitcast.27), channel_id=1, source_target_pairs={{0,384},{128,0},{256,128},{384,256},{1,385},{129,1},{257,129},{385... | collective-permute-start | bytes 2359304 | tf_op jit(solution)/shard_map/ppermute | solution.py:180
  7.4 0.7 tile.13
  8.1 0.1 tile.14
  8.1 0.6 tile.15
  8.8 5.5 %all-to-all-start = ((s32[16,1,128]{2,1,0:T(1,128)}), s32[16,1,128]{2,1,0:T(1,128)S(1)}, u32[]{:S(2)}, u32[]{:S(2)}) async-start(s32[16,1,128]{2,1,0:T(1,128)} %tile.15), calls=%async_computation | async-start | bytes 16384 | tf_op jit(solution)/shard_map/all_to_all | solution.py:172
  14.3 2.5 %dynamic-slice_bitcast_fusion = (bf16[256,1024]{1,0:T(8,128)(2,1)}, bf16[256,1024]{1,0:T(8,128)(2,1)}, bf16[256,1024]{1,0:T(8,128)(2,1)}) fusion(bf16[1,256,4096]{2,1,0:T(8,128)(2,1)} %param.4, s32[]{:T(128)S(6)} %select_n.29, s32[]{:T(128)S(6)} %select_n.25, s32[]{:T(128)S(6)} %select_n.27), kind=kLoop, calls=%fused_computation.2 | loop fusion | bytes 3145740 | tf_op jit(solution)/shard_map/dynamic_slice | solution.py:200
  16.8 4.4 %collective-permute-start.5 = (bf16[256,1024]{1,0:T(8,128)(2,1)}, bf16[256,1024]{1,0:T(8,128)(2,1)S(1)}, u32[]{:S(2)}, u32[]{:S(2)}) collective-permute-start(bf16[256,1024]{1,0:T(8,128)(2,1)} %get-tuple-element.15), channel_id=1, source_target_pairs={{0,384},{128,0},{256,128},{384,256},{1,385},{129,1},{257,129},{385... | collective-permute-start | bytes 1572872 | tf_op jit(solution)/shard_map/ppermute | solution.py:180
  21.3 1.9 %collective-permute-start.6 = (bf16[256,1024]{1,0:T(8,128)(2,1)}, bf16[256,1024]{1,0:T(8,128)(2,1)}, u32[]{:S(2)}, u32[]{:S(2)}) collective-permute-start(bf16[256,1024]{1,0:T(8,128)(2,1)} %get-tuple-element.13), channel_id=1, source_target_pairs={{0,128},{128,256},{256,384},{384,0},{1,129},{129,257},{257,385},{3... | collective-permute-start | bytes 1572872 | tf_op jit(solution)/shard_map/ppermute | solution.py:180
  23.2 3.7 %collective-permute-start.4 = (bf16[256,1024]{1,0:T(8,128)(2,1)}, bf16[256,1024]{1,0:T(8,128)(2,1)S(1)}, u32[]{:S(2)}, u32[]{:S(2)}) collective-permute-start(bf16[256,1024]{1,0:T(8,128)(2,1)} %get-tuple-element.14), channel_id=1, source_target_pairs={{0,256},{128,384},{256,0},{384,128},{1,257},{129,385},{257,1},{385... | collective-permute-start | bytes 1572872 | tf_op jit(solution)/shard_map/ppermute | solution.py:180
  26.9 0.1 stack.35.place.refs_0_
  26.9 0.0 collective-permute-done.h3
  26.9 0.8 slice.8
  27.7 3.4 %collective-permute-start.1 = (bf16[128,1536]{1,0:T(8,128)(2,1)}, bf16[128,1536]{1,0:T(8,128)(2,1)S(1)}, u32[]{:S(2)}, u32[]{:S(2)}) collective-permute-start(bf16[128,1536]{1,0:T(8,128)(2,1)} %slice.8), channel_id=1, source_target_pairs={{0,128},{128,256},{256,384},{384,0},{1,129},{129,257},{257,385},{3... | collective-permute-start | bytes 1179656 | tf_op jit(solution)/shard_map/ppermute | solution.py:180
  31.1 0.0 collective-permute-done.2.h1
  31.2 0.8 slice.9
  32.0 3.1 %collective-permute-start.3 = (bf16[128,1536]{1,0:T(8,128)(2,1)}, bf16[128,1536]{1,0:T(8,128)(2,1)S(1)}, u32[]{:S(2)}, u32[]{:S(2)}) collective-permute-start(bf16[128,1536]{1,0:T(8,128)(2,1)} %slice.9), channel_id=1, source_target_pairs={{0,384},{128,0},{256,128},{384,256},{1,385},{129,1},{257,129},{385... | collective-permute-start | bytes 1179656 | tf_op jit(solution)/shard_map/ppermute | solution.py:180
  35.0 0.0 all-to-all-done
  35.1 0.0 copy-start
  35.1 0.0 copy-start.1
  35.1 15.4 %shard_map.37 = (bf16[2,1536,512]{2,1,0:T(8,128)(2,1)S(1)}, bf16[2,1536,512]{2,1,0:T(8,128)(2,1)S(1)}) custom-call(s32[8]{0:T(128)S(1)} %stack.35.place.refs_0_, s32[16,128]{1,0:T(8,128)S(1)} %bitcast.29), custom_call_target="tpu_custom_call" | custom-call | flops 15728640000 | bytes 6291456 | tf_op jit(solution)/shard_map/pallas_call | solution.py:69
  50.5 0.0 collective-permute-done.5.g1
  50.5 0.0 collective-permute-done.6.g3
  50.5 0.0 copy-done
  50.5 0.0 copy-done.1
  50.5 4.2 %shard_map.38 = (f32[1536,512]{1,0:T(8,128)S(1)}, f32[1536,512]{1,0:T(8,128)S(1)}) custom-call(s32[8]{0:T(128)S(1)} %stack.35.place.refs_0_, bf16[256,1536]{1,0:T(8,128)(2,1)S(1)} %bitcast.28, bf16[256,1536]{1,0:T(8,128)(2,1)S(1)} %collective-permute-done.2.h1, bf16[256,1536]{1,0:T(8,128)(2,1)S(1)} %collective-permute-done.h3, ...), custom_call_target="tpu_custom_call" | custom-call | flops 2415919104 | bytes 4194304 | tf_op jit(solution)/shard_map/pallas_call | solution.py:131
  54.7 0.0 collective-permute-done.4.refs_3_
  54.8 0.0 collective-permute-done.1.refs_1_
  54.8 0.0 collective-permute-done.3.refs_2_
  54.8 1.3 shard_map.40
  56.1 8.0 %collective-permute-start.7 = (bf16[32,96,256]{2,1,0:T(8,128)(2,1)S(1)}, bf16[32,96,256]{2,1,0:T(8,128)(2,1)S(1)}, u32[]{:S(2)}, u32[]{:S(2)}) collective-permute-start(bf16[32,96,256]{2,1,0:T(8,128)(2,1)S(1)} %shard_map.40), channel_id=1, source_target_pairs={{0,1},{1,0},{2,3},{3,2},{4,5},{5,4},{6,7},{7,6},{8,9},{9,8},{10,11... | collective-permute-start | bytes 4718600 | tf_op jit(solution)/shard_map/ppermute | solution.py:209
  64.1 1.3 shard_map.39
  65.3 1.7 %collective-permute-done.7 = bf16[32,96,256]{2,1,0:T(8,128)(2,1)S(1)} collective-permute-done((bf16[32,96,256]{2,1,0:T(8,128)(2,1)S(1)}, bf16[32,96,256]{2,1,0:T(8,128)(2,1)S(1)}, u32[]{:S(2)}, u32[]{:S(2)}) %collective-permute-start.7) | collective-permute-done | bytes 1572896 | tf_op jit(solution)/shard_map/ppermute | solution.py:209
  67.1 0.6 add_convert_fusion
  67.6 26.8 %all_to_all.18 = bf16[32,96,256]{2,1,0:T(8,128)(2,1)S(1)} all-to-all(bf16[32,96,256]{2,1,0:T(8,128)(2,1)S(1)} %add_convert_fusion), channel_id=1, replica_groups=mesh['y'=4,'x'=4,'zh'=4,'z1'=2,'z0'=2,'core'=2] {'y','x','z0'}, dimensions={0} | all-to-all | bytes 3145728 | tf_op jit(solution)/shard_map/all_to_all | solution.py:172
  94.5 0.2 bitcast_reduce_fusion
  94.7 9.6 %all_to_all.19 = bf16[4,96,256]{2,1,0:T(8,128)(2,1)S(1)} all-to-all(bf16[4,96,256]{2,1,0:T(8,128)(2,1)S(1)} %bitcast_reduce_fusion), channel_id=1, replica_groups=mesh['y'=4,'x'=4,'zh'=4,'z1'=2,'z0'=2,'core'=2] {'z1'}, dimensions={0} | all-to-all | bytes 393216 | tf_op jit(solution)/shard_map/all_to_all | solution.py:172
  104.3 24.9 %all-gather = bf16[8,96,256]{2,1,0:T(8,128)(2,1)S(1)} all-gather(bf16[2,96,256]{2,1,0:T(8,128)(2,1)S(1)} %reduce_sum.37), channel_id=2, replica_groups=mesh['y'=4,'x'=4,'zh'=4,'z1'=2,'z0'=2,'core'=2] {'zh'}, dimensions={0}, use_global_device_ids=true | all-gather | bytes 491520 | tf_op jit(solution)/shard_map/all_gather | solution.py:215
  129.3 0.1 reduce_sum.38
  129.3 23.1 %all-gather.1 = bf16[16,96,256]{2,1,0:T(8,128)(2,1)S(1)} all-gather(bf16[2,96,256]{2,1,0:T(8,128)(2,1)S(1)} %reduce_sum.38), channel_id=3, replica_groups=mesh['y'=4,'x'=4,'zh'=4,'z1'=2,'z0'=2,'core'=2] {'z1','z0','core'}, dimensions={0}, use_global_device_ids=true | all-gather | bytes 884736 | tf_op jit(solution)/shard_map/all_gather | solution.py:216
  152.4 1.5 shard_map.41
  (1 shorter events, 0.0 us)
Async XLA Ops:
  0.0 26.9 %collective-permute-start = (bf16[256,1536]{1,0:T(8,128)(2,1)}, bf16[256,1536]{1,0:T(8,128)(2,1)S(1)}, u32[]{:S(2)}, u32[]{:S(2)}) collective-permute-start(bf16[256,1536]{1,0:T(8,128)(2,1)} %bitcast.26), channel_id=1, source_target_pairs={{0,128},{128,256},{256,384},{384,0},{1,129},{129,257},{257,385},{3... | collective-permute-start | bytes 2359304 | tf_op jit(solution)/shard_map/ppermute | solution.py:180
  4.0 27.1 %collective-permute-start.2 = (bf16[256,1536]{1,0:T(8,128)(2,1)}, bf16[256,1536]{1,0:T(8,128)(2,1)S(1)}, u32[]{:S(2)}, u32[]{:S(2)}) collective-permute-start(bf16[256,1536]{1,0:T(8,128)(2,1)} %bitcast.27), channel_id=1, source_target_pairs={{0,384},{128,0},{256,128},{384,256},{1,385},{129,1},{257,129},{385... | collective-permute-start | bytes 2359304 | tf_op jit(solution)/shard_map/ppermute | solution.py:180
  8.8 26.3 %all-to-all-start = ((s32[16,1,128]{2,1,0:T(1,128)}), s32[16,1,128]{2,1,0:T(1,128)S(1)}, u32[]{:S(2)}, u32[]{:S(2)}) async-start(s32[16,1,128]{2,1,0:T(1,128)} %tile.15), calls=%async_computation | async-start | bytes 16384 | tf_op jit(solution)/shard_map/all_to_all | solution.py:172
  16.8 33.7 %collective-permute-start.5 = (bf16[256,1024]{1,0:T(8,128)(2,1)}, bf16[256,1024]{1,0:T(8,128)(2,1)S(1)}, u32[]{:S(2)}, u32[]{:S(2)}) collective-permute-start(bf16[256,1024]{1,0:T(8,128)(2,1)} %get-tuple-element.15), channel_id=1, source_target_pairs={{0,384},{128,0},{256,128},{384,256},{1,385},{129,1},{257,129},{385... | collective-permute-start | bytes 1572872 | tf_op jit(solution)/shard_map/ppermute | solution.py:180
  21.3 29.2 %collective-permute-start.6 = (bf16[256,1024]{1,0:T(8,128)(2,1)}, bf16[256,1024]{1,0:T(8,128)(2,1)}, u32[]{:S(2)}, u32[]{:S(2)}) collective-permute-start(bf16[256,1024]{1,0:T(8,128)(2,1)} %get-tuple-element.13), channel_id=1, source_target_pairs={{0,128},{128,256},{256,384},{384,0},{1,129},{129,257},{257,385},{3... | collective-permute-start | bytes 1572872 | tf_op jit(solution)/shard_map/ppermute | solution.py:180
  23.2 31.6 %collective-permute-start.4 = (bf16[256,1024]{1,0:T(8,128)(2,1)}, bf16[256,1024]{1,0:T(8,128)(2,1)S(1)}, u32[]{:S(2)}, u32[]{:S(2)}) collective-permute-start(bf16[256,1024]{1,0:T(8,128)(2,1)} %get-tuple-element.14), channel_id=1, source_target_pairs={{0,256},{128,384},{256,0},{384,128},{1,257},{129,385},{257,1},{385... | collective-permute-start | bytes 1572872 | tf_op jit(solution)/shard_map/ppermute | solution.py:180
  27.7 27.0 %collective-permute-start.1 = (bf16[128,1536]{1,0:T(8,128)(2,1)}, bf16[128,1536]{1,0:T(8,128)(2,1)S(1)}, u32[]{:S(2)}, u32[]{:S(2)}) collective-permute-start(bf16[128,1536]{1,0:T(8,128)(2,1)} %slice.8), channel_id=1, source_target_pairs={{0,128},{128,256},{256,384},{384,0},{1,129},{129,257},{257,385},{3... | collective-permute-start | bytes 1179656 | tf_op jit(solution)/shard_map/ppermute | solution.py:180
  32.0 22.8 %collective-permute-start.3 = (bf16[128,1536]{1,0:T(8,128)(2,1)}, bf16[128,1536]{1,0:T(8,128)(2,1)S(1)}, u32[]{:S(2)}, u32[]{:S(2)}) collective-permute-start(bf16[128,1536]{1,0:T(8,128)(2,1)} %slice.9), channel_id=1, source_target_pairs={{0,384},{128,0},{256,128},{384,256},{1,385},{129,1},{257,129},{385... | collective-permute-start | bytes 1179656 | tf_op jit(solution)/shard_map/ppermute | solution.py:180
  35.1 15.5 %copy-start = (bf16[1,256,4096]{2,1,0:T(8,128)(2,1)S(1)}, bf16[1,256,4096]{2,1,0:T(8,128)(2,1)}, u32[]{:S(2)}) copy-start(bf16[1,256,4096]{2,1,0:T(8,128)(2,1)} %param.4) | copy-start | bytes 6291460
  35.1 15.5 %copy-start.1 = (bf16[1,256,1536]{2,1,0:T(8,128)(2,1)S(1)}, bf16[1,256,1536]{2,1,0:T(8,128)(2,1)}, u32[]{:S(2)}) copy-start(bf16[1,256,1536]{2,1,0:T(8,128)(2,1)} %param.3) | copy-start | bytes 2359300
  56.1 11.0 %collective-permute-start.7 = (bf16[32,96,256]{2,1,0:T(8,128)(2,1)S(1)}, bf16[32,96,256]{2,1,0:T(8,128)(2,1)S(1)}, u32[]{:S(2)}, u32[]{:S(2)}) collective-permute-start(bf16[32,96,256]{2,1,0:T(8,128)(2,1)S(1)} %shard_map.40), channel_id=1, source_target_pairs={{0,1},{1,0},{2,3},{3,2},{4,5},{5,4},{6,7},{7,6},{8,9},{9,8},{10,11... | collective-permute-start | bytes 4718600 | tf_op jit(solution)/shard_map/ppermute | solution.py:209

commit v9 on v8

--- a/solution.py
+++ b/solution.py
@@ -211,7 +211,10 @@
 
     got = exchange(both.astype(jnp.bfloat16), ("y", "x", "z0"))
     owned = added(got.reshape(SIDE, 2 * SIDE, *got.shape[1:]), 1)
-    near = added(exchange(owned, "z1").reshape(2, 2, *got.shape[1:]))
+    z1 = lax.axis_index("z1")
+    given = lax.dynamic_slice_in_dim(owned, (1 - z1) * 2, 2, 0)
+    kept = lax.dynamic_slice_in_dim(owned, z1 * 2, 2, 0)
+    near = added(jnp.stack([kept, lax.ppermute(given, "z1", SWAP)]))
     total = added(lax.all_gather(near, "zh"))
     return weave(place, lax.all_gather(total, ("z1", "z0", "core")), columns)[None]
 

time: 154 us -> 154 us (level)
  blocking collectives: 84.5 us -> 47.8 us
  waiting for transfers between devices: 1.75 us -> 27.8 us
  starting transfers between devices: 37.3 us -> 46.6 us
    all_to_all x2 -> x0, blocking collectives: 36.4 us -> none  [exchange(): return lax.all_to_all(blocks, axes, 0, 0, tiled=True)]
    all_to_all x1 -> x2, waiting for transfers between devices: 0.01 us -> 22.7 us  [exchange(): return lax.all_to_all(blocks, axes, 0, 0, tiled=True)]
    ppermute x0 -> x1, starting transfers between devices: none -> 4.89 us  [per_device(): near = added(jnp.stack([kept, lax.ppermute(given, 'z1', SWAP)]))]
    all_to_all x1 -> x2, starting transfers between devices: 5.47 us -> 9.92 us  [exchange(): return lax.all_to_all(blocks, axes, 0, 0, tiled=True)]
    ppermute x0 -> x1, waiting for transfers between devices: none -> 3.37 us  [per_device(): near = added(jnp.stack([kept, lax.ppermute(given, 'z1', SWAP)]))]
    all_gather x1, blocking collectives: 23.1 us -> 21.3 us  [per_device(): lax.all_gather(total, ('z1', 'z0', 'core'))]
    all_gather x1, blocking collectives: 24.9 us -> 26.5 us  [per_device(): total = added(lax.all_gather(near, 'zh'))]
  transfers between devices with their start and end apart: 9 -> 11, of which waited for: 1 -> 3; matrix products, arithmetic and copies ran while one was open for 4% -> 4% of each run, Pallas kernels for 14% -> 14%
where the time goes in v9:
time: 154 us
  blocking collectives  47.8 us (31%)
  starting transfers between devices  46.6 us (30%)
  waiting for transfers between devices  27.8 us (18%)
  Pallas kernels  23.7 us (15%)
  local copies, waits for them, and re-layouts  5.54 us (4%)
  other arithmetic  2.02 us (1%)
    all_gather x1, blocking collectives, per_device(): total = added(lax.all_gather(near, 'zh'))  26.5 us
    ppermute x7, starting transfers between devices, along_y(): lax.ppermute(block, 'y', [(at, (at + step) % SIDE) for at in range(SIDE)])  23.8 us
    all_to_all x2, waiting for transfers between devices, exchange(): return lax.all_to_all(blocks, axes, 0, 0, tiled=True)  22.7 us
    all_gather x1, blocking collectives, per_device(): lax.all_gather(total, ('z1', 'z0', 'core'))  21.3 us
    pallas_call x1, Pallas kernels, factors(): pl.pallas_call(factor_kernel, grid_spec=pltpu.PrefetchScalarGridSpec(num_...  15.4 us
    all_to_all x2, starting transfers between devices, exchange(): return lax.all_to_all(blocks, axes, 0, 0, tiled=True)  9.92 us
    pallas_call x4, Pallas kernels, in_vmem(): pl.pallas_call(body, in_specs=[pl.BlockSpec(memory_space=pltpu.SMEM)] + [...  8.29 us
    ppermute x1, starting transfers between devices, per_device(): received = lax.ppermute(sent, 'core', SWAP)  7.96 us
  transfers between devices with their start and end apart: 11, of which 3 were waited for; matrix products, arithmetic and copies ran while one was open for 4% of the time, Pallas kernels for 14%

profile of v9, /device:TPU:1, one launch (start us, length us, event | category | flops | bytes accessed | tf_op | source)
XLA Modules:
  0.0 153.8 jit_solution(16479735744659094599)
XLA Ops:
  0.0 4.0 %collective-permute-start = (bf16[256,1536]{1,0:T(8,128)(2,1)}, bf16[256,1536]{1,0:T(8,128)(2,1)S(1)}, u32[]{:S(2)}, u32[]{:S(2)}) collective-permute-start(bf16[256,1536]{1,0:T(8,128)(2,1)} %bitcast.25), channel_id=1, source_target_pairs={{0,128},{128,256},{256,384},{384,0},{1,129},{129,257},{257,385},{3... | collective-permute-start | bytes 2359304 | tf_op jit(solution)/shard_map/ppermute | solution.py:180
  4.0 3.4 %collective-permute-start.2 = (bf16[256,1536]{1,0:T(8,128)(2,1)}, bf16[256,1536]{1,0:T(8,128)(2,1)S(1)}, u32[]{:S(2)}, u32[]{:S(2)}) collective-permute-start(bf16[256,1536]{1,0:T(8,128)(2,1)} %bitcast.26), channel_id=1, source_target_pairs={{0,384},{128,0},{256,128},{384,256},{1,385},{129,1},{257,129},{385... | collective-permute-start | bytes 2359304 | tf_op jit(solution)/shard_map/ppermute | solution.py:180
  7.4 0.7 tile.13
  8.1 0.1 tile.14
  8.1 0.6 tile.15
  8.7 5.5 %all-to-all-start = ((s32[16,1,128]{2,1,0:T(1,128)}), s32[16,1,128]{2,1,0:T(1,128)S(1)}, u32[]{:S(2)}, u32[]{:S(2)}) async-start(s32[16,1,128]{2,1,0:T(1,128)} %tile.15), calls=%async_computation | async-start | bytes 16384 | tf_op jit(solution)/shard_map/all_to_all | solution.py:172
  14.3 2.5 %dynamic-slice_bitcast_fusion = (bf16[256,1024]{1,0:T(8,128)(2,1)}, bf16[256,1024]{1,0:T(8,128)(2,1)}, bf16[256,1024]{1,0:T(8,128)(2,1)}) fusion(bf16[1,256,4096]{2,1,0:T(8,128)(2,1)} %param.4, s32[]{:T(128)S(6)} %select_n.35, s32[]{:T(128)S(6)} %select_n.31, s32[]{:T(128)S(6)} %select_n.33), kind=kLoop, calls=%fused_computation.2 | loop fusion | bytes 3145740 | tf_op jit(solution)/shard_map/dynamic_slice | solution.py:200
  16.8 4.4 %collective-permute-start.5 = (bf16[256,1024]{1,0:T(8,128)(2,1)}, bf16[256,1024]{1,0:T(8,128)(2,1)S(1)}, u32[]{:S(2)}, u32[]{:S(2)}) collective-permute-start(bf16[256,1024]{1,0:T(8,128)(2,1)} %get-tuple-element.15), channel_id=1, source_target_pairs={{0,384},{128,0},{256,128},{384,256},{1,385},{129,1},{257,129},{385... | collective-permute-start | bytes 1572872 | tf_op jit(solution)/shard_map/ppermute | solution.py:180
  21.3 1.9 %collective-permute-start.6 = (bf16[256,1024]{1,0:T(8,128)(2,1)}, bf16[256,1024]{1,0:T(8,128)(2,1)}, u32[]{:S(2)}, u32[]{:S(2)}) collective-permute-start(bf16[256,1024]{1,0:T(8,128)(2,1)} %get-tuple-element.13), channel_id=1, source_target_pairs={{0,128},{128,256},{256,384},{384,0},{1,129},{129,257},{257,385},{3... | collective-permute-start | bytes 1572872 | tf_op jit(solution)/shard_map/ppermute | solution.py:180
  23.2 3.7 %collective-permute-start.4 = (bf16[256,1024]{1,0:T(8,128)(2,1)}, bf16[256,1024]{1,0:T(8,128)(2,1)S(1)}, u32[]{:S(2)}, u32[]{:S(2)}) collective-permute-start(bf16[256,1024]{1,0:T(8,128)(2,1)} %get-tuple-element.14), channel_id=1, source_target_pairs={{0,256},{128,384},{256,0},{384,128},{1,257},{129,385},{257,1},{385... | collective-permute-start | bytes 1572872 | tf_op jit(solution)/shard_map/ppermute | solution.py:180
  26.9 0.1 stack.38.place.refs_0_
  26.9 0.0 collective-permute-done.h3
  26.9 0.8 slice.8
  27.7 3.4 %collective-permute-start.1 = (bf16[128,1536]{1,0:T(8,128)(2,1)}, bf16[128,1536]{1,0:T(8,128)(2,1)S(1)}, u32[]{:S(2)}, u32[]{:S(2)}) collective-permute-start(bf16[128,1536]{1,0:T(8,128)(2,1)} %slice.8), channel_id=1, source_target_pairs={{0,128},{128,256},{256,384},{384,0},{1,129},{129,257},{257,385},{3... | collective-permute-start | bytes 1179656 | tf_op jit(solution)/shard_map/ppermute | solution.py:180
  31.1 0.0 collective-permute-done.2.h1
  31.1 0.8 slice.9
  31.9 3.1 %collective-permute-start.3 = (bf16[128,1536]{1,0:T(8,128)(2,1)}, bf16[128,1536]{1,0:T(8,128)(2,1)S(1)}, u32[]{:S(2)}, u32[]{:S(2)}) collective-permute-start(bf16[128,1536]{1,0:T(8,128)(2,1)} %slice.9), channel_id=1, source_target_pairs={{0,384},{128,0},{256,128},{384,256},{1,385},{129,1},{257,129},{385... | collective-permute-start | bytes 1179656 | tf_op jit(solution)/shard_map/ppermute | solution.py:180
  35.0 0.0 all-to-all-done
  35.0 0.0 copy-start
  35.0 0.0 copy-start.1
  35.0 15.4 %shard_map.37 = (bf16[2,1536,512]{2,1,0:T(8,128)(2,1)S(1)}, bf16[2,1536,512]{2,1,0:T(8,128)(2,1)S(1)}) custom-call(s32[8]{0:T(128)S(1)} %stack.38.place.refs_0_, s32[16,128]{1,0:T(8,128)S(1)} %bitcast.28), custom_call_target="tpu_custom_call" | custom-call | flops 15728640000 | bytes 6291456 | tf_op jit(solution)/shard_map/pallas_call | solution.py:69
  50.4 0.0 collective-permute-done.5.g1
  50.4 0.0 collective-permute-done.6.g3
  50.4 0.0 copy-done
  50.5 0.0 copy-done.1
  50.5 4.2 %shard_map.38 = (f32[1536,512]{1,0:T(8,128)S(1)}, f32[1536,512]{1,0:T(8,128)S(1)}) custom-call(s32[8]{0:T(128)S(1)} %stack.38.place.refs_0_, bf16[256,1536]{1,0:T(8,128)(2,1)S(1)} %bitcast.27, bf16[256,1536]{1,0:T(8,128)(2,1)S(1)} %collective-permute-done.2.h1, bf16[256,1536]{1,0:T(8,128)(2,1)S(1)} %collective-permute-done.h3, ...), custom_call_target="tpu_custom_call" | custom-call | flops 2415919104 | bytes 4194304 | tf_op jit(solution)/shard_map/pallas_call | solution.py:131
  54.7 0.0 collective-permute-done.4.refs_3_
  54.7 0.0 collective-permute-done.1.refs_1_
  54.7 0.0 collective-permute-done.3.refs_2_
  54.7 1.3 shard_map.40
  56.0 8.0 %collective-permute-start.7 = (bf16[32,96,256]{2,1,0:T(8,128)(2,1)S(1)}, bf16[32,96,256]{2,1,0:T(8,128)(2,1)S(1)}, u32[]{:S(2)}, u32[]{:S(2)}) collective-permute-start(bf16[32,96,256]{2,1,0:T(8,128)(2,1)S(1)} %shard_map.40), channel_id=1, source_target_pairs={{0,1},{1,0},{2,3},{3,2},{4,5},{5,4},{6,7},{7,6},{8,9},{9,8},{10,11... | collective-permute-start | bytes 4718600 | tf_op jit(solution)/shard_map/ppermute | solution.py:209
  64.0 1.3 shard_map.39
  65.3 1.7 %collective-permute-done.7 = bf16[32,96,256]{2,1,0:T(8,128)(2,1)S(1)} collective-permute-done((bf16[32,96,256]{2,1,0:T(8,128)(2,1)S(1)}, bf16[32,96,256]{2,1,0:T(8,128)(2,1)S(1)}, u32[]{:S(2)}, u32[]{:S(2)}) %collective-permute-start.7) | collective-permute-done | bytes 1572896 | tf_op jit(solution)/shard_map/ppermute | solution.py:209
  67.0 1.7 %add_convert_fusion = bf16[32,96,256]{2,1,0:T(8,128)(2,1)} fusion(bf16[32,96,256]{2,1,0:T(8,128)(2,1)S(1)} %collective-permute-done.7, bf16[32,96,256]{2,1,0:T(8,128)(2,1)S(1)} %shard_map.39), kind=kLoop, calls=%fused_computation | loop fusion | flops 3145728 | bytes 4718592 | tf_op jit(solution)/shard_map/convert_element_type | solution.py:212
  68.7 4.4 %all-to-all-start.1 = ((bf16[32,96,256]{2,1,0:T(8,128)(2,1)}), bf16[32,96,256]{2,1,0:T(8,128)(2,1)S(1)}, u32[]{:S(2)}, u32[]{:S(2)}) async-start(bf16[32,96,256]{2,1,0:T(8,128)(2,1)} %add_convert_fusion), calls=%async_computation.1 | async-start | bytes 3145728 | tf_op jit(solution)/shard_map/all_to_all | solution.py:172
  73.2 22.7 %all-to-all-done.1 = bf16[32,96,256]{2,1,0:T(8,128)(2,1)S(1)} async-done(((bf16[32,96,256]{2,1,0:T(8,128)(2,1)}), bf16[32,96,256]{2,1,0:T(8,128)(2,1)S(1)}, u32[]{:S(2)}, u32[]{:S(2)}) %all-to-all-start.1) | async-done | bytes 1572896 | tf_op jit(solution)/shard_map/all_to_all | solution.py:172
  95.9 0.2 bitcast_reduce_fusion
  96.1 4.9 %collective-permute-start.8 = (bf16[2,96,256]{2,1,0:T(8,128)(2,1)S(1)}, bf16[2,96,256]{2,1,0:T(8,128)(2,1)S(1)}, u32[]{:S(2)}, u32[]{:S(2)}) collective-permute-start(bf16[2,96,256]{2,1,0:T(8,128)(2,1)S(1)} %constant_dynamic-slice_fusion), channel_id=1, source_target_pairs={{0,4},{4,0},{1,5},{5,1},{2,6},{6,2},{3,7},{7,3},{8,12},{12,8},{9,1... | collective-permute-start | bytes 294920 | tf_op jit(solution)/shard_map/ppermute | solution.py:217
  101.0 3.4 %collective-permute-done.8 = bf16[2,96,256]{2,1,0:T(8,128)(2,1)S(1)} collective-permute-done((bf16[2,96,256]{2,1,0:T(8,128)(2,1)S(1)}, bf16[2,96,256]{2,1,0:T(8,128)(2,1)S(1)}, u32[]{:S(2)}, u32[]{:S(2)}) %collective-permute-start.8) | collective-permute-done | bytes 98336 | tf_op jit(solution)/shard_map/ppermute | solution.py:217
  104.4 26.5 %all-gather = bf16[8,96,256]{2,1,0:T(8,128)(2,1)S(1)} all-gather(bf16[2,96,256]{2,1,0:T(8,128)(2,1)S(1)} %dynamic-slice_add_fusion), channel_id=2, replica_groups=mesh['y'=4,'x'=4,'zh'=4,'z1'=2,'z0'=2,'core'=2] {'zh'}, dimensions={0}, use_global_device_ids=true | all-gather | bytes 491520 | tf_op jit(solution)/shard_map/all_gather | solution.py:218
  130.9 0.1 reduce_sum.36
  131.0 21.3 %all-gather.1 = bf16[16,96,256]{2,1,0:T(8,128)(2,1)S(1)} all-gather(bf16[2,96,256]{2,1,0:T(8,128)(2,1)S(1)} %reduce_sum.36), channel_id=3, replica_groups=mesh['y'=4,'x'=4,'zh'=4,'z1'=2,'z0'=2,'core'=2] {'z1','z0','core'}, dimensions={0}, use_global_device_ids=true | all-gather | bytes 884736 | tf_op jit(solution)/shard_map/all_gather | solution.py:219
  152.3 1.5 shard_map.41
  (2 shorter events, 0.0 us)
Async XLA Ops:
  0.0 26.9 %collective-permute-start = (bf16[256,1536]{1,0:T(8,128)(2,1)}, bf16[256,1536]{1,0:T(8,128)(2,1)S(1)}, u32[]{:S(2)}, u32[]{:S(2)}) collective-permute-start(bf16[256,1536]{1,0:T(8,128)(2,1)} %bitcast.25), channel_id=1, source_target_pairs={{0,128},{128,256},{256,384},{384,0},{1,129},{129,257},{257,385},{3... | collective-permute-start | bytes 2359304 | tf_op jit(solution)/shard_map/ppermute | solution.py:180
  4.0 27.1 %collective-permute-start.2 = (bf16[256,1536]{1,0:T(8,128)(2,1)}, bf16[256,1536]{1,0:T(8,128)(2,1)S(1)}, u32[]{:S(2)}, u32[]{:S(2)}) collective-permute-start(bf16[256,1536]{1,0:T(8,128)(2,1)} %bitcast.26), channel_id=1, source_target_pairs={{0,384},{128,0},{256,128},{384,256},{1,385},{129,1},{257,129},{385... | collective-permute-start | bytes 2359304 | tf_op jit(solution)/shard_map/ppermute | solution.py:180
  8.7 26.2 %all-to-all-start = ((s32[16,1,128]{2,1,0:T(1,128)}), s32[16,1,128]{2,1,0:T(1,128)S(1)}, u32[]{:S(2)}, u32[]{:S(2)}) async-start(s32[16,1,128]{2,1,0:T(1,128)} %tile.15), calls=%async_computation | async-start | bytes 16384 | tf_op jit(solution)/shard_map/all_to_all | solution.py:172
  16.8 33.6 %collective-permute-start.5 = (bf16[256,1024]{1,0:T(8,128)(2,1)}, bf16[256,1024]{1,0:T(8,128)(2,1)S(1)}, u32[]{:S(2)}, u32[]{:S(2)}) collective-permute-start(bf16[256,1024]{1,0:T(8,128)(2,1)} %get-tuple-element.15), channel_id=1, source_target_pairs={{0,384},{128,0},{256,128},{384,256},{1,385},{129,1},{257,129},{385... | collective-permute-start | bytes 1572872 | tf_op jit(solution)/shard_map/ppermute | solution.py:180
  21.3 29.2 %collective-permute-start.6 = (bf16[256,1024]{1,0:T(8,128)(2,1)}, bf16[256,1024]{1,0:T(8,128)(2,1)}, u32[]{:S(2)}, u32[]{:S(2)}) collective-permute-start(bf16[256,1024]{1,0:T(8,128)(2,1)} %get-tuple-element.13), channel_id=1, source_target_pairs={{0,128},{128,256},{256,384},{384,0},{1,129},{129,257},{257,385},{3... | collective-permute-start | bytes 1572872 | tf_op jit(solution)/shard_map/ppermute | solution.py:180
  23.2 31.5 %collective-permute-start.4 = (bf16[256,1024]{1,0:T(8,128)(2,1)}, bf16[256,1024]{1,0:T(8,128)(2,1)S(1)}, u32[]{:S(2)}, u32[]{:S(2)}) collective-permute-start(bf16[256,1024]{1,0:T(8,128)(2,1)} %get-tuple-element.14), channel_id=1, source_target_pairs={{0,256},{128,384},{256,0},{384,128},{1,257},{129,385},{257,1},{385... | collective-permute-start | bytes 1572872 | tf_op jit(solution)/shard_map/ppermute | solution.py:180
  27.7 27.0 %collective-permute-start.1 = (bf16[128,1536]{1,0:T(8,128)(2,1)}, bf16[128,1536]{1,0:T(8,128)(2,1)S(1)}, u32[]{:S(2)}, u32[]{:S(2)}) collective-permute-start(bf16[128,1536]{1,0:T(8,128)(2,1)} %slice.8), channel_id=1, source_target_pairs={{0,128},{128,256},{256,384},{384,0},{1,129},{129,257},{257,385},{3... | collective-permute-start | bytes 1179656 | tf_op jit(solution)/shard_map/ppermute | solution.py:180
  31.9 22.8 %collective-permute-start.3 = (bf16[128,1536]{1,0:T(8,128)(2,1)}, bf16[128,1536]{1,0:T(8,128)(2,1)S(1)}, u32[]{:S(2)}, u32[]{:S(2)}) collective-permute-start(bf16[128,1536]{1,0:T(8,128)(2,1)} %slice.9), channel_id=1, source_target_pairs={{0,384},{128,0},{256,128},{384,256},{1,385},{129,1},{257,129},{385... | collective-permute-start | bytes 1179656 | tf_op jit(solution)/shard_map/ppermute | solution.py:180
  35.0 15.5 %copy-start = (bf16[1,256,4096]{2,1,0:T(8,128)(2,1)S(1)}, bf16[1,256,4096]{2,1,0:T(8,128)(2,1)}, u32[]{:S(2)}) copy-start(bf16[1,256,4096]{2,1,0:T(8,128)(2,1)} %param.4) | copy-start | bytes 6291460
  35.0 15.5 %copy-start.1 = (bf16[1,256,1536]{2,1,0:T(8,128)(2,1)S(1)}, bf16[1,256,1536]{2,1,0:T(8,128)(2,1)}, u32[]{:S(2)}) copy-start(bf16[1,256,1536]{2,1,0:T(8,128)(2,1)} %param.3) | copy-start | bytes 2359300
  56.0 11.0 %collective-permute-start.7 = (bf16[32,96,256]{2,1,0:T(8,128)(2,1)S(1)}, bf16[32,96,256]{2,1,0:T(8,128)(2,1)S(1)}, u32[]{:S(2)}, u32[]{:S(2)}) collective-permute-start(bf16[32,96,256]{2,1,0:T(8,128)(2,1)S(1)} %shard_map.40), channel_id=1, source_target_pairs={{0,1},{1,0},{2,3},{3,2},{4,5},{5,4},{6,7},{7,6},{8,9},{9,8},{10,11... | collective-permute-start | bytes 4718600 | tf_op jit(solution)/shard_map/ppermute | solution.py:209
  68.7 27.2 %all-to-all-start.1 = ((bf16[32,96,256]{2,1,0:T(8,128)(2,1)}), bf16[32,96,256]{2,1,0:T(8,128)(2,1)S(1)}, u32[]{:S(2)}, u32[]{:S(2)}) async-start(bf16[32,96,256]{2,1,0:T(8,128)(2,1)} %add_convert_fusion), calls=%async_computation.1 | async-start | bytes 3145728 | tf_op jit(solution)/shard_map/all_to_all | solution.py:172
  96.1 8.3 %collective-permute-start.8 = (bf16[2,96,256]{2,1,0:T(8,128)(2,1)S(1)}, bf16[2,96,256]{2,1,0:T(8,128)(2,1)S(1)}, u32[]{:S(2)}, u32[]{:S(2)}) collective-permute-start(bf16[2,96,256]{2,1,0:T(8,128)(2,1)S(1)} %constant_dynamic-slice_fusion), channel_id=1, source_target_pairs={{0,4},{4,0},{1,5},{5,1},{2,6},{6,2},{3,7},{7,3},{8,12},{12,8},{9,1... | collective-permute-start | bytes 294920 | tf_op jit(solution)/shard_map/ppermute | solution.py:217

commit v10 on v8

--- a/solution.py
+++ b/solution.py
@@ -168,6 +168,21 @@
     return in_vmem(weave_kernel, place, [blocks], shape, 1)
 
 
+def spread_kernel(seeds_ref, out_ref):
+    row = jnp.concatenate([seeds_ref[...]] * (128 // seeds_ref.shape[1]), axis=1)
+    out_ref[...] = jnp.broadcast_to(row, out_ref.shape)
+
+
+def spread(seeds):
+    return pl.pallas_call(
+        spread_kernel,
+        in_specs=[pl.BlockSpec(memory_space=pltpu.VMEM)],
+        out_specs=pl.BlockSpec(memory_space=pltpu.VMEM),
+        out_shape=jax.ShapeDtypeStruct((OWNERS, 128), seeds.dtype),
+        compiler_params=pltpu.CompilerParams(vmem_limit_bytes=2**20),
+    )(seeds)
+
+
 def exchange(blocks, axes):
     return lax.all_to_all(blocks, axes, 0, 0, tiled=True)
 
@@ -185,7 +200,7 @@
     tokens, columns = grad_out.shape[1:]
     quarter = columns // SIDE
     half = quarter // 2
-    words = exchange(jnp.tile(seed_table[0, 0], (OWNERS, 4)), ("y", "x"))
+    words = exchange(spread(seed_table[0, 0]), ("y", "x"))
     other = 1 - core
     groups = half // 32
     place = [x, y, (y * 2 + other) * groups, (y * 2 + core) * groups, y * 2 + other, y * 2 + core, other, core]

time: 154 us -> 154 us (level)
  transfers between devices with their start and end apart: 9 -> 9, of which waited for: 1 -> 1; matrix products, arithmetic and copies ran while one was open for 4% -> 3% of each run, Pallas kernels for 14% -> 14%
where the time goes in v10:
time: 154 us
  blocking collectives  84.5 us (55%)
  starting transfers between devices  37.3 us (24%)
  Pallas kernels  24.4 us (16%)
  local copies, waits for them, and re-layouts  4.86 us (3%)
  waiting for transfers between devices  1.75 us (1%)
    all_to_all x2, blocking collectives, exchange(): return lax.all_to_all(blocks, axes, 0, 0, tiled=True)  36.5 us
    all_gather x1, blocking collectives, per_device(): total = added(lax.all_gather(near, 'zh'))  24.9 us
    ppermute x7, starting transfers between devices, along_y(): lax.ppermute(block, 'y', [(at, (at + step) % SIDE) for at in range(SIDE)])  23.8 us
    all_gather x1, blocking collectives, per_device(): lax.all_gather(total, ('z1', 'z0', 'core'))  23.1 us
    pallas_call x1, Pallas kernels, factors(): pl.pallas_call(factor_kernel, grid_spec=pltpu.PrefetchScalarGridSpec(num_...  15.4 us
    pallas_call x4, Pallas kernels, in_vmem(): pl.pallas_call(body, in_specs=[pl.BlockSpec(memory_space=pltpu.SMEM)] + [...  8.29 us
    ppermute x1, starting transfers between devices, per_device(): received = lax.ppermute(sent, 'core', SWAP)  8.01 us
    all_to_all x1, starting transfers between devices, exchange(): return lax.all_to_all(blocks, axes, 0, 0, tiled=True)  5.47 us
  transfers between devices with their start and end apart: 9, of which 1 were waited for; matrix products, arithmetic and copies ran while one was open for 3% of the time, Pallas kernels for 14%

profile of v10, /device:TPU:1, one launch (start us, length us, event | category | flops | bytes accessed | tf_op | source)
XLA Modules:
  0.0 154.0 jit_solution(11610051673813112196)
XLA Ops:
  0.0 4.0 %collective-permute-start = (bf16[256,1536]{1,0:T(8,128)(2,1)}, bf16[256,1536]{1,0:T(8,128)(2,1)S(1)}, u32[]{:S(2)}, u32[]{:S(2)}) collective-permute-start(bf16[256,1536]{1,0:T(8,128)(2,1)} %bitcast.29), channel_id=1, source_target_pairs={{0,128},{128,256},{256,384},{384,0},{1,129},{129,257},{257,385},{3... | collective-permute-start | bytes 2359304 | tf_op jit(solution)/shard_map/ppermute | solution.py:195
  4.0 3.4 %collective-permute-start.2 = (bf16[256,1536]{1,0:T(8,128)(2,1)}, bf16[256,1536]{1,0:T(8,128)(2,1)S(1)}, u32[]{:S(2)}, u32[]{:S(2)}) collective-permute-start(bf16[256,1536]{1,0:T(8,128)(2,1)} %bitcast.30), channel_id=1, source_target_pairs={{0,384},{128,0},{256,128},{384,256},{1,385},{129,1},{257,129},{385... | collective-permute-start | bytes 2359304 | tf_op jit(solution)/shard_map/ppermute | solution.py:195
  7.4 0.0 copy-start.2
  7.4 0.6 copy-done.2
  8.1 0.7 shard_map.37
  8.7 5.5 %all-to-all-start = ((s32[16,1,128]{2,1,0:T(1,128)}), s32[16,1,128]{2,1,0:T(1,128)S(1)}, u32[]{:S(2)}, u32[]{:S(2)}) async-start(s32[16,1,128]{2,1,0:T(1,128)} %bitcast.12), calls=%async_computation | async-start | bytes 16384 | tf_op jit(solution)/shard_map/all_to_all | solution.py:187
  14.3 2.5 %dynamic-slice_bitcast_fusion = (bf16[256,1024]{1,0:T(8,128)(2,1)}, bf16[256,1024]{1,0:T(8,128)(2,1)}, bf16[256,1024]{1,0:T(8,128)(2,1)}) fusion(bf16[1,256,4096]{2,1,0:T(8,128)(2,1)} %param.4, s32[]{:T(128)S(6)} %select_n.29, s32[]{:T(128)S(6)} %select_n.25, s32[]{:T(128)S(6)} %select_n.27), kind=kLoop, calls=%fused_computation.2 | loop fusion | bytes 3145740 | tf_op jit(solution)/shard_map/dynamic_slice | solution.py:215
  16.8 4.4 %collective-permute-start.5 = (bf16[256,1024]{1,0:T(8,128)(2,1)}, bf16[256,1024]{1,0:T(8,128)(2,1)S(1)}, u32[]{:S(2)}, u32[]{:S(2)}) collective-permute-start(bf16[256,1024]{1,0:T(8,128)(2,1)} %get-tuple-element.15), channel_id=1, source_target_pairs={{0,384},{128,0},{256,128},{384,256},{1,385},{129,1},{257,129},{385... | collective-permute-start | bytes 1572872 | tf_op jit(solution)/shard_map/ppermute | solution.py:195
  21.2 1.9 %collective-permute-start.6 = (bf16[256,1024]{1,0:T(8,128)(2,1)}, bf16[256,1024]{1,0:T(8,128)(2,1)}, u32[]{:S(2)}, u32[]{:S(2)}) collective-permute-start(bf16[256,1024]{1,0:T(8,128)(2,1)} %get-tuple-element.13), channel_id=1, source_target_pairs={{0,128},{128,256},{256,384},{384,0},{1,129},{129,257},{257,385},{3... | collective-permute-start | bytes 1572872 | tf_op jit(solution)/shard_map/ppermute | solution.py:195
  23.2 3.7 %collective-permute-start.4 = (bf16[256,1024]{1,0:T(8,128)(2,1)}, bf16[256,1024]{1,0:T(8,128)(2,1)S(1)}, u32[]{:S(2)}, u32[]{:S(2)}) collective-permute-start(bf16[256,1024]{1,0:T(8,128)(2,1)} %get-tuple-element.14), channel_id=1, source_target_pairs={{0,256},{128,384},{256,0},{384,128},{1,257},{129,385},{257,1},{385... | collective-permute-start | bytes 1572872 | tf_op jit(solution)/shard_map/ppermute | solution.py:195
  26.8 0.1 stack.35.place.refs_0_
  26.9 0.0 collective-permute-done.h3
  26.9 0.8 slice.8
  27.7 3.4 %collective-permute-start.1 = (bf16[128,1536]{1,0:T(8,128)(2,1)}, bf16[128,1536]{1,0:T(8,128)(2,1)S(1)}, u32[]{:S(2)}, u32[]{:S(2)}) collective-permute-start(bf16[128,1536]{1,0:T(8,128)(2,1)} %slice.8), channel_id=1, source_target_pairs={{0,128},{128,256},{256,384},{384,0},{1,129},{129,257},{257,385},{3... | collective-permute-start | bytes 1179656 | tf_op jit(solution)/shard_map/ppermute | solution.py:195
  31.1 0.0 collective-permute-done.2.h1
  31.1 0.8 slice.9
  31.9 3.1 %collective-permute-start.3 = (bf16[128,1536]{1,0:T(8,128)(2,1)}, bf16[128,1536]{1,0:T(8,128)(2,1)S(1)}, u32[]{:S(2)}, u32[]{:S(2)}) collective-permute-start(bf16[128,1536]{1,0:T(8,128)(2,1)} %slice.9), channel_id=1, source_target_pairs={{0,384},{128,0},{256,128},{384,256},{1,385},{129,1},{257,129},{385... | collective-permute-start | bytes 1179656 | tf_op jit(solution)/shard_map/ppermute | solution.py:195
  35.0 0.0 all-to-all-done
  35.0 0.0 copy-start
  35.0 0.0 copy-start.1
  35.0 15.4 %shard_map.38 = (bf16[2,1536,512]{2,1,0:T(8,128)(2,1)S(1)}, bf16[2,1536,512]{2,1,0:T(8,128)(2,1)S(1)}) custom-call(s32[8]{0:T(128)S(1)} %stack.35.place.refs_0_, s32[16,128]{1,0:T(8,128)S(1)} %bitcast.32), custom_call_target="tpu_custom_call" | custom-call | flops 15728640000 | bytes 6291456 | tf_op jit(solution)/shard_map/pallas_call | solution.py:69
  50.4 0.0 collective-permute-done.5.g1
  50.4 0.0 collective-permute-done.6.g3
  50.5 0.0 copy-done
  50.5 0.0 copy-done.1
  50.5 4.2 %shard_map.39 = (f32[1536,512]{1,0:T(8,128)S(1)}, f32[1536,512]{1,0:T(8,128)S(1)}) custom-call(s32[8]{0:T(128)S(1)} %stack.35.place.refs_0_, bf16[256,1536]{1,0:T(8,128)(2,1)S(1)} %bitcast.31, bf16[256,1536]{1,0:T(8,128)(2,1)S(1)} %collective-permute-done.2.h1, bf16[256,1536]{1,0:T(8,128)(2,1)S(1)} %collective-permute-done.h3, ...), custom_call_target="tpu_custom_call" | custom-call | flops 2415919104 | bytes 4194304 | tf_op jit(solution)/shard_map/pallas_call | solution.py:131
  54.7 0.0 collective-permute-done.4.refs_3_
  54.7 0.0 collective-permute-done.1.refs_1_
  54.7 0.0 collective-permute-done.3.refs_2_
  54.7 1.3 shard_map.41
  56.0 8.0 %collective-permute-start.7 = (bf16[32,96,256]{2,1,0:T(8,128)(2,1)S(1)}, bf16[32,96,256]{2,1,0:T(8,128)(2,1)S(1)}, u32[]{:S(2)}, u32[]{:S(2)}) collective-permute-start(bf16[32,96,256]{2,1,0:T(8,128)(2,1)S(1)} %shard_map.41), channel_id=1, source_target_pairs={{0,1},{1,0},{2,3},{3,2},{4,5},{5,4},{6,7},{7,6},{8,9},{9,8},{10,11... | collective-permute-start | bytes 4718600 | tf_op jit(solution)/shard_map/ppermute | solution.py:224
  64.0 1.3 shard_map.40
  65.3 1.7 %collective-permute-done.7 = bf16[32,96,256]{2,1,0:T(8,128)(2,1)S(1)} collective-permute-done((bf16[32,96,256]{2,1,0:T(8,128)(2,1)S(1)}, bf16[32,96,256]{2,1,0:T(8,128)(2,1)S(1)}, u32[]{:S(2)}, u32[]{:S(2)}) %collective-permute-start.7) | collective-permute-done | bytes 1572896 | tf_op jit(solution)/shard_map/ppermute | solution.py:224
  67.1 0.6 add_convert_fusion
  67.6 26.8 %all_to_all.21 = bf16[32,96,256]{2,1,0:T(8,128)(2,1)S(1)} all-to-all(bf16[32,96,256]{2,1,0:T(8,128)(2,1)S(1)} %add_convert_fusion), channel_id=1, replica_groups=mesh['y'=4,'x'=4,'zh'=4,'z1'=2,'z0'=2,'core'=2] {'y','x','z0'}, dimensions={0} | all-to-all | bytes 3145728 | tf_op jit(solution)/shard_map/all_to_all | solution.py:187
  94.5 0.2 bitcast_reduce_fusion
  94.7 9.6 %all_to_all.22 = bf16[4,96,256]{2,1,0:T(8,128)(2,1)S(1)} all-to-all(bf16[4,96,256]{2,1,0:T(8,128)(2,1)S(1)} %bitcast_reduce_fusion), channel_id=1, replica_groups=mesh['y'=4,'x'=4,'zh'=4,'z1'=2,'z0'=2,'core'=2] {'z1'}, dimensions={0} | all-to-all | bytes 393216 | tf_op jit(solution)/shard_map/all_to_all | solution.py:187
  104.3 24.9 %all-gather = bf16[8,96,256]{2,1,0:T(8,128)(2,1)S(1)} all-gather(bf16[2,96,256]{2,1,0:T(8,128)(2,1)S(1)} %reduce_sum.37), channel_id=2, replica_groups=mesh['y'=4,'x'=4,'zh'=4,'z1'=2,'z0'=2,'core'=2] {'zh'}, dimensions={0}, use_global_device_ids=true | all-gather | bytes 491520 | tf_op jit(solution)/shard_map/all_gather | solution.py:230
  129.3 0.1 reduce_sum.38
  129.3 23.1 %all-gather.1 = bf16[16,96,256]{2,1,0:T(8,128)(2,1)S(1)} all-gather(bf16[2,96,256]{2,1,0:T(8,128)(2,1)S(1)} %reduce_sum.38), channel_id=3, replica_groups=mesh['y'=4,'x'=4,'zh'=4,'z1'=2,'z0'=2,'core'=2] {'z1','z0','core'}, dimensions={0}, use_global_device_ids=true | all-gather | bytes 884736 | tf_op jit(solution)/shard_map/all_gather | solution.py:231
  152.4 1.5 shard_map.42
  (1 shorter events, 0.0 us)
Async XLA Ops:
  0.0 26.9 %collective-permute-start = (bf16[256,1536]{1,0:T(8,128)(2,1)}, bf16[256,1536]{1,0:T(8,128)(2,1)S(1)}, u32[]{:S(2)}, u32[]{:S(2)}) collective-permute-start(bf16[256,1536]{1,0:T(8,128)(2,1)} %bitcast.29), channel_id=1, source_target_pairs={{0,128},{128,256},{256,384},{384,0},{1,129},{129,257},{257,385},{3... | collective-permute-start | bytes 2359304 | tf_op jit(solution)/shard_map/ppermute | solution.py:195
  4.0 27.1 %collective-permute-start.2 = (bf16[256,1536]{1,0:T(8,128)(2,1)}, bf16[256,1536]{1,0:T(8,128)(2,1)S(1)}, u32[]{:S(2)}, u32[]{:S(2)}) collective-permute-start(bf16[256,1536]{1,0:T(8,128)(2,1)} %bitcast.30), channel_id=1, source_target_pairs={{0,384},{128,0},{256,128},{384,256},{1,385},{129,1},{257,129},{385... | collective-permute-start | bytes 2359304 | tf_op jit(solution)/shard_map/ppermute | solution.py:195
  7.4 0.7 copy-start.2
  8.7 26.3 %all-to-all-start = ((s32[16,1,128]{2,1,0:T(1,128)}), s32[16,1,128]{2,1,0:T(1,128)S(1)}, u32[]{:S(2)}, u32[]{:S(2)}) async-start(s32[16,1,128]{2,1,0:T(1,128)} %bitcast.12), calls=%async_computation | async-start | bytes 16384 | tf_op jit(solution)/shard_map/all_to_all | solution.py:187
  16.8 33.6 %collective-permute-start.5 = (bf16[256,1024]{1,0:T(8,128)(2,1)}, bf16[256,1024]{1,0:T(8,128)(2,1)S(1)}, u32[]{:S(2)}, u32[]{:S(2)}) collective-permute-start(bf16[256,1024]{1,0:T(8,128)(2,1)} %get-tuple-element.15), channel_id=1, source_target_pairs={{0,384},{128,0},{256,128},{384,256},{1,385},{129,1},{257,129},{385... | collective-permute-start | bytes 1572872 | tf_op jit(solution)/shard_map/ppermute | solution.py:195
  21.2 29.2 %collective-permute-start.6 = (bf16[256,1024]{1,0:T(8,128)(2,1)}, bf16[256,1024]{1,0:T(8,128)(2,1)}, u32[]{:S(2)}, u32[]{:S(2)}) collective-permute-start(bf16[256,1024]{1,0:T(8,128)(2,1)} %get-tuple-element.13), channel_id=1, source_target_pairs={{0,128},{128,256},{256,384},{384,0},{1,129},{129,257},{257,385},{3... | collective-permute-start | bytes 1572872 | tf_op jit(solution)/shard_map/ppermute | solution.py:195
  23.2 31.5 %collective-permute-start.4 = (bf16[256,1024]{1,0:T(8,128)(2,1)}, bf16[256,1024]{1,0:T(8,128)(2,1)S(1)}, u32[]{:S(2)}, u32[]{:S(2)}) collective-permute-start(bf16[256,1024]{1,0:T(8,128)(2,1)} %get-tuple-element.14), channel_id=1, source_target_pairs={{0,256},{128,384},{256,0},{384,128},{1,257},{129,385},{257,1},{385... | collective-permute-start | bytes 1572872 | tf_op jit(solution)/shard_map/ppermute | solution.py:195
  27.7 27.0 %collective-permute-start.1 = (bf16[128,1536]{1,0:T(8,128)(2,1)}, bf16[128,1536]{1,0:T(8,128)(2,1)S(1)}, u32[]{:S(2)}, u32[]{:S(2)}) collective-permute-start(bf16[128,1536]{1,0:T(8,128)(2,1)} %slice.8), channel_id=1, source_target_pairs={{0,128},{128,256},{256,384},{384,0},{1,129},{129,257},{257,385},{3... | collective-permute-start | bytes 1179656 | tf_op jit(solution)/shard_map/ppermute | solution.py:195
  31.9 22.8 %collective-permute-start.3 = (bf16[128,1536]{1,0:T(8,128)(2,1)}, bf16[128,1536]{1,0:T(8,128)(2,1)S(1)}, u32[]{:S(2)}, u32[]{:S(2)}) collective-permute-start(bf16[128,1536]{1,0:T(8,128)(2,1)} %slice.9), channel_id=1, source_target_pairs={{0,384},{128,0},{256,128},{384,256},{1,385},{129,1},{257,129},{385... | collective-permute-start | bytes 1179656 | tf_op jit(solution)/shard_map/ppermute | solution.py:195
  35.0 15.5 %copy-start = (bf16[1,256,4096]{2,1,0:T(8,128)(2,1)S(1)}, bf16[1,256,4096]{2,1,0:T(8,128)(2,1)}, u32[]{:S(2)}) copy-start(bf16[1,256,4096]{2,1,0:T(8,128)(2,1)} %param.4) | copy-start | bytes 6291460
  35.0 15.5 %copy-start.1 = (bf16[1,256,1536]{2,1,0:T(8,128)(2,1)S(1)}, bf16[1,256,1536]{2,1,0:T(8,128)(2,1)}, u32[]{:S(2)}) copy-start(bf16[1,256,1536]{2,1,0:T(8,128)(2,1)} %param.3) | copy-start | bytes 2359300
  56.0 11.0 %collective-permute-start.7 = (bf16[32,96,256]{2,1,0:T(8,128)(2,1)S(1)}, bf16[32,96,256]{2,1,0:T(8,128)(2,1)S(1)}, u32[]{:S(2)}, u32[]{:S(2)}) collective-permute-start(bf16[32,96,256]{2,1,0:T(8,128)(2,1)S(1)} %shard_map.41), channel_id=1, source_target_pairs={{0,1},{1,0},{2,3},{3,2},{4,5},{5,4},{6,7},{7,6},{8,9},{9,8},{10,11... | collective-permute-start | bytes 4718600 | tf_op jit(solution)/shard_map/ppermute | solution.py:224
